TPU v7x, 32 devices: a whole 2x2x4 slice. The times are simulated.
32 devices in a mesh: group: 2 (over y), req: 8 (over z, x), tp: 2 (over core).
Axes of the slice: x: 2, y: 2, z: 4, core: 2. Of those that a mesh axis runs over, the one named last changes fastest.
Arguments:
- hidden: bfloat16 [64, 16384], P(('group', 'req')), parts along dimension 0, may hold values from -6 to 6
- adapter_ids: int32 [64], P('group'), parts along dimension 0, may hold values from 0 to 63
- home_slot: int32 [64], replicated, may hold values from 0 to 63, as said below
- lengths: int32 [64], P(('group', 'req')), parts along dimension 0, may hold values from 2 to 512, as said below
- query: bfloat16 [64, 2048], P(('group', 'req'), 'tp'), parts along dimension 0, may hold values from -128 to 128
- kv_base: bfloat16 [64, 256], P(('group', 'req')), parts along dimension 0, may hold values from -6 to 6
- cache: bfloat16 [64, 512, 256], P(('group', 'req')), parts along dimension 0, may hold values from -5 to 5
- adapter_down: bfloat16 [16384, 1024], P('req', 'tp'), may hold values from -0.046875 to 0.046875
- adapter_up: bfloat16 [64, 16, 256], P('req', 'tp'), may hold values from -3 to 3
Outputs:
- new_kv: bfloat16 [64, 256], P(('group', 'req')), parts along dimension 0
- attended: bfloat16 [64, 2048], P(('group', 'req'), 'tp'), parts along dimension 0
There are 2 independent parts, one for each index of `group`. A program takes and returns all parts, laid end to end along the dimension named above; an argument that names none is the same for every part. Nothing has to cross between parts.
Inputs may be any that keep to these rules, and one draw needn't show every extreme that they name: `home_slot`: distinct bank slots; slots 0 and 63 always hold an adapter. `lengths`: some request reaches 512.
All inputs are finite; a program needn't handle non-finite values.
Results may differ from a plain program's by a relative error of at most 0.02.
Values may be sent and summed in bfloat16 or wider, within the bound.
No kernel may reach another device: no remote copies, remote signals or barrier semaphores. Data moves between devices by JAX's collectives and lax.ppermute only.
A program may use at most 64 MiB of HBM per device.

v0:
```python
import jax
import jax.numpy as jnp
from jax import lax
from jax.sharding import PartitionSpec as P

HD = 128
ADAPTERS = 64


def attend(query, cache, new_kv, lengths):
    count = query.shape[0]
    heads = query.shape[1] // HD
    scale = HD ** (-0.5)
    q_rows = query.reshape(count, heads, HD)
    keys = cache[:, :, :HD]
    values = cache[:, :, HD:]
    k_new = new_kv[:, :HD]
    v_new = new_kv[:, HD:]
    scores = jnp.einsum("bhd,bld->bhl", q_rows, keys, preferred_element_type=jnp.float32) * scale
    valid = jnp.arange(cache.shape[1], dtype=jnp.int32)[None, None, :] < lengths[:, None, None]
    scores = jnp.where(valid, scores, -jnp.inf)
    own = jnp.einsum("bhd,bd->bh", q_rows, k_new, preferred_element_type=jnp.float32) * scale
    top = jnp.maximum(jnp.max(scores, axis=-1), own)
    weights = jnp.exp(scores - top[:, :, None])
    own_weight = jnp.exp(own - top)
    total = jnp.sum(weights, axis=-1) + own_weight
    probs = (weights / total[:, :, None]).astype(jnp.bfloat16)
    own_p = (own_weight / total).astype(jnp.bfloat16)
    result = jnp.einsum("bhl,bld->bhd", probs, values, preferred_element_type=jnp.float32)
    result = result + own_p.astype(jnp.float32)[:, :, None] * v_new.astype(jnp.float32)[:, None, :]
    return result.reshape(count, heads * HD).astype(jnp.bfloat16)


def slot_of(wanted, home_slot):
    match = wanted[:, None] == jnp.arange(ADAPTERS, dtype=jnp.int32)[None, :]
    return jnp.sum(jnp.where(match, home_slot[None, :], 0), axis=1)


def apply_up(low_rows, slots, factors):
    count = factors.shape[0]
    ranks = factors.shape[1]
    match = slots[:, None] == jnp.arange(count, dtype=jnp.int32)[None, :]
    weighted = jnp.where(match[:, :, None], low_rows[:, None, :], jnp.zeros((), jnp.bfloat16))
    weighted = weighted.reshape(low_rows.shape[0], count * ranks)
    return jnp.dot(
        weighted,
        factors.reshape(count * ranks, factors.shape[2]),
        preferred_element_type=jnp.float32,
    )


def shards(
    hidden, adapter_ids, home_slot, lengths, query, kv_base, cache, adapter_down, adapter_up
):
    per_dev = hidden.shape[0]
    ranks = adapter_up.shape[1]
    block = lax.all_to_all(hidden, "req", split_axis=1, concat_axis=0, tiled=True)
    everyone = block.shape[0]
    projected = jnp.dot(block, adapter_down, preferred_element_type=jnp.float32)
    projected = projected.reshape(everyone, ranks, ADAPTERS)
    picker = (adapter_ids[:, None] == jnp.arange(ADAPTERS, dtype=jnp.int32)[None, :]).astype(
        jnp.float32
    )
    low_part = jnp.einsum("bra,ba->br", projected, picker)
    low_mine = lax.psum_scatter(low_part, "req", scatter_dimension=0, tiled=True).astype(
        jnp.bfloat16
    )
    mine_ids = lax.dynamic_slice_in_dim(adapter_ids, lax.axis_index("req") * per_dev, per_dev, 0)
    mine_slots = slot_of(mine_ids, home_slot)
    delta_part = apply_up(
        low_mine, mine_slots, lax.all_gather(adapter_up, "req", axis=0, tiled=True)
    )
    delta = lax.psum(delta_part, "tp")
    new_kv = (kv_base.astype(jnp.float32) + delta).astype(jnp.bfloat16)
    attended = attend(query, cache, new_kv, lengths)
    return (new_kv, attended)


def solution(mesh):
    placed = (
        P(("group", "req"), None),
        P("group"),
        P(),
        P(("group", "req")),
        P(("group", "req"), "tp"),
        P(("group", "req"), None),
        P(("group", "req"), None, None),
        P("req", "tp"),
        P("req", "tp", None),
    )
    return jax.shard_map(
        shards,
        mesh=mesh,
        in_specs=placed,
        out_specs=(P(("group", "req"), None), P(("group", "req"), "tp")),
        check_vma=False,
    )
```

profile of v0, /device:TPU:0, one launch (start us, length us, event | category | flops | bytes accessed | tf_op | source)
XLA Modules:
  0.0 77.9 jit_solution(9733244398019279140)
XLA Ops:
  0.6 7.3 %all-to-all-start = ((bf16[4,8,2048]{2,0,1:T(4,128)(2,1)}), bf16[4,8,2048]{2,0,1:T(4,128)(2,1)S(1)}, u32[]{:S(2)}, u32[]{:S(2)}) async-start(bf16[4,8,2048]{2,0,1:T(4,128)(2,1)} %bitcast.35), calls=%async_computation | async-start | bytes 262144 | tf_op jit(solution)/shard_map/all_to_all | solution.py:57
  7.9 0.7 dynamic_slice.3
  8.6 0.8 %select_reduce_fusion = s32[4]{0:T(128)S(1)} fusion(s32[64]{0:T(128)} %param.11, s32[4]{0:T(128)S(1)} %dynamic_slice.3), kind=kLoop, calls=%fused_computation.33 | loop fusion | flops 764 | bytes 288 | tf_op jit(solution)/shard_map/reduce_sum | solution.py:36
  9.5 0.1 iota_compare_fusion.2
  9.5 0.8 copy.20
  10.3 0.7 iota_compare_fusion.1
  11.0 1.4 %fusion.25 = (f32[4,8]{1,0:T(4,128)S(1)}, f32[4,8,512]{2,1,0:T(8,128)S(1)}) fusion(bf16[4,512,256]{2,1,0:T(8,128)(2,1)} %param.15, bf16[1,4,8,128]{3,1,2,0:T(4,128)(2,1)} %bitcast.37, pred[4,512]{1,0:T(4,128)(4,1)S(1)} %iota_compare_fusion.1), kind=kOutput, calls=%fused_computation.43 | convolution fusion | flops 4243424 | bytes 600192 | tf_op jit(solution)/shard_map/bhd,bld->bhl/dot_general | solution.py:19
  12.4 33.5 %all_gather.3 = bf16[64,8,256]{2,0,1:T(8,128)(2,1)} all-gather(bf16[8,8,256]{2,0,1:T(8,128)(2,1)S(1)} %copy.20), channel_id=1, replica_groups=mesh['group'=2,'req'=8,'tp'=2] {'req'}, dimensions={0}, use_global_device_ids=true | all-gather | bytes 294912 | tf_op jit(solution)/shard_map/all_gather | solution.py:71
  45.9 0.0 copy-start.5
  45.9 0.0 copy-start.4
  45.9 3.0 %copy.19 = bf16[2048,512]{0,1:T(8,128)(2,1)S(1)} copy(bf16[2048,512]{1,0:T(8,128)(2,1)} %param.16) | data formatting | bytes 4194304 | tf_op args[7]
  48.9 0.0 copy-start.3
  48.9 0.0 copy-start.1
  48.9 0.0 copy-start
  49.0 0.0 copy-done.5
  49.0 0.6 dynamic-slice
  50.2 0.0 copy-done.4
  50.2 0.1 fusion.11
  50.3 0.0 all-to-all-done
  50.3 1.1 %fusion.26 = bf16[32,8,64]{2,0,1:T(8,128)(2,1)S(1)} fusion(bf16[32,2048,1]{1,0,2:T(8,128)(2,1)S(1)} %reshape.67, bf16[8,64,2048]{2,1,0:T(8,128)(2,1)S(1)} %bitcast.33), kind=kOutput, calls=%fused_computation.44 | convolution fusion | flops 67108864 | bytes 2260992 | tf_op jit(solution)/shard_map/dot_general | solution.py:59
  51.4 0.2 fusion.5
  51.6 0.1 copy.23
  51.6 21.3 %all-reduce = bf16[32,8]{0,1:T(8,128)(2,1)S(1)} all-reduce(f32[32,8]{0,1:T(8,128)S(1)} %bitcast.36), channel_id=2, replica_groups=mesh['group'=2,'req'=8,'tp'=2] {'req'}, use_global_device_ids=true, to_apply=%region_1.2.clone | all-reduce | flops 256 | bytes 1536
  72.9 0.1 dynamic-slice_convert_fusion
  73.0 1.2 %convolution_bitcast_fusion = f32[4,256]{1,0:T(4,128)S(1)} fusion(bf16[64,8,256]{2,0,1:T(8,128)(2,1)} %all_gather.3, pred[4,64]{1,0:T(4,128)(4,1)S(1)} %iota_compare_fusion.2, bf16[4,8]{0,1:T(8,128)(2,1)S(1)} %dynamic-slice_convert_fusion), kind=kOutput, calls=%fused_computation.5 | convolution fusion | flops 1050624 | bytes 266560 | tf_op jit(solution)/shard_map/dot_general | solution.py:45
  74.2 2.4 %psum.7 = f32[4,256]{1,0:T(4,128)S(1)} all-reduce(f32[4,256]{1,0:T(4,128)S(1)} %convolution_bitcast_fusion), channel_id=1, replica_groups=mesh['group'=2,'req'=8,'tp'=2] {'tp'}, use_global_device_ids=true, to_apply=%region_2.3 | all-reduce | flops 1024 | bytes 8192 | tf_op jit(solution)/shard_map/psum | solution.py:73
  76.7 0.0 copy-done.3
  76.7 0.0 copy-start.2
  76.7 0.0 copy-done.1
  76.7 0.1 fusion.12
  76.8 0.2 fusion.8
  77.0 0.0 copy-done
  77.0 0.2 fusion.2
  77.3 0.6 copy.47
  77.9 0.0 copy-done.2
  (5 shorter events, 0.1 us)
Async XLA Ops:
  0.6 49.7 %all-to-all-start = ((bf16[4,8,2048]{2,0,1:T(4,128)(2,1)}), bf16[4,8,2048]{2,0,1:T(4,128)(2,1)S(1)}, u32[]{:S(2)}, u32[]{:S(2)}) async-start(bf16[4,8,2048]{2,0,1:T(4,128)(2,1)} %bitcast.35), calls=%async_computation | async-start | bytes 262144 | tf_op jit(solution)/shard_map/all_to_all | solution.py:57
  45.9 3.0 %copy-start.5 = (u32[32]{0:T(128)S(1)}, u32[32]{0:T(128)}, u32[]{:S(2)}) copy-start(u32[32]{0:T(128)} %constant.28) | copy-start | bytes 388
  45.9 4.3 %copy-start.4 = (s32[32]{0:T(128)S(1)}, s32[32]{0:T(128)}, u32[]{:S(2)}) copy-start(s32[32]{0:T(128)} %param.10) | copy-start | bytes 388
  48.9 27.8 %copy-start.3 = (bf16[4,256]{1,0:T(4,128)(2,1)S(1)}, bf16[4,256]{1,0:T(4,128)(2,1)}, u32[]{:S(2)}) copy-start(bf16[4,256]{1,0:T(4,128)(2,1)} %param.14) | copy-start | bytes 6148
  48.9 27.8 %copy-start.1 = (bf16[4,1024]{1,0:T(4,128)(2,1)S(1)}, bf16[4,1024]{1,0:T(4,128)(2,1)}, u32[]{:S(2)}) copy-start(bf16[4,1024]{1,0:T(4,128)(2,1)} %param.13) | copy-start | bytes 24580
  48.9 28.1 %copy-start = (bf16[4,512,256]{2,1,0:T(8,128)(2,1)S(1)}, bf16[4,512,256]{2,1,0:T(8,128)(2,1)}, u32[]{:S(2)}) copy-start(bf16[4,512,256]{2,1,0:T(8,128)(2,1)} %param.15) | copy-start | bytes 3145732
  76.7 1.2 %copy-start.2 = (bf16[4,256]{1,0:T(4,128)(2,1)}, bf16[4,256]{1,0:T(4,128)(2,1)S(1)}, u32[]{:S(2)}) copy-start(bf16[4,256]{1,0:T(4,128)(2,1)S(1)} %add_convert_fusion) | copy-start | bytes 6148
where the time goes:
time: 78.4 us; the launch traced here: 77.9 us
  blocking collectives  57.3 us (73%)
  starting transfers between devices  7.26 us (9%)
  local copies, waits for them, and re-layouts  5.86 us (7%)
  matrix products  4.2 us (5%)
  other arithmetic  1.91 us (2%)
  between operations  1.39 us (2%)
    all_gather x1, blocking collectives, shards(): lax.all_gather(adapter_up, 'req', axis=0, tiled=True)  33.5 us
    unnamed x1, blocking collectives  21.3 us
    all_to_all x1, starting transfers between devices, shards(): lax.all_to_all(hidden, 'req', split_axis=1, concat_axis=0, tiled=True)  7.26 us
    unnamed x16, local copies, waits for them, and re-layouts  4.96 us
    psum x1, blocking collectives, shards(): delta = lax.psum(delta_part, 'tp')  2.45 us
  transfers between devices with their start and end apart: 1, of which 0 were waited for; matrix products, arithmetic and copies ran while one was open for 10% of the time, Pallas kernels for 0%

commit v1 on v0

v1 whole, which is shorter than its diff:
```python
import jax
import jax.numpy as jnp
from jax import lax
from jax.sharding import PartitionSpec as P

HD = 128
ADAPTERS = 64


def cached_part(query, cache, lengths):
    count = query.shape[0]
    heads = query.shape[1] // HD
    scale = HD ** (-0.5)
    q_rows = query.reshape(count, heads, HD)
    keys = cache[:, :, :HD]
    values = cache[:, :, HD:]
    scores = jnp.einsum("bhd,bld->bhl", q_rows, keys, preferred_element_type=jnp.float32) * scale
    valid = jnp.arange(cache.shape[1], dtype=jnp.int32)[None, None, :] < lengths[:, None, None]
    scores = jnp.where(valid, scores, -jnp.inf)
    top = jnp.max(scores, axis=-1)
    weights = jnp.exp(scores - top[:, :, None])
    total = jnp.sum(weights, axis=-1)
    result = jnp.einsum(
        "bhl,bld->bhd", weights.astype(jnp.bfloat16), values, preferred_element_type=jnp.float32
    )
    return q_rows, top, total, result


def merge_own(q_rows, top, total, result, new_kv):
    count, heads, _ = q_rows.shape
    scale = HD ** (-0.5)
    k_new = new_kv[:, :HD].astype(jnp.float32)
    v_new = new_kv[:, HD:].astype(jnp.float32)
    own = jnp.sum(q_rows.astype(jnp.float32) * k_new[:, None, :], axis=-1) * scale
    high = jnp.maximum(top, own)
    keep = jnp.exp(top - high)
    own_weight = jnp.exp(own - high)
    norm = 1.0 / (total * keep + own_weight)
    out = result * (keep * norm)[:, :, None] + (own_weight * norm)[:, :, None] * v_new[:, None, :]
    return out.reshape(count, heads * HD).astype(jnp.bfloat16)


def shards(
    hidden, adapter_ids, home_slot, lengths, query, kv_base, cache, adapter_down, adapter_up
):
    per_dev = hidden.shape[0]
    slots, ranks, width = adapter_up.shape
    parts = lax.axis_size("req")
    me = lax.axis_index("req")
    everyone = per_dev * parts
    block = lax.all_to_all(hidden, "req", split_axis=1, concat_axis=0, tiled=True)
    picker = adapter_ids[:, None] == jnp.arange(ADAPTERS, dtype=jnp.int32)[None, :]
    wanted = jnp.sum(jnp.where(picker, home_slot[None, :], 0), axis=1) - me * slots
    mine = (wanted[:, None] == jnp.arange(slots, dtype=jnp.int32)[None, :]).astype(jnp.bfloat16)
    rows = jnp.dot(
        mine, adapter_up.reshape(slots, ranks * width), preferred_element_type=jnp.float32
    ).astype(jnp.bfloat16)
    rows = rows.reshape(parts, per_dev * ranks * width)
    q_rows, top, total, result = cached_part(query, cache, lengths)
    projected = jnp.dot(block, adapter_down, preferred_element_type=jnp.float32)
    projected = projected.reshape(everyone, ranks, ADAPTERS)
    low_part = jnp.sum(jnp.where(picker[:, None, :], projected, 0.0), axis=2)
    high = low_part.astype(jnp.bfloat16)
    rest = (low_part - high.astype(jnp.float32)).astype(jnp.bfloat16)
    packed = jnp.concatenate(
        [
            rows,
            high.reshape(parts, per_dev * ranks),
            rest.reshape(parts, per_dev * ranks),
        ],
        axis=1,
    )
    got = lax.all_to_all(packed, "req", split_axis=0, concat_axis=0, tiled=True)
    got = jnp.sum(got.astype(jnp.float32), axis=0)
    size = per_dev * ranks
    up_rows = got[: size * width].reshape(per_dev, ranks, width)
    low = (got[size * width : size * width + size] + got[size * width + size :]).astype(jnp.bfloat16)
    low = low.reshape(per_dev, ranks).astype(jnp.float32)
    delta = jnp.sum(low[:, :, None] * up_rows, axis=1)
    delta = delta + lax.ppermute(delta, "tp", [(0, 1), (1, 0)])
    new_kv = (kv_base.astype(jnp.float32) + delta).astype(jnp.bfloat16)
    attended = merge_own(q_rows, top, total, result, new_kv)
    return (new_kv, attended)


def solution(mesh):
    placed = (
        P(("group", "req"), None),
        P("group"),
        P(),
        P(("group", "req")),
        P(("group", "req"), "tp"),
        P(("group", "req"), None),
        P(("group", "req"), None, None),
        P("req", "tp"),
        P("req", "tp", None),
    )
    return jax.shard_map(
        shards,
        mesh=mesh,
        in_specs=placed,
        out_specs=(P(("group", "req"), None), P(("group", "req"), "tp")),
        check_vma=False,
    )
```

time: 78.4 us -> 34.6 us (0.44)
  blocking collectives: 57.3 us -> 0 us
  waiting for transfers between devices: 0.01 us -> 8.89 us
  starting transfers between devices: 7.26 us -> 12.5 us
  matrix products: 4.2 us -> 1.96 us
  other arithmetic: 1.91 us -> 3.8 us
    all_gather x1 -> x0, blocking collectives: 33.5 us -> none  [shards(): lax.all_gather(adapter_up, 'req', axis=0, tiled=True)]
    unnamed x1 -> x0, blocking collectives: 21.3 us -> none
    all_to_all x0 -> x1, waiting for transfers between devices: none -> 7.03 us  [shards(): got = lax.all_to_all(packed, 'req', split_axis=0, concat_axis=0, tiled=True)]
    all_to_all x0 -> x1, starting transfers between devices: none -> 5.12 us  [shards(): got = lax.all_to_all(packed, 'req', split_axis=0, concat_axis=0, tiled=True)]
    psum x1 -> x0, blocking collectives: 2.45 us -> none  [shards(): delta = lax.psum(delta_part, 'tp')]
    dot_general x5 -> x3, matrix products: 3.13 us -> 0.8 us  [the longest x1 0.32 us: cached_part(): jnp.einsum('bhd,bld->bhl', q_rows, keys, preferred_element_type=jnp.float32)]
    ppermute x0 -> x1, waiting for transfers between devices: none -> 0.98 us  [shards(): delta = delta + lax.ppermute(delta, 'tp', [(0, 1), (1, 0)])]
    all_to_all x1, waiting for transfers between devices: 0.01 us -> 0.88 us  [shards(): lax.all_to_all(hidden, 'req', split_axis=1, concat_axis=0, tiled=True)]
  transfers between devices with their start and end apart: 1 -> 3, of which waited for: 0 -> 3; matrix products, arithmetic and copies ran while one was open for 10% -> 20% of each run, Pallas kernels for 0% -> 0%
where the time goes in v1:
time: 34.6 us; the launch traced here: 34.1 us
  starting transfers between devices  12.5 us (36%)
  waiting for transfers between devices  8.89 us (26%)
  local copies, waits for them, and re-layouts  6.26 us (18%)
  other arithmetic  3.8 us (11%)
  matrix products  1.96 us (6%)
  between operations  0.77 us (2%)
    all_to_all x1, starting transfers between devices, shards(): lax.all_to_all(hidden, 'req', split_axis=1, concat_axis=0, tiled=True)  7.26 us
    all_to_all x1, waiting for transfers between devices, shards(): got = lax.all_to_all(packed, 'req', split_axis=0, concat_axis=0, tiled=True)  7.03 us
    unnamed x13, local copies, waits for them, and re-layouts  5.26 us
    all_to_all x1, starting transfers between devices, shards(): got = lax.all_to_all(packed, 'req', split_axis=0, concat_axis=0, tiled=True)  5.12 us
    dot_general x1, matrix products, shards(): projected = jnp.dot(block, adapter_down, preferred_element_type=jnp.float32)  1.16 us
    ppermute x1, waiting for transfers between devices, shards(): delta = delta + lax.ppermute(delta, 'tp', [(0, 1), (1, 0)])  0.98 us
    all_to_all x1, waiting for transfers between devices, shards(): lax.all_to_all(hidden, 'req', split_axis=1, concat_axis=0, tiled=True)  0.88 us
    reduce_sum x1, other arithmetic, shards(): jnp.sum(jnp.where(picker, home_slot[None, :], 0), axis=1) - me * slots  0.85 us
  transfers between devices with their start and end apart: 3, of which 3 were waited for; matrix products, arithmetic and copies ran while one was open for 20% of the time, Pallas kernels for 0%

profile of v1, /device:TPU:0, one launch (start us, length us, event | category | flops | bytes accessed | tf_op | source)
XLA Modules:
  0.0 34.1 jit_solution(1088337870521007907)
XLA Ops:
  0.6 7.3 %all-to-all-start = ((bf16[4,8,2048]{2,0,1:T(4,128)(2,1)}), bf16[4,8,2048]{2,0,1:T(4,128)(2,1)S(1)}, u32[]{:S(2)}, u32[]{:S(2)}) async-start(bf16[4,8,2048]{2,0,1:T(4,128)(2,1)} %bitcast.27), calls=%async_computation | async-start | bytes 262144 | tf_op jit(solution)/shard_map/all_to_all | solution.py:51
  7.9 0.8 %copy.26 = bf16[1,8,8,256]{3,1,2,0:T(8,128)(2,1)S(1)} copy(bf16[1,8,8,256]{3,2,1,0:T(8,128)(2,1)} %bitcast.30) | data formatting | bytes 65536
  8.7 0.8 %select_reduce_fusion = s32[32]{0:T(128)S(1)} fusion(s32[64]{0:T(128)} %param.11, s32[32]{0:T(128)} %param.10), kind=kLoop, calls=%fused_computation.19 | loop fusion | flops 6112 | bytes 512 | tf_op jit(solution)/shard_map/reduce_sum | solution.py:53
  9.5 0.2 convolution_convert_fusion
  9.8 0.7 %iota_compare_fusion.3 = pred[4,512]{1,0:T(4,128)(4,1)S(1)} fusion(s32[4]{0:T(128)} %param.12), kind=kLoop, calls=%fused_computation.23 | loop fusion | flops 2048 | bytes 2064 | tf_op jit(solution)/shard_map/lt | solution.py:18
  10.5 2.9 %copy.23 = bf16[2048,512]{0,1:T(8,128)(2,1)S(1)} copy(bf16[2048,512]{1,0:T(8,128)(2,1)} %param.16) | data formatting | bytes 4194304 | tf_op args[7]
  13.4 0.0 copy-start
  13.4 0.0 copy-start.1
  13.4 0.1 reshape.120
  13.6 0.8 %iota_compare_fusion.1 = pred[32,64]{1,0:T(8,128)(4,1)S(1)} fusion(s32[32]{0:T(128)} %param.10), kind=kLoop, calls=%fused_computation.20 | loop fusion | flops 2048 | bytes 2176 | tf_op jit(solution)/shard_map/eq | solution.py:52
  14.4 0.9 %all-to-all-done = bf16[4,8,2048]{2,0,1:T(4,128)(2,1)S(1)} async-done(((bf16[4,8,2048]{2,0,1:T(4,128)(2,1)}), bf16[4,8,2048]{2,0,1:T(4,128)(2,1)S(1)}, u32[]{:S(2)}, u32[]{:S(2)}) %all-to-all-start) | async-done | bytes 131104 | tf_op jit(solution)/shard_map/all_to_all | solution.py:51
  15.3 1.2 %fusion = f32[32,8]{0,1:T(8,128)S(1)} fusion(bf16[32,2048,1]{1,0,2:T(8,128)(2,1)S(1)} %reshape.124, bf16[8,64,2048]{2,1,0:T(8,128)(2,1)S(1)} %bitcast.23, pred[32,64]{1,0:T(8,128)(4,1)S(1)} %iota_compare_fusion.1), kind=kOutput, calls=%fused_computation.2 | convolution fusion | flops 67141376 | bytes 2231296 | tf_op jit(solution)/shard_map/dot_general | solution.py:60
  16.4 0.0 copy-start.3
  16.5 0.1 copy.24
  16.5 0.1 reduce_sum.58
  16.6 0.1 concatenate.3
  16.7 0.5 %broadcast.46 = bf16[]{:T(256)} broadcast(bf16[]{:T(256)} %constant.45), dimensions={} | broadcast | bytes 4 | tf_op jit(solution)/shard_map/all_to_all | solution.py:73
  17.2 0.7 %reduce.1 = bf16[8,8256]{1,0:T(8,128)(2,1)S(1)} reduce(bf16[8,1,8256]{2,0,1:T(8,128)(2,1)S(1)} %bitcast.24, bf16[]{:T(256)} %broadcast.46), dimensions={1}, to_apply=%copy.25.reduce_sub_computation | reduce | bytes 264194 | tf_op jit(solution)/shard_map/all_to_all | solution.py:73
  17.9 0.8 %reshape.126 = bf16[8,2,4128]{2,1,0:T(2,128)(2,1)} reshape(bf16[8,8256]{1,0:T(8,128)(2,1)S(1)} %reduce.1) | data formatting | bytes 264192
  18.7 5.1 %all-to-all-start.1 = ((bf16[8,2,4128]{2,1,0:T(2,128)(2,1)}), bf16[8,2,4128]{2,1,0:T(2,128)(2,1)S(1)}, u32[]{:S(2)}, u32[]{:S(2)}) async-start(bf16[8,2,4128]{2,1,0:T(2,128)(2,1)} %reshape.126), calls=%async_computation.1 | async-start | bytes 270336 | tf_op jit(solution)/shard_map/all_to_all | solution.py:73
  23.8 0.0 copy-done
  23.8 0.0 copy-done.1
  23.8 0.3 fusion.20
  24.2 7.0 %all-to-all-done.1 = bf16[8,2,4128]{2,1,0:T(2,128)(2,1)S(1)} async-done(((bf16[8,2,4128]{2,1,0:T(2,128)(2,1)}), bf16[8,2,4128]{2,1,0:T(2,128)(2,1)S(1)}, u32[]{:S(2)}, u32[]{:S(2)}) %all-to-all-start.1) | async-done | bytes 132128 | tf_op jit(solution)/shard_map/all_to_all | solution.py:73
  31.2 0.1 reshape.127
  31.3 0.3 convert_reduce_fusion
  31.6 0.1 fusion.17
  31.7 0.1 reshape.123
  31.8 0.1 multiply_reduce_fusion
  31.9 0.1 collective-permute-start
  32.0 0.2 fusion.7
  32.2 1.0 %collective-permute-done = f32[4,256]{1,0:T(4,128)S(1)} collective-permute-done((f32[4,256]{1,0:T(4,128)S(1)}, f32[4,256]{1,0:T(4,128)S(1)}, u32[]{:S(2)}, u32[]{:S(2)}) %collective-permute-start) | collective-permute-done | bytes 4128 | tf_op jit(solution)/shard_map/ppermute | solution.py:80
  33.1 0.0 copy-done.3
  33.1 0.0 copy-start.2
  33.2 0.1 multiply_reduce_fusion.1
  33.3 0.2 fusion.4
  33.5 0.6 %copy.37 = bf16[1,4,8,128]{3,1,2,0:T(4,128)(2,1)} copy(bf16[1,4,8,128]{3,2,1,0:T(8,128)(2,1)S(1)} %fusion.4) | data formatting | bytes 16384
  34.1 0.0 copy-done.2
  (8 shorter events, 0.1 us)
Async XLA Ops:
  0.6 14.6 %all-to-all-start = ((bf16[4,8,2048]{2,0,1:T(4,128)(2,1)}), bf16[4,8,2048]{2,0,1:T(4,128)(2,1)S(1)}, u32[]{:S(2)}, u32[]{:S(2)}) async-start(bf16[4,8,2048]{2,0,1:T(4,128)(2,1)} %bitcast.27), calls=%async_computation | async-start | bytes 262144 | tf_op jit(solution)/shard_map/all_to_all | solution.py:51
  13.4 10.4 %copy-start = (bf16[4,512,256]{2,1,0:T(8,128)(2,1)S(1)}, bf16[4,512,256]{2,1,0:T(8,128)(2,1)}, u32[]{:S(2)}) copy-start(bf16[4,512,256]{2,1,0:T(8,128)(2,1)} %param.15) | copy-start | bytes 3145732
  13.4 10.4 %copy-start.1 = (bf16[4,1024]{1,0:T(4,128)(2,1)S(1)}, bf16[4,1024]{1,0:T(4,128)(2,1)}, u32[]{:S(2)}) copy-start(bf16[4,1024]{1,0:T(4,128)(2,1)} %param.13) | copy-start | bytes 24580
  16.4 16.7 %copy-start.3 = (bf16[4,256]{1,0:T(4,128)(2,1)S(1)}, bf16[4,256]{1,0:T(4,128)(2,1)}, u32[]{:S(2)}) copy-start(bf16[4,256]{1,0:T(4,128)(2,1)} %param.14) | copy-start | bytes 6148
  18.7 12.5 %all-to-all-start.1 = ((bf16[8,2,4128]{2,1,0:T(2,128)(2,1)}), bf16[8,2,4128]{2,1,0:T(2,128)(2,1)S(1)}, u32[]{:S(2)}, u32[]{:S(2)}) async-start(bf16[8,2,4128]{2,1,0:T(2,128)(2,1)} %reshape.126), calls=%async_computation.1 | async-start | bytes 270336 | tf_op jit(solution)/shard_map/all_to_all | solution.py:73
  31.9 1.2 %collective-permute-start = (f32[4,256]{1,0:T(4,128)S(1)}, f32[4,256]{1,0:T(4,128)S(1)}, u32[]{:S(2)}, u32[]{:S(2)}) collective-permute-start(f32[4,256]{1,0:T(4,128)S(1)} %multiply_reduce_fusion), channel_id=1, source_target_pairs={{0,1},{1,0},{2,3},{3,2},{4,5},{5,4},{6,7},{7,6},{8,9},{9,8},{10,11... | collective-permute-start | bytes 12296 | tf_op jit(solution)/shard_map/ppermute | solution.py:80
  33.1 1.0 %copy-start.2 = (bf16[4,256]{1,0:T(4,128)(2,1)}, bf16[4,256]{1,0:T(4,128)(2,1)S(1)}, u32[]{:S(2)}) copy-start(bf16[4,256]{1,0:T(4,128)(2,1)S(1)} %add_convert_fusion) | copy-start | bytes 6148

commit v2 on v0

v2 whole, which is shorter than its diff:
```python
import functools

import jax
import jax.numpy as jnp
from jax import lax
from jax.experimental import pallas as pl
from jax.experimental.pallas import tpu as pltpu
from jax.sharding import PartitionSpec as P

HD = 128
ADAPTERS = 64
F32 = jnp.float32
BF16 = jnp.bfloat16
VMEM = pl.BlockSpec(memory_space=pltpu.VMEM)
SMEM = pl.BlockSpec(memory_space=pltpu.SMEM)
HBM = pl.BlockSpec(memory_space=pltpu.HBM)
PARAMS = pltpu.CompilerParams(vmem_limit_bytes=8 * 1024 * 1024)


def iota(shape, dim):
    return lax.broadcasted_iota(jnp.int32, shape, dim)


def one_hot_ids(ids):
    shape = (ADAPTERS, ids.shape[1])
    return (iota(shape, 0) == jnp.broadcast_to(ids, shape)).astype(BF16)


def across(a, b):
    return lax.dot_general(a, b, (((0,), (0,)), ((), ())), preferred_element_type=F32)


def rotate_kernel(order, hidden_ref, out_ref, held_ref, sems):
    block = out_ref.shape[2]
    copies = [
        pltpu.make_async_copy(
            hidden_ref.at[:, pl.ds(q * block, block)], held_ref.at[p], sems.at[p]
        )
        for p, q in enumerate(order)
    ]
    for copy in copies:
        copy.start()
    for copy in copies:
        copy.wait()
    copy = pltpu.make_async_copy(held_ref, out_ref, sems.at[0])
    copy.start()
    copy.wait()


def local_kernel(
    order, base_ref, lengths_ref, ids_hbm, home_hbm, query_hbm, up_hbm, cache_hbm, down_hbm,
    q_ref, acc_ref, top_ref, total_ref, rows_ref, pick_ref, down_ref,
    ids_ref, home_ref, query_ref, up_ref, cache_ref, flat_ref, wide_ref, sems
):
    pairs = (
        (ids_hbm, ids_ref),
        (home_hbm, home_ref),
        (query_hbm, query_ref),
        (up_hbm, up_ref),
        (cache_hbm, cache_ref),
        (down_hbm, down_ref),
    )
    copies = [pltpu.make_async_copy(a, b, sems.at[i]) for i, (a, b) in enumerate(pairs)]
    for copy in copies:
        copy.start()
    for copy in copies[:4]:
        copy.wait()
    slots, ranks, width = up_ref.shape
    depth = flat_ref.shape[0]
    count = cache_ref.shape[0]
    heads = query_ref.shape[1] // HD
    scale = HD ** (-0.5)
    chosen_ids = one_hot_ids(ids_ref[...])
    if depth > slots:
        flat_ref[...] = jnp.zeros_like(flat_ref)
    wide_ref[...] = up_ref[...].astype(F32)
    for r in range(ranks):
        flat_ref[:slots, r * width : (r + 1) * width] = wide_ref[:, r, :]
    shape = (depth, ADAPTERS)
    here = jnp.broadcast_to(home_ref[...], shape) - base_ref[0] == iota(shape, 0)
    held = here & (iota(shape, 0) < slots)
    match = jnp.dot(held.astype(BF16), chosen_ids, preferred_element_type=F32)
    rows = across(match.astype(BF16), flat_ref[...].astype(BF16)).astype(BF16)
    columns = pick_ref.shape[1]
    spread = (iota((ADAPTERS, columns), 1) % ADAPTERS == iota((ADAPTERS, columns), 0)).astype(BF16)
    pick = across(chosen_ids, spread)
    shift = order[0] * count
    if shift:
        pick = jnp.concatenate([pick[shift:], pick[:shift]], axis=0)
    pick_ref[...] = pick
    for p, q in enumerate(order):
        rows_ref[p] = rows[q * count : (q + 1) * count]
    query = query_ref[...].astype(F32)
    for h in range(heads):
        q_ref[pl.ds(h, count, stride=heads), :] = query[:, h * HD : (h + 1) * HD]
    copies[4].wait()
    for b in range(count):
        part = pl.ds(b * heads, heads)
        scores = lax.dot_general(
            q_ref[part, :].astype(BF16),
            cache_ref[b, :, :HD],
            (((1,), (1,)), ((), ())),
            preferred_element_type=F32,
        )
        valid = iota(scores.shape, 1) < lengths_ref[b]
        scores = jnp.where(valid, scores * scale, -jnp.inf)
        top = jnp.max(scores, axis=1, keepdims=True)
        weights = jnp.exp(scores - top)
        total = jnp.sum(weights, axis=1, keepdims=True)
        acc_ref[part, :] = jnp.dot(
            weights.astype(BF16), cache_ref[b, :, HD:], preferred_element_type=F32
        )
        top_ref[part, :] = jnp.broadcast_to(top, (heads, HD))
        total_ref[part, :] = jnp.broadcast_to(total, (heads, HD))
    copies[5].wait()


def low_kernel(ranks, block_ref, down_ref, pick_ref, rows_ref, out_ref):
    parts, per_dev, _ = out_ref.shape
    span = rows_ref.shape[2]
    projected = jnp.dot(block_ref[...], down_ref[...], preferred_element_type=F32)
    chosen = projected * pick_ref[...]
    high = chosen.astype(BF16)
    rest = (chosen - high.astype(F32)).astype(BF16)
    columns = chosen.shape[1]
    ends = (iota((columns, 128), 0) // ADAPTERS, iota((columns, 128), 1))
    fold = (ends[0] == ends[1]).astype(BF16)
    fold_rest = (ends[0] + ranks == ends[1]).astype(BF16)
    low = jnp.dot(high, fold, preferred_element_type=F32)
    low = low + jnp.dot(rest, fold_rest, preferred_element_type=F32)
    low = low.astype(BF16)
    for p in range(parts):
        out_ref[p, :, :span] = rows_ref[p]
        out_ref[p, :, span:] = low[p * per_dev : (p + 1) * per_dev]


def delta_kernel(ranks, got_ref, out_ref):
    parts, count, _ = got_ref.shape
    width = out_ref.shape[1]
    got = got_ref[0].astype(F32)
    for p in range(1, parts):
        got = got + got_ref[p].astype(F32)
    low = got[:, ranks * width :]
    delta = jnp.zeros((count, width), F32)
    for r in range(ranks):
        share = (low[:, r : r + 1] + low[:, r + ranks : r + ranks + 1]).astype(BF16).astype(F32)
        delta = delta + share * got[:, r * width : (r + 1) * width]
    out_ref[...] = delta


def merge_kernel(
    mine_ref, other_ref, base_ref, q_ref, acc_ref, top_ref, total_ref, kv_ref, out_ref, wide_ref
):
    count = base_ref.shape[0]
    heads = q_ref.shape[0] // count
    scale = HD ** (-0.5)
    delta = mine_ref[...] + other_ref[...]
    new_kv = (base_ref[...].astype(F32) + delta).astype(BF16)
    kv_ref[...] = new_kv
    fresh = new_kv.astype(F32)
    for b in range(count):
        rows = pl.ds(b * heads, heads)
        key = fresh[b : b + 1, :HD]
        value = fresh[b : b + 1, HD:]
        own = jnp.sum(q_ref[rows, :] * key, axis=1, keepdims=True) * scale
        own = jnp.broadcast_to(own, (heads, HD))
        top = top_ref[rows, :]
        high = jnp.maximum(top, own)
        keep = jnp.exp(top - high)
        weight = jnp.exp(own - high)
        norm = 1.0 / (total_ref[rows, :] * keep + weight)
        wide_ref[rows, :] = (acc_ref[rows, :] * keep + weight * value) * norm
    for h in range(heads):
        out_ref[:, h * HD : (h + 1) * HD] = wide_ref[pl.ds(h, count, stride=heads), :].astype(BF16)


def shards(
    hidden, adapter_ids, home_slot, lengths, query, kv_base, cache, adapter_down, adapter_up
):
    per_dev = hidden.shape[0]
    slots, ranks, width = adapter_up.shape
    parts = lax.axis_size("req")
    everyone = per_dev * parts
    block = hidden.shape[1] // parts
    heads = query.shape[1] // HD
    center = (parts // 2 + 1) % parts
    order = [(center + p) % parts for p in range(parts)]
    depth = -(-slots // 8) * 8
    base = (lax.axis_index("req") * slots).astype(jnp.int32).reshape(1)
    span = ranks * width
    pin = lambda x: pltpu.with_memory_space_constraint(x, pltpu.HBM)
    blocks = pl.pallas_call(
        functools.partial(rotate_kernel, order),
        out_shape=jax.ShapeDtypeStruct((parts, per_dev, block), BF16),
        in_specs=[HBM],
        out_specs=HBM,
        scratch_shapes=[
            pltpu.VMEM((parts, per_dev, block), BF16),
            pltpu.SemaphoreType.DMA((parts,)),
        ],
        compiler_params=PARAMS,
    )(pin(hidden))
    blocks = lax.all_to_all(
        blocks, "req", split_axis=0, concat_axis=0, tiled=True, axis_index_groups=[order]
    )
    small = jax.ShapeDtypeStruct((per_dev * heads, HD), F32)
    q_rows, acc, top, total, rows, pick, down = pl.pallas_call(
        functools.partial(local_kernel, order),
        out_shape=(small, small, small, small)
        + (
            jax.ShapeDtypeStruct((parts, per_dev, span), BF16),
            jax.ShapeDtypeStruct((everyone, ranks * ADAPTERS), F32),
            jax.ShapeDtypeStruct(adapter_down.shape, BF16),
        ),
        in_specs=[SMEM, SMEM] + [HBM] * 6,
        out_specs=(VMEM,) * 7,
        scratch_shapes=[
            pltpu.VMEM((1, everyone), jnp.int32),
            pltpu.VMEM((1, ADAPTERS), jnp.int32),
            pltpu.VMEM(query.shape, BF16),
            pltpu.VMEM(adapter_up.shape, BF16),
            pltpu.VMEM(cache.shape, BF16),
            pltpu.VMEM((depth, span), F32),
            pltpu.VMEM((slots, ranks, width), F32),
            pltpu.SemaphoreType.DMA((6,)),
        ],
        compiler_params=PARAMS,
    )(
        base,
        lengths,
        pin(adapter_ids.reshape(1, everyone)),
        pin(home_slot.reshape(1, ADAPTERS)),
        pin(query),
        pin(adapter_up),
        pin(cache),
        pin(adapter_down),
    )
    packed = pl.pallas_call(
        functools.partial(low_kernel, ranks),
        out_shape=jax.ShapeDtypeStruct((parts, per_dev, span + 128), BF16),
        in_specs=[VMEM] * 4,
        out_specs=VMEM,
        compiler_params=PARAMS,
    )(blocks.reshape(everyone, block), down, pick, rows)
    got = lax.all_to_all(
        packed, "req", split_axis=0, concat_axis=0, tiled=True, axis_index_groups=[order]
    )
    delta = pl.pallas_call(
        functools.partial(delta_kernel, ranks),
        out_shape=jax.ShapeDtypeStruct((per_dev, width), F32),
        in_specs=[VMEM],
        out_specs=VMEM,
        compiler_params=PARAMS,
    )(got)
    other = lax.ppermute(delta, "tp", [(0, 1), (1, 0)])
    new_kv, attended = pl.pallas_call(
        merge_kernel,
        out_shape=(
            jax.ShapeDtypeStruct(kv_base.shape, BF16),
            jax.ShapeDtypeStruct(query.shape, BF16),
        ),
        in_specs=[VMEM] * 7,
        out_specs=(VMEM, VMEM),
        scratch_shapes=[pltpu.VMEM((per_dev * heads, HD), F32)],
        compiler_params=PARAMS,
    )(delta, other, kv_base, q_rows, acc, top, total)
    return (new_kv, attended)


def solution(mesh):
    placed = (
        P(("group", "req"), None),
        P("group"),
        P(),
        P(("group", "req")),
        P(("group", "req"), "tp"),
        P(("group", "req"), None),
        P(("group", "req"), None, None),
        P("req", "tp"),
        P("req", "tp", None),
    )
    return jax.shard_map(
        shards,
        mesh=mesh,
        in_specs=placed,
        out_specs=(P(("group", "req"), None), P(("group", "req"), "tp")),
        check_vma=False,
    )
```

time: 78.4 us -> 27.1 us (0.35)
  blocking collectives: 57.3 us -> 9.03 us
  Pallas kernels: 0 us -> 5.99 us
  local copies, waits for them, and re-layouts: 5.86 us -> 0.7 us
  matrix products: 4.2 us -> 0 us
  other arithmetic: 1.91 us -> 0 us
  waiting for transfers between devices: 0.01 us -> 1.87 us
  starting transfers between devices: 7.26 us -> 8.33 us
    all_gather x1 -> x0, blocking collectives: 33.5 us -> none  [shards(): lax.all_gather(adapter_up, 'req', axis=0, tiled=True)]
    unnamed x1 -> x0, blocking collectives: 21.3 us -> none
    all_to_all x0 -> x1, blocking collectives: none -> 9.03 us  [shards(): lax.all_to_all(packed, 'req', split_axis=0, concat_axis=0, tiled=True, ax...]
    pallas_call x0 -> x5, Pallas kernels: none -> 5.99 us  [the longest x1 2.95 us: shards(): pl.pallas_call(functools.partial(local_kernel, order), out_shape=(small,...]
    unnamed x16 -> x4, local copies, waits for them, and re-layouts: 4.96 us -> 0.66 us
    dot_general x6 -> x0, matrix products: 4.2 us -> none  [the longest x1 1.38 us: attend(): jnp.einsum('bhd,bld->bhl', q_rows, keys, preferred_element_type=jnp.float32)]
    psum x1 -> x0, blocking collectives: 2.45 us -> none  [shards(): delta = lax.psum(delta_part, 'tp')]
    ppermute x0 -> x1, waiting for transfers between devices: none -> 1.15 us  [shards(): other = lax.ppermute(delta, 'tp', [(0, 1), (1, 0)])]
  transfers between devices with their start and end apart: 1 -> 2, of which waited for: 0 -> 2; matrix products, arithmetic and copies ran while one was open for 10% -> 0% of each run, Pallas kernels for 0% -> 11%
where the time goes in v2:
time: 27.1 us; the launch traced here: 26.6 us
  blocking collectives  9.03 us (33%)
  starting transfers between devices  8.33 us (31%)
  Pallas kernels  5.99 us (22%)
  waiting for transfers between devices  1.87 us (7%)
  local copies, waits for them, and re-layouts  0.7 us (3%)
  between operations  0.67 us (2%)
    all_to_all x1, blocking collectives, shards(): lax.all_to_all(packed, 'req', split_axis=0, concat_axis=0, tiled=True, ax...  9.03 us
    all_to_all x1, starting transfers between devices, shards(): lax.all_to_all(blocks, 'req', split_axis=0, concat_axis=0, tiled=True, ax...  8.26 us
    pallas_call x1, Pallas kernels, shards(): pl.pallas_call(functools.partial(local_kernel, order), out_shape=(small,...  2.95 us
    pallas_call x1, Pallas kernels, shards(): pl.pallas_call(functools.partial(rotate_kernel, order), out_shape=jax.Sha...  1.55 us
    ppermute x1, waiting for transfers between devices, shards(): other = lax.ppermute(delta, 'tp', [(0, 1), (1, 0)])  1.15 us
    pallas_call x1, Pallas kernels, shards(): pl.pallas_call(merge_kernel, out_shape=(jax.ShapeDtypeStruct(kv_base.shap...  0.71 us
    all_to_all x1, waiting for transfers between devices, shards(): lax.all_to_all(blocks, 'req', split_axis=0, concat_axis=0, tiled=True, ax...  0.71 us
    unnamed x4, local copies, waits for them, and re-layouts  0.66 us
  transfers between devices with their start and end apart: 2, of which 2 were waited for; matrix products, arithmetic and copies ran while one was open for 0% of the time, Pallas kernels for 11%

profile of v2, /device:TPU:0, one launch (start us, length us, event | category | flops | bytes accessed | tf_op | source)
XLA Modules:
  0.0 26.6 jit_solution(17092966118355282638)
XLA Ops:
  0.6 1.5 %shard_map.104 = bf16[8,4,2048]{2,1,0:T(4,128)(2,1)} custom-call(bf16[4,16384]{1,0:T(4,128)(2,1)} %hidden_ref.1), custom_call_target="tpu_custom_call" | custom-call | tf_op jit(solution)/shard_map/pallas_call | solution.py:192
  2.2 8.3 %all-to-all-start = ((bf16[8,4,2048]{2,1,0:T(4,128)(2,1)}), bf16[8,4,2048]{2,1,0:T(4,128)(2,1)S(1)}, u32[]{:S(2)}, u32[]{:S(2)}) async-start(bf16[8,4,2048]{2,1,0:T(4,128)(2,1)} %shard_map.104), calls=%async_computation | async-start | bytes 262144 | tf_op jit(solution)/shard_map/all_to_all | solution.py:203
  10.4 0.0 copy-start.1
  10.4 0.7 %copy-done.1 = s32[4]{0:T(128)S(1)} copy-done((s32[4]{0:T(128)S(1)}, s32[4]{0:T(128)}, u32[]{:S(2)}) %copy-start.1) | copy-done | bytes 40
  11.1 3.0 %shard_map.105 = (f32[32,128]{1,0:T(8,128)S(1)}, f32[32,128]{1,0:T(8,128)S(1)}, f32[32,128]{1,0:T(8,128)S(1)}, f32[32,128]{1,0:T(8,128)S(1)}, bf16[8,4,2048]{2,1...) custom-call(s32[1]{0:T(128)} %bitcast.base_ref, s32[4]{0:T(128)S(1)} %copy-done.1, ...), custom_call_target="tpu_custom_call" | custom-call | tf_op jit(solution)/shard_map/pallas_call | solution.py:207
  14.1 0.0 copy-start
  14.1 0.7 %all-to-all-done = bf16[8,4,2048]{2,1,0:T(4,128)(2,1)S(1)} async-done(((bf16[8,4,2048]{2,1,0:T(4,128)(2,1)}), bf16[8,4,2048]{2,1,0:T(4,128)(2,1)S(1)}, u32[]{:S(2)}, u32[]{:S(2)}) %all-to-all-start) | async-done | bytes 131104 | tf_op jit(solution)/shard_map/all_to_all | solution.py:203
  14.8 0.6 %shard_map.106 = bf16[8,4,2176]{2,1,0:T(4,128)(2,1)S(1)} custom-call(bf16[32,2048]{1,0:T(8,128)(2,1)S(1)} %reshape.16.block_ref, bf16[2048,512]{1,0:T(8,128)(2,1)S(1)} %get-tuple-element.9.down_ref, f32[32,512]{1,0:T(8,128)S(1)} %get-tuple-element.10.pick_ref, bf16[8,4,2048]{2,1,0:T(4,128)(2,1)S(1)} %get-tuple-element.11.rows_ref), custom_call_target="tpu_custom_call" | custom-call | tf_op jit(solution)/shard_map/pallas_call | solution.py:238
  15.4 9.0 %all_to_all.10.got_ref = bf16[8,4,2176]{2,1,0:T(4,128)(2,1)S(1)} all-to-all(bf16[8,4,2176]{2,1,0:T(4,128)(2,1)S(1)} %shard_map.106), channel_id=1, replica_groups={{10,12,14,0,2,4,6,8},{11,13,15,1,3,5,7,9},{26,28,30,16,18,20,22,24},{27..., dimensions={0} | all-to-all | bytes 278528 | tf_op jit(solution)/shard_map/all_to_all | solution.py:245
  24.5 0.2 shard_map.107.mine_ref
  24.6 0.1 collective-permute-start
  24.7 1.2 %collective-permute-done.other_ref = f32[4,256]{1,0:T(4,128)S(1)} collective-permute-done((f32[4,256]{1,0:T(4,128)S(1)}, f32[4,256]{1,0:T(4,128)S(1)}, u32[]{:S(2)}, u32[]{:S(2)}) %collective-permute-start) | collective-permute-done | bytes 4128 | tf_op jit(solution)/shard_map/ppermute | solution.py:255
  25.9 0.0 copy-done
  25.9 0.7 %shard_map.108 = (bf16[4,256]{1,0:T(4,128)(2,1)}, bf16[4,1024]{1,0:T(4,128)(2,1)}) custom-call(f32[4,256]{1,0:T(4,128)S(1)} %shard_map.107.mine_ref, f32[4,256]{1,0:T(4,128)S(1)} %collective-permute-done.other_ref, bf16[4,256]{1,0:T(4,128)(2,1)S(1)} %copy-done, f32[32,128]{1,0:T(8,128)S(1)} %get-tuple-element.12.q_ref, ...), custom_call_target="tpu_custom_call" | custom-call | tf_op jit(solution)/shard_map/pallas_call | solution.py:256
  (1 shorter events, 0.0 us)
Async XLA Ops:
  2.2 12.6 %all-to-all-start = ((bf16[8,4,2048]{2,1,0:T(4,128)(2,1)}), bf16[8,4,2048]{2,1,0:T(4,128)(2,1)S(1)}, u32[]{:S(2)}, u32[]{:S(2)}) async-start(bf16[8,4,2048]{2,1,0:T(4,128)(2,1)} %shard_map.104), calls=%async_computation | async-start | bytes 262144 | tf_op jit(solution)/shard_map/all_to_all | solution.py:203
  10.4 0.7 %copy-start.1 = (s32[4]{0:T(128)S(1)}, s32[4]{0:T(128)}, u32[]{:S(2)}) copy-start(s32[4]{0:T(128)} %lengths_ref.1) | copy-start | bytes 52
  14.1 11.8 %copy-start = (bf16[4,256]{1,0:T(4,128)(2,1)S(1)}, bf16[4,256]{1,0:T(4,128)(2,1)}, u32[]{:S(2)}) copy-start(bf16[4,256]{1,0:T(4,128)(2,1)} %base_ref.1) | copy-start | bytes 6148
  24.6 1.2 %collective-permute-start = (f32[4,256]{1,0:T(4,128)S(1)}, f32[4,256]{1,0:T(4,128)S(1)}, u32[]{:S(2)}, u32[]{:S(2)}) collective-permute-start(f32[4,256]{1,0:T(4,128)S(1)} %shard_map.107.mine_ref), channel_id=1, source_target_pairs={{0,1},{1,0},{2,3},{3,2},{4,5},{5,4},{6,7},{7,6},{8,9},{9,8},{10,11... | collective-permute-start | bytes 12296 | tf_op jit(solution)/shard_map/ppermute | solution.py:255

commit v3 on v0

v3 whole, which is shorter than its diff:
```python
import functools

import jax
import jax.numpy as jnp
from jax import lax
from jax.experimental import pallas as pl
from jax.experimental.pallas import tpu as pltpu
from jax.sharding import PartitionSpec as P

HD = 128
ADAPTERS = 64
F32 = jnp.float32
BF16 = jnp.bfloat16
VMEM = pl.BlockSpec(memory_space=pltpu.VMEM)
SMEM = pl.BlockSpec(memory_space=pltpu.SMEM)
HBM = pl.BlockSpec(memory_space=pltpu.HBM)
PARAMS = pltpu.CompilerParams(vmem_limit_bytes=8 * 1024 * 1024)


def iota(shape, dim):
    return lax.broadcasted_iota(jnp.int32, shape, dim)


def one_hot_ids(ids):
    shape = (ADAPTERS, ids.shape[1])
    return (iota(shape, 0) == jnp.broadcast_to(ids, shape)).astype(BF16)


def across(a, b):
    return lax.dot_general(a, b, (((0,), (0,)), ((), ())), preferred_element_type=F32)


def rotate_kernel(order, hidden_ref, out_ref, sems):
    block = out_ref.shape[2]
    copies = [
        pltpu.make_async_copy(
            hidden_ref.at[:, pl.ds(q * block, block)], out_ref.at[p], sems.at[p]
        )
        for p, q in enumerate(order)
    ]
    for copy in copies:
        copy.start()
    for copy in copies:
        copy.wait()


def pack_kernel(
    order, base_ref, ids_hbm, home_hbm, up_hbm, far_hbm, out_ref,
    ids_ref, home_ref, up_ref, far_ref, flat_ref, wide_ref, sems
):
    pairs = ((ids_hbm, ids_ref), (home_hbm, home_ref), (up_hbm, up_ref), (far_hbm, far_ref))
    copies = [pltpu.make_async_copy(a, b, sems.at[i]) for i, (a, b) in enumerate(pairs)]
    for copy in copies:
        copy.start()
    for copy in copies:
        copy.wait()
    slots, ranks, width = up_ref.shape
    depth = flat_ref.shape[0]
    count = out_ref.shape[1]
    if depth > slots:
        flat_ref[...] = jnp.zeros_like(flat_ref)
    for half, ref in enumerate((up_ref, far_ref)):
        wide_ref[...] = ref[...].astype(F32)
        for r in range(ranks):
            at = (half * ranks + r) * width
            flat_ref[:slots, at : at + width] = wide_ref[:, r, :]
    shape = (depth, ADAPTERS)
    here = jnp.broadcast_to(home_ref[...], shape) - base_ref[0] == iota(shape, 0)
    held = here & (iota(shape, 0) < slots)
    match = jnp.dot(held.astype(BF16), one_hot_ids(ids_ref[...]), preferred_element_type=F32)
    rows = across(match.astype(BF16), flat_ref[...].astype(BF16)).astype(BF16)
    for p, q in enumerate(order):
        out_ref[p] = rows[q * count : (q + 1) * count]


def attend_kernel(
    lengths_ref, query_hbm, far_hbm, cache_hbm, mine_ref, far_ref,
    query_ref, cache_ref, q_ref, sems
):
    pairs = ((query_hbm, query_ref.at[0]), (far_hbm, query_ref.at[1]), (cache_hbm, cache_ref))
    copies = [pltpu.make_async_copy(a, b, sems.at[i]) for i, (a, b) in enumerate(pairs)]
    for copy in copies:
        copy.start()
    for copy in copies:
        copy.wait()
    count = cache_ref.shape[0]
    heads = query_ref.shape[2] // HD
    scale = HD ** (-0.5)
    for half in range(2):
        query = query_ref[half].astype(F32)
        for h in range(heads):
            q_ref[pl.ds(half * heads + h, count, stride=2 * heads), :] = query[
                :, h * HD : (h + 1) * HD
            ]
    for b in range(count):
        scores = lax.dot_general(
            q_ref[b * 2 * heads : (b + 1) * 2 * heads, :].astype(BF16),
            cache_ref[b, :, :HD],
            (((1,), (1,)), ((), ())),
            preferred_element_type=F32,
        )
        valid = iota(scores.shape, 1) < lengths_ref[b]
        scores = jnp.where(valid, scores * scale, -jnp.inf)
        top = jnp.max(scores, axis=1, keepdims=True)
        weights = jnp.exp(scores - top)
        total = jnp.sum(weights, axis=1, keepdims=True)
        acc = jnp.dot(weights.astype(BF16), cache_ref[b, :, HD:], preferred_element_type=F32)
        both = jnp.where(iota(acc.shape, 1) < HD // 2, top, total)
        at = b * heads
        for half, ref in enumerate((mine_ref, far_ref)):
            part = slice(half * heads, (half + 1) * heads)
            ref[at : at + heads, :] = acc[part]
            ref[(count + b) * heads : (count + b + 1) * heads, :] = both[part]


def gather_kernel(got_ref, stats_ref, out_ref):
    total = got_ref[0].astype(F32)
    for p in range(1, got_ref.shape[0]):
        total = total + got_ref[p].astype(F32)
    count, span = total.shape
    for j in range(span // HD):
        out_ref[j * count : (j + 1) * count, :] = total[:, j * HD : (j + 1) * HD]
    out_ref[span // HD * count :, :] = stats_ref[...]


def spare_kernel(*refs):
    pass


def low_kernel(order, ids_ref, block_ref, down_ref, far_hbm, out_ref, far_ref, sems):
    parts, per_dev, _ = out_ref.shape
    depth, columns = down_ref.shape
    ranks = columns // ADAPTERS
    pieces = sems.shape[0]
    step = depth // pieces
    copies = [
        pltpu.make_async_copy(
            far_hbm.at[pl.ds(i * step, step)], far_ref.at[pl.ds(i * step, step)], sems.at[i]
        )
        for i in range(pieces)
    ]
    for copy in copies:
        copy.start()
    names = across(one_hot_ids(ids_ref[...]), iota((ADAPTERS, 128), 0).astype(BF16))
    names = names.astype(jnp.int32)
    shift = order[0] * per_dev
    if shift:
        names = jnp.concatenate([names[shift:], names[:shift]], axis=0)
    lane = iota(names.shape, 1)
    spot = names + lane % 2 * ADAPTERS
    rank = lane % (2 * ranks)

    def take(values, half, low):
        for j in range(columns // 128):
            got = jnp.take_along_axis(values[:, j * 128 : (j + 1) * 128], spot, axis=1)
            low = jnp.where(rank // 2 == j + half * ranks // 2, got, low)
        return low

    near = jnp.dot(block_ref[...], down_ref[...], preferred_element_type=F32)
    low = take(near, 1, jnp.zeros(names.shape, F32))
    far = jnp.zeros(near.shape, F32)
    for i in range(pieces):
        copies[i].wait()
        part = slice(i * step, (i + 1) * step)
        far = far + jnp.dot(block_ref[:, part], far_ref[part, :], preferred_element_type=F32)
    low = take(far, 0, low)
    high = low.astype(BF16).astype(F32)
    low = jnp.where(lane < 2 * ranks, high, low - high).astype(BF16)
    for p in range(parts):
        out_ref[p] = low[p * per_dev : (p + 1) * per_dev]


def total_kernel(ranks, got_ref, out_ref):
    total = got_ref[0].astype(F32)
    for p in range(1, got_ref.shape[0]):
        total = total + got_ref[p].astype(F32)
    total = total + pltpu.roll(total, 128 - 2 * ranks, 1)
    out_ref[: total.shape[0], :] = total.astype(BF16).astype(F32)


def merge_kernel(
    ranks, mine_ref, other_ref, stats_ref, base_ref, query_ref,
    kv_ref, out_ref, q_ref, wide_ref
):
    count, width = base_ref.shape
    heads = query_ref.shape[1] // HD
    halves = width // HD
    scale = HD ** (-0.5)
    lower = lax.axis_index("tp") == 0
    tile = halves * count
    span = 2 * ranks * tile
    query = query_ref[...].astype(F32)
    for h in range(heads):
        q_ref[pl.ds(h, count, stride=heads), :] = query[:, h * HD : (h + 1) * HD]
    low = jnp.where(lower, other_ref[:count, :], mine_ref[:count, :])
    low = jnp.concatenate([low] * halves, axis=0)
    base = base_ref[...].astype(F32)
    fresh = jnp.concatenate([base[:, j * HD : (j + 1) * HD] for j in range(halves)], axis=0)
    for r in range(2 * ranks):
        part = slice(r * tile, (r + 1) * tile)
        row = jnp.where(lower, mine_ref[part, :], other_ref[part, :])
        fresh = fresh + low[:, r : r + 1] * row
    fresh = fresh.astype(BF16).astype(F32)
    for j in range(halves):
        kv_ref[:, j * HD : (j + 1) * HD] = fresh[j * count : (j + 1) * count].astype(BF16)
    for b in range(count):
        part = slice(b * heads, (b + 1) * heads)
        far = slice(span + b * heads, span + (b + 1) * heads)
        key = fresh[b : b + 1]
        value = fresh[count + b : count + b + 1]
        own = jnp.sum(q_ref[part, :] * key, axis=1, keepdims=True) * scale
        acc = jnp.where(lower, stats_ref[part, :], other_ref[far, :])
        part = slice((count + b) * heads, (count + b + 1) * heads)
        far = slice(span + (count + b) * heads, span + (count + b + 1) * heads)
        both = jnp.where(lower, stats_ref[part, :], other_ref[far, :])
        top = both[:, :1]
        high = jnp.maximum(top, own)
        keep = jnp.exp(top - high)
        weight = jnp.exp(own - high)
        norm = 1.0 / (both[:, HD - 1 :] * keep + weight)
        part = slice(b * heads, (b + 1) * heads)
        wide_ref[part, :] = acc * (keep * norm) + (weight * norm) * value
    for h in range(heads):
        out_ref[:, h * HD : (h + 1) * HD] = wide_ref[pl.ds(h, count, stride=heads), :].astype(BF16)


def shards(
    hidden, adapter_ids, home_slot, lengths, query, kv_base, cache, adapter_down, adapter_up
):
    per_dev = hidden.shape[0]
    slots, ranks, width = adapter_up.shape
    parts = lax.axis_size("req")
    everyone = per_dev * parts
    block = hidden.shape[1] // parts
    heads = query.shape[1] // HD
    span = 2 * ranks * width
    center = (parts // 2 + 1) % parts
    order = [(center + p) % parts for p in range(parts)]
    depth = -(-slots // 8) * 8
    base = (lax.axis_index("req") * slots).astype(jnp.int32).reshape(1)
    core = lax.axis_index("tp").astype(jnp.int32)
    swap = [(0, 1), (1, 0)]
    stats_shape = jax.ShapeDtypeStruct((2 * per_dev * heads, HD), F32)
    trade_shape = jax.ShapeDtypeStruct((span // HD * per_dev + 2 * per_dev * heads, HD), F32)
    blocks_shape = jax.ShapeDtypeStruct((parts, per_dev, block), BF16)

    def pin(x):
        return pltpu.with_memory_space_constraint(x, pltpu.HBM)

    def exchange(x):
        return lax.all_to_all(
            x, "req", split_axis=0, concat_axis=0, tiled=True, axis_index_groups=[order]
        )

    ids = adapter_ids.reshape(1, everyone)
    far_up = lax.ppermute(adapter_up, "tp", swap)
    far_query = lax.ppermute(query, "tp", swap)
    blocks = pl.pallas_call(
        functools.partial(rotate_kernel, order),
        out_shape=blocks_shape,
        in_specs=[HBM],
        out_specs=VMEM,
        scratch_shapes=[pltpu.SemaphoreType.DMA((parts,))],
        cost_estimate=pl.CostEstimate(flops=0, transcendentals=0, bytes_accessed=1 << 23),
        compiler_params=PARAMS,
    )(pin(hidden))
    far_up, far_query, down, blocks = lax.optimization_barrier(
        (far_up, far_query, adapter_down, blocks)
    )
    far_down = lax.ppermute(down, "tp", swap)

    def lower(blocks, far_up, far_query, lengths, ids, query, cache, home, up, base):
        packed = pl.pallas_call(
            functools.partial(pack_kernel, order),
            out_shape=jax.ShapeDtypeStruct((parts, per_dev, span), BF16),
            in_specs=[SMEM] + [HBM] * 4,
            out_specs=VMEM,
            scratch_shapes=[
                pltpu.VMEM((1, everyone), jnp.int32),
                pltpu.VMEM((1, ADAPTERS), jnp.int32),
                pltpu.VMEM(up.shape, BF16),
                pltpu.VMEM(up.shape, BF16),
                pltpu.VMEM((depth, span), F32),
                pltpu.VMEM((slots, ranks, width), F32),
                pltpu.SemaphoreType.DMA((4,)),
            ],
            compiler_params=PARAMS,
        )(base, pin(ids), pin(home), pin(up), pin(far_up))
        got = exchange(packed)
        mine, far = pl.pallas_call(
            attend_kernel,
            out_shape=(stats_shape, stats_shape),
            in_specs=[SMEM] + [HBM] * 3,
            out_specs=(VMEM, VMEM),
            scratch_shapes=[
                pltpu.VMEM((2,) + query.shape, BF16),
                pltpu.VMEM(cache.shape, BF16),
                pltpu.VMEM((2 * per_dev * heads, HD), F32),
                pltpu.SemaphoreType.DMA((3,)),
            ],
            compiler_params=PARAMS,
        )(lengths, pin(query), pin(far_query), pin(cache))
        trade = pl.pallas_call(
            gather_kernel,
            out_shape=trade_shape,
            in_specs=[VMEM, VMEM],
            out_specs=VMEM,
            compiler_params=PARAMS,
        )(got, far)
        return blocks, mine, trade

    def upper(blocks, far_up, far_query, lengths, ids, query, cache, home, up, base):
        got = exchange(blocks)
        mine, trade = pl.pallas_call(
            spare_kernel,
            out_shape=(stats_shape, trade_shape),
            in_specs=[VMEM],
            out_specs=(VMEM, VMEM),
            compiler_params=PARAMS,
        )(got)
        return got, mine, trade

    got, stats, trade = lax.cond(
        core == 1, upper, lower,
        blocks, far_up, far_query, lengths, ids, query, cache,
        home_slot.reshape(1, ADAPTERS), adapter_up, base,
    )
    pieces = 4 if block % 64 == 0 else 1

    def upper_low(ids, got, down, far_down, trade):
        low = pl.pallas_call(
            functools.partial(low_kernel, order),
            out_shape=jax.ShapeDtypeStruct((parts, per_dev, 128), BF16),
            in_specs=[VMEM] * 3 + [HBM],
            out_specs=VMEM,
            scratch_shapes=[
                pltpu.VMEM(adapter_down.shape, BF16),
                pltpu.SemaphoreType.DMA((pieces,)),
            ],
            compiler_params=PARAMS,
        )(ids, got, down, pin(far_down))
        return pl.pallas_call(
            functools.partial(total_kernel, ranks),
            out_shape=trade_shape,
            in_specs=[VMEM],
            out_specs=VMEM,
            compiler_params=PARAMS,
        )(exchange(low))

    def lower_low(ids, got, down, far_down, trade):
        return trade

    mine = lax.cond(
        core == 1, upper_low, lower_low,
        ids, got.reshape(everyone, block), adapter_down, far_down, trade,
    )
    other = lax.ppermute(mine, "tp", swap)
    new_kv, attended = pl.pallas_call(
        functools.partial(merge_kernel, ranks),
        out_shape=(
            jax.ShapeDtypeStruct(kv_base.shape, BF16),
            jax.ShapeDtypeStruct(query.shape, BF16),
        ),
        in_specs=[VMEM] * 5,
        out_specs=(VMEM, VMEM),
        scratch_shapes=[
            pltpu.VMEM((per_dev * heads, HD), F32),
            pltpu.VMEM((per_dev * heads, HD), F32),
        ],
        compiler_params=PARAMS,
    )(mine, other, stats, kv_base, query)
    return (new_kv, attended)


def solution(mesh):
    placed = (
        P(("group", "req"), None),
        P("group"),
        P(),
        P(("group", "req")),
        P(("group", "req"), "tp"),
        P(("group", "req"), None),
        P(("group", "req"), None, None),
        P("req", "tp"),
        P("req", "tp", None),
    )
    return jax.shard_map(
        shards,
        mesh=mesh,
        in_specs=placed,
        out_specs=(P(("group", "req"), None), P(("group", "req"), "tp")),
        check_vma=False,
    )
```

time: 78.4 us -> 25.3 us (0.32)
  blocking collectives: 57.3 us -> 0 us
  Pallas kernels: 0 us -> 6.98 us
  starting transfers between devices: 7.26 us -> 13.4 us
  local copies, waits for them, and re-layouts: 5.86 us -> 0.63 us
  matrix products: 4.2 us -> 0 us
  waiting for transfers between devices: 0.01 us -> 3.23 us
  other arithmetic: 1.91 us -> 0 us
    all_gather x1 -> x0, blocking collectives: 33.5 us -> none  [shards(): lax.all_gather(adapter_up, 'req', axis=0, tiled=True)]
    unnamed x1 -> x0, blocking collectives: 21.3 us -> none
    pallas_call x0 -> x5, Pallas kernels: none -> 6.98 us  [the longest x1 3.02 us: lower(): pl.pallas_call(attend_kernel, out_shape=(stats_shape, stats_shape), in_sp...]
    ppermute x0 -> x4, starting transfers between devices: none -> 5.18 us  [the longest x1 4.41 us: shards(): other = lax.ppermute(mine, 'tp', swap)]
    unnamed x16 -> x6, local copies, waits for them, and re-layouts: 4.96 us -> 0.02 us
    dot_general x6 -> x0, matrix products: 4.2 us -> none  [the longest x1 1.38 us: attend(): jnp.einsum('bhd,bld->bhl', q_rows, keys, preferred_element_type=jnp.float32)]
    psum x1 -> x0, blocking collectives: 2.45 us -> none  [shards(): delta = lax.psum(delta_part, 'tp')]
    all_to_all x1, waiting for transfers between devices: 0.01 us -> 1.92 us  [exchange(): lax.all_to_all(x, 'req', split_axis=0, concat_axis=0, tiled=True, axis_in...]
  transfers between devices with their start and end apart: 1 -> 5, of which waited for: 0 -> 3; matrix products, arithmetic and copies ran while one was open for 10% -> 0% of each run, Pallas kernels for 0% -> 24%
where the time goes in v3:
time: 25.3 us; the launch traced here: 24.9 us
  starting transfers between devices  13.4 us (53%)
  Pallas kernels  6.98 us (28%)
  waiting for transfers between devices  3.23 us (13%)
  between operations  0.7 us (3%)
  local copies, waits for them, and re-layouts  0.63 us (2%)
    all_to_all x1, starting transfers between devices, exchange(): lax.all_to_all(x, 'req', split_axis=0, concat_axis=0, tiled=True, axis_in...  8.19 us
    ppermute x1, starting transfers between devices, shards(): other = lax.ppermute(mine, 'tp', swap)  4.41 us
    pallas_call x1, Pallas kernels, lower(): pl.pallas_call(attend_kernel, out_shape=(stats_shape, stats_shape), in_sp...  3.02 us
    pallas_call x1, Pallas kernels, lower(): pl.pallas_call(functools.partial(pack_kernel, order), out_shape=jax.Shape...  1.95 us
    all_to_all x1, waiting for transfers between devices, exchange(): lax.all_to_all(x, 'req', split_axis=0, concat_axis=0, tiled=True, axis_in...  1.92 us
    pallas_call x1, Pallas kernels, shards(): pl.pallas_call(functools.partial(merge_kernel, ranks), out_shape=(jax.Sha...  1.03 us
    ppermute x1, waiting for transfers between devices, shards(): other = lax.ppermute(mine, 'tp', swap)  0.94 us
    pallas_call x1, Pallas kernels, shards(): pl.pallas_call(functools.partial(rotate_kernel, order), out_shape=blocks_...  0.94 us
  transfers between devices with their start and end apart: 5, of which 3 were waited for; matrix products, arithmetic and copies ran while one was open for 0% of the time, Pallas kernels for 24%

profile of v3, /device:TPU:0, one launch (start us, length us, event | category | flops | bytes accessed | tf_op | source)
XLA Modules:
  0.0 24.9 jit_solution(16240432032308445946)
XLA Ops:
  0.6 0.0 copy-start.1
  0.6 0.5 %collective-permute-start = (bf16[8,8,256]{2,1,0:T(8,128)(2,1)}, bf16[8,8,256]{2,1,0:T(8,128)(2,1)S(1)}, u32[]{:S(2)}, u32[]{:S(2)}) collective-permute-start(bf16[8,8,256]{2,1,0:T(8,128)(2,1)} %param.21), channel_id=1, source_target_pairs={{0,1},{1,0},{2,3},{3,2},{4,5},{5,4},{6,7},{7,6},{8,9},{9,8},{10,11... | collective-permute-start | bytes 98312 | tf_op jit(solution)/shard_map/ppermute | solution.py:256
  1.2 0.1 collective-permute-start.1
  1.2 0.9 %shard_map.107 = bf16[8,4,2048]{2,1,0:T(4,128)(2,1)S(1)} custom-call(bf16[4,16384]{1,0:T(4,128)(2,1)} %hidden_ref.1), custom_call_target="tpu_custom_call" | custom-call | bytes 8388608 | tf_op jit(solution)/shard_map/pallas_call | solution.py:258
  2.2 0.4 %collective-permute-done.1 = bf16[4,1024]{1,0:T(4,128)(2,1)S(1)} collective-permute-done((bf16[4,1024]{1,0:T(4,128)(2,1)}, bf16[4,1024]{1,0:T(4,128)(2,1)S(1)}, u32[]{:S(2)}, u32[]{:S(2)}) %collective-permute-start.1) | collective-permute-done | bytes 8224 | tf_op jit(solution)/shard_map/ppermute | solution.py:257
  2.5 0.0 collective-permute-done
  2.5 0.2 collective-permute-start.2
  2.7 15.8 %conditional.2 = (bf16[8,4,2048]{2,1,0:T(4,128)(2,1)S(1)}, f32[64,128]{1,0:T(8,128)S(1)}, f32[192,128]{1,0:T(8,128)S(1)}) conditional(s32[]{:T(128)} %convert_element_type.4, (s32[4]{0:T(128)}, bf16[4,1024]{1,0:T(4,128)(2,1)}, bf16[4,1024]{1,0:T(4,128)(2,1)S(1)}, bf16[4,512,256]{2,1,0:T(8,128)(2,1)}, s32[]{:T(128)}, /*index=5*/s32[64]{0:T(128)}, ...), branch_computations={%region_0.0_spmd, %region_1.0_spmd} | conditional | flops 1 | bytes 950396 | solution.py:323
  2.7 0.0 copy-start.2
  2.7 0.0 copy-start.4
  2.7 0.6 %copy-done.2 = bf16[8,8,256]{2,1,0:T(8,128)(2,1)} copy-done((bf16[8,8,256]{2,1,0:T(8,128)(2,1)}, bf16[8,8,256]{2,1,0:T(8,128)(2,1)S(1)}, u32[]{:S(2)}) %copy-start.2) | copy-done | bytes 32792 | tf_op jit(solution)/shard_map/cond
  3.3 2.0 %branch_0_fun.4 = bf16[8,4,4096]{2,1,0:T(4,128)(2,1)} custom-call(s32[1]{0:T(128)} %bitcast.base_ref, s32[1,32]{1,0:T(1,128)} %get-tuple-element.46.ids_hbm, s32[1,64]{1,0:T(1,128)} %bitcast.5, bf16[8,8,256]{2,1,0:T(8,128)(2,1)} %get-tuple-element.48.up_hbm, bf16[8,8,256]{2,1,0:T(8,128)(2,1)} %copy-done.2), custom_call_target="tpu_custom_call" | custom-call | tf_op jit(solution)/shard_map/cond/branch_0_fun/pallas_call | solution.py:273
  5.3 8.2 %all-to-all-start = ((bf16[8,4,4096]{2,1,0:T(4,128)(2,1)}), bf16[8,4,4096]{2,1,0:T(4,128)(2,1)S(1)}, u32[]{:S(2)}, u32[]{:S(2)}) async-start(bf16[8,4,4096]{2,1,0:T(4,128)(2,1)} %branch_0_fun.4), calls=%async_computation | async-start | bytes 524288 | tf_op jit(solution)/shard_map/cond/branch_0_fun/all_to_all | solution.py:251
  13.5 0.0 copy-done.4
  13.5 3.0 %branch_0_fun.3 = (f32[64,128]{1,0:T(8,128)S(1)}, f32[64,128]{1,0:T(8,128)S(1)}) custom-call(s32[4]{0:T(128)} %get-tuple-element.76.lengths_ref, bf16[4,1024]{1,0:T(4,128)(2,1)} %get-tuple-element.41.query_hbm, bf16[4,1024]{1,0:T(4,128)(2,1)} %copy-done.4, bf16[4,512,256]{2,1,0:T(8,128)(2,1)} %get-tuple-element.77.cache_hbm), custom_call_target="tpu_custom_call" | custom-call | tf_op jit(solution)/shard_map/cond/branch_0_fun/pallas_call | solution.py:290
  16.5 1.9 %all-to-all-done.got_ref = bf16[8,4,4096]{2,1,0:T(4,128)(2,1)S(1)} async-done(((bf16[8,4,4096]{2,1,0:T(4,128)(2,1)}), bf16[8,4,4096]{2,1,0:T(4,128)(2,1)S(1)}, u32[]{:S(2)}, u32[]{:S(2)}) %all-to-all-start) | async-done | bytes 262176 | tf_op jit(solution)/shard_map/cond/branch_0_fun/all_to_all | solution.py:251
  18.5 0.0 collective-permute-done.2
  18.5 0.0 copy-done.1
  18.5 0.0 copy-start
  18.5 0.0 copy-start.3
  18.5 4.4 %collective-permute-start.3 = (f32[192,128]{1,0:T(8,128)S(1)}, f32[192,128]{1,0:T(8,128)S(1)}, u32[]{:S(2)}, u32[]{:S(2)}) collective-permute-start(f32[192,128]{1,0:T(8,128)S(1)} %get-tuple-element.85.mine_ref), channel_id=1, source_target_pairs={{0,1},{1,0},{2,3},{3,2},{4,5},{5,4},{6,7},{7,6},{8,9},{9,8},{10,11... | collective-permute-start | bytes 294920 | tf_op jit(solution)/shard_map/ppermute | solution.py:357
  23.0 0.9 %collective-permute-done.3.other_ref = f32[192,128]{1,0:T(8,128)S(1)} collective-permute-done((f32[192,128]{1,0:T(8,128)S(1)}, f32[192,128]{1,0:T(8,128)S(1)}, u32[]{:S(2)}, u32[]{:S(2)}) %collective-permute-start.3) | collective-permute-done | bytes 98336 | tf_op jit(solution)/shard_map/ppermute | solution.py:357
  23.9 0.0 copy-done
  23.9 0.0 copy-done.3
  23.9 1.0 %shard_map.108 = (bf16[4,256]{1,0:T(4,128)(2,1)}, bf16[4,1024]{1,0:T(4,128)(2,1)}) custom-call(f32[192,128]{1,0:T(8,128)S(1)} %get-tuple-element.85.mine_ref, f32[192,128]{1,0:T(8,128)S(1)} %collective-permute-done.3.other_ref, f32[64,128]{1,0:T(8,128)S(1)} %get-tuple-element.72.stats_ref, bf16[4,256]{1,0:T(4,128)(2,1)S(1)} %copy-done, ...), custom_call_target="tpu_custom_call" | custom-call | tf_op jit(solution)/shard_map/pallas_call | solution.py:358
  (2 shorter events, 0.0 us)
Async XLA Ops:
  0.6 17.9 %copy-start.1 = (bf16[2048,512]{1,0:T(8,128)(2,1)S(1)}, bf16[2048,512]{1,0:T(8,128)(2,1)}, u32[]{:S(2)}) copy-start(bf16[2048,512]{1,0:T(8,128)(2,1)} %param.20) | copy-start | bytes 6291460
  0.6 1.9 %collective-permute-start = (bf16[8,8,256]{2,1,0:T(8,128)(2,1)}, bf16[8,8,256]{2,1,0:T(8,128)(2,1)S(1)}, u32[]{:S(2)}, u32[]{:S(2)}) collective-permute-start(bf16[8,8,256]{2,1,0:T(8,128)(2,1)} %param.21), channel_id=1, source_target_pairs={{0,1},{1,0},{2,3},{3,2},{4,5},{5,4},{6,7},{7,6},{8,9},{9,8},{10,11... | collective-permute-start | bytes 98312 | tf_op jit(solution)/shard_map/ppermute | solution.py:256
  1.2 1.4 %collective-permute-start.1 = (bf16[4,1024]{1,0:T(4,128)(2,1)}, bf16[4,1024]{1,0:T(4,128)(2,1)S(1)}, u32[]{:S(2)}, u32[]{:S(2)}) collective-permute-start(bf16[4,1024]{1,0:T(4,128)(2,1)} %query_ref.1), channel_id=1, source_target_pairs={{0,1},{1,0},{2,3},{3,2},{4,5},{5,4},{6,7},{7,6},{8,9},{9,8},{10,11... | collective-permute-start | bytes 24584 | tf_op jit(solution)/shard_map/ppermute | solution.py:257
  2.5 15.9 %collective-permute-start.2 = (bf16[2048,512]{1,0:T(8,128)(2,1)}, bf16[2048,512]{1,0:T(8,128)(2,1)}, u32[]{:S(2)}, u32[]{:S(2)}) collective-permute-start(bf16[2048,512]{1,0:T(8,128)(2,1)} %param.20), channel_id=1, source_target_pairs={{0,1},{1,0},{2,3},{3,2},{4,5},{5,4},{6,7},{7,6},{8,9},{9,8},{10,11... | collective-permute-start | bytes 6291464 | tf_op jit(solution)/shard_map/ppermute | solution.py:270
  2.7 0.6 %copy-start.2 = (bf16[8,8,256]{2,1,0:T(8,128)(2,1)}, bf16[8,8,256]{2,1,0:T(8,128)(2,1)S(1)}, u32[]{:S(2)}) copy-start(bf16[8,8,256]{2,1,0:T(8,128)(2,1)S(1)} %get-tuple-element.49.far_hbm) | copy-start | bytes 98308 | tf_op jit(solution)/shard_map/cond
  2.7 10.8 %copy-start.4 = (bf16[4,1024]{1,0:T(4,128)(2,1)}, bf16[4,1024]{1,0:T(4,128)(2,1)S(1)}, u32[]{:S(2)}) copy-start(bf16[4,1024]{1,0:T(4,128)(2,1)S(1)} %get-tuple-element.42.far_hbm) | copy-start | bytes 24580 | tf_op jit(solution)/shard_map/cond
  5.3 13.1 %all-to-all-start = ((bf16[8,4,4096]{2,1,0:T(4,128)(2,1)}), bf16[8,4,4096]{2,1,0:T(4,128)(2,1)S(1)}, u32[]{:S(2)}, u32[]{:S(2)}) async-start(bf16[8,4,4096]{2,1,0:T(4,128)(2,1)} %branch_0_fun.4), calls=%async_computation | async-start | bytes 524288 | tf_op jit(solution)/shard_map/cond/branch_0_fun/all_to_all | solution.py:251
  18.5 5.4 %copy-start = (bf16[4,256]{1,0:T(4,128)(2,1)S(1)}, bf16[4,256]{1,0:T(4,128)(2,1)}, u32[]{:S(2)}) copy-start(bf16[4,256]{1,0:T(4,128)(2,1)} %base_ref.1) | copy-start | bytes 6148
  18.5 5.4 %copy-start.3 = (bf16[4,1024]{1,0:T(4,128)(2,1)S(1)}, bf16[4,1024]{1,0:T(4,128)(2,1)}, u32[]{:S(2)}) copy-start(bf16[4,1024]{1,0:T(4,128)(2,1)} %query_ref.1) | copy-start | bytes 24580
  18.5 5.4 %collective-permute-start.3 = (f32[192,128]{1,0:T(8,128)S(1)}, f32[192,128]{1,0:T(8,128)S(1)}, u32[]{:S(2)}, u32[]{:S(2)}) collective-permute-start(f32[192,128]{1,0:T(8,128)S(1)} %get-tuple-element.85.mine_ref), channel_id=1, source_target_pairs={{0,1},{1,0},{2,3},{3,2},{4,5},{5,4},{6,7},{7,6},{8,9},{9,8},{10,11... | collective-permute-start | bytes 294920 | tf_op jit(solution)/shard_map/ppermute | solution.py:357

commit v4 on v3

--- a/solution.py
+++ b/solution.py
@@ -32,23 +32,26 @@
 
 def rotate_kernel(order, hidden_ref, out_ref, sems):
     block = out_ref.shape[2]
-    copies = [
-        pltpu.make_async_copy(
-            hidden_ref.at[:, pl.ds(q * block, block)], out_ref.at[p], sems.at[p]
-        )
-        for p, q in enumerate(order)
-    ]
-    for copy in copies:
-        copy.start()
-    for copy in copies:
-        copy.wait()
+
+    @pl.when(lax.axis_index("tp") == 1)
+    def _():
+        copies = [
+            pltpu.make_async_copy(
+                hidden_ref.at[:, pl.ds(q * block, block)], out_ref.at[p], sems.at[p]
+            )
+            for p, q in enumerate(order)
+        ]
+        for copy in copies:
+            copy.start()
+        for copy in copies:
+            copy.wait()
 
 
 def pack_kernel(
-    order, base_ref, ids_hbm, home_hbm, up_hbm, far_hbm, out_ref,
-    ids_ref, home_ref, up_ref, far_ref, flat_ref, wide_ref, sems
+    order, base_ref, ids_hbm, home_hbm, up_hbm, far_ref, out_ref,
+    ids_ref, home_ref, up_ref, flat_ref, wide_ref, sems
 ):
-    pairs = ((ids_hbm, ids_ref), (home_hbm, home_ref), (up_hbm, up_ref), (far_hbm, far_ref))
+    pairs = ((ids_hbm, ids_ref), (home_hbm, home_ref), (up_hbm, up_ref))
     copies = [pltpu.make_async_copy(a, b, sems.at[i]) for i, (a, b) in enumerate(pairs)]
     for copy in copies:
         copy.start()
@@ -74,20 +77,20 @@
 
 
 def attend_kernel(
-    lengths_ref, query_hbm, far_hbm, cache_hbm, mine_ref, far_ref,
+    lengths_ref, query_hbm, far_query_ref, cache_hbm, mine_ref, far_ref,
     query_ref, cache_ref, q_ref, sems
 ):
-    pairs = ((query_hbm, query_ref.at[0]), (far_hbm, query_ref.at[1]), (cache_hbm, cache_ref))
+    pairs = ((query_hbm, query_ref), (cache_hbm, cache_ref))
     copies = [pltpu.make_async_copy(a, b, sems.at[i]) for i, (a, b) in enumerate(pairs)]
     for copy in copies:
         copy.start()
     for copy in copies:
         copy.wait()
     count = cache_ref.shape[0]
-    heads = query_ref.shape[2] // HD
+    heads = query_ref.shape[1] // HD
     scale = HD ** (-0.5)
-    for half in range(2):
-        query = query_ref[half].astype(F32)
+    for half, ref in enumerate((query_ref, far_query_ref)):
+        query = ref[...].astype(F32)
         for h in range(heads):
             q_ref[pl.ds(half * heads + h, count, stride=2 * heads), :] = query[
                 :, h * HD : (h + 1) * HD
@@ -127,12 +130,16 @@
     pass
 
 
-def low_kernel(order, ids_ref, block_ref, down_ref, far_hbm, out_ref, far_ref, sems):
+def low_kernel(
+    order, ids_hbm, block_ref, down_ref, far_hbm, out_ref, ids_ref, far_ref, low_ref, sems
+):
     parts, per_dev, _ = out_ref.shape
     depth, columns = down_ref.shape
     ranks = columns // ADAPTERS
-    pieces = sems.shape[0]
+    pieces = sems.shape[0] - 1
     step = depth // pieces
+    named = pltpu.make_async_copy(ids_hbm, ids_ref, sems.at[pieces])
+    named.start()
     copies = [
         pltpu.make_async_copy(
             far_hbm.at[pl.ds(i * step, step)], far_ref.at[pl.ds(i * step, step)], sems.at[i]
@@ -141,6 +148,8 @@
     ]
     for copy in copies:
         copy.start()
+    near = jnp.dot(block_ref[...], down_ref[...], preferred_element_type=F32)
+    named.wait()
     names = across(one_hot_ids(ids_ref[...]), iota((ADAPTERS, 128), 0).astype(BF16))
     names = names.astype(jnp.int32)
     shift = order[0] * per_dev
@@ -156,14 +165,13 @@
             low = jnp.where(rank // 2 == j + half * ranks // 2, got, low)
         return low
 
-    near = jnp.dot(block_ref[...], down_ref[...], preferred_element_type=F32)
-    low = take(near, 1, jnp.zeros(names.shape, F32))
+    low_ref[...] = take(near, 1, jnp.zeros(names.shape, F32))
     far = jnp.zeros(near.shape, F32)
     for i in range(pieces):
         copies[i].wait()
         part = slice(i * step, (i + 1) * step)
         far = far + jnp.dot(block_ref[:, part], far_ref[part, :], preferred_element_type=F32)
-    low = take(far, 0, low)
+    low = take(far, 0, low_ref[...])
     high = low.astype(BF16).astype(F32)
     low = jnp.where(lane < 2 * ranks, high, low - high).astype(BF16)
     for p in range(parts):
@@ -253,8 +261,6 @@
         )
 
     ids = adapter_ids.reshape(1, everyone)
-    far_up = lax.ppermute(adapter_up, "tp", swap)
-    far_query = lax.ppermute(query, "tp", swap)
     blocks = pl.pallas_call(
         functools.partial(rotate_kernel, order),
         out_shape=blocks_shape,
@@ -264,42 +270,45 @@
         cost_estimate=pl.CostEstimate(flops=0, transcendentals=0, bytes_accessed=1 << 23),
         compiler_params=PARAMS,
     )(pin(hidden))
-    far_up, far_query, down, blocks = lax.optimization_barrier(
-        (far_up, far_query, adapter_down, blocks)
+    blocks, near_up, near_query, near_down = lax.optimization_barrier(
+        (blocks, adapter_up, query, adapter_down)
     )
-    far_down = lax.ppermute(down, "tp", swap)
-
-    def lower(blocks, far_up, far_query, lengths, ids, query, cache, home, up, base):
+    far_up = lax.ppermute(near_up, "tp", swap)
+    far_query = lax.ppermute(near_query, "tp", swap)
+    far_down = lax.ppermute(near_down, "tp", swap)
+    got = lax.cond(core == 1, exchange, lambda blocks: blocks, blocks)
+    got, far_up, far_query = lax.optimization_barrier((got, far_up, far_query))
+
+    def lower(far_up, far_query, lengths, ids, query, cache, home, up, base):
         packed = pl.pallas_call(
             functools.partial(pack_kernel, order),
             out_shape=jax.ShapeDtypeStruct((parts, per_dev, span), BF16),
-            in_specs=[SMEM] + [HBM] * 4,
+            in_specs=[SMEM] + [HBM] * 3 + [VMEM],
             out_specs=VMEM,
             scratch_shapes=[
                 pltpu.VMEM((1, everyone), jnp.int32),
                 pltpu.VMEM((1, ADAPTERS), jnp.int32),
                 pltpu.VMEM(up.shape, BF16),
-                pltpu.VMEM(up.shape, BF16),
                 pltpu.VMEM((depth, span), F32),
                 pltpu.VMEM((slots, ranks, width), F32),
-                pltpu.SemaphoreType.DMA((4,)),
+                pltpu.SemaphoreType.DMA((3,)),
             ],
             compiler_params=PARAMS,
-        )(base, pin(ids), pin(home), pin(up), pin(far_up))
+        )(base, pin(ids), pin(home), pin(up), far_up)
         got = exchange(packed)
         mine, far = pl.pallas_call(
             attend_kernel,
             out_shape=(stats_shape, stats_shape),
-            in_specs=[SMEM] + [HBM] * 3,
+            in_specs=[SMEM, HBM, VMEM, HBM],
             out_specs=(VMEM, VMEM),
             scratch_shapes=[
-                pltpu.VMEM((2,) + query.shape, BF16),
+                pltpu.VMEM(query.shape, BF16),
                 pltpu.VMEM(cache.shape, BF16),
                 pltpu.VMEM((2 * per_dev * heads, HD), F32),
-                pltpu.SemaphoreType.DMA((3,)),
+                pltpu.SemaphoreType.DMA((2,)),
             ],
             compiler_params=PARAMS,
-        )(lengths, pin(query), pin(far_query), pin(cache))
+        )(lengths, pin(query), far_query, pin(cache))
         trade = pl.pallas_call(
             gather_kernel,
             out_shape=trade_shape,
@@ -307,38 +316,39 @@
             out_specs=VMEM,
             compiler_params=PARAMS,
         )(got, far)
-        return blocks, mine, trade
-
-    def upper(blocks, far_up, far_query, lengths, ids, query, cache, home, up, base):
-        got = exchange(blocks)
-        mine, trade = pl.pallas_call(
+        return mine, trade
+
+    def upper(far_up, far_query, lengths, ids, query, cache, home, up, base):
+        return pl.pallas_call(
             spare_kernel,
             out_shape=(stats_shape, trade_shape),
-            in_specs=[VMEM],
+            in_specs=[],
             out_specs=(VMEM, VMEM),
             compiler_params=PARAMS,
-        )(got)
-        return got, mine, trade
-
-    got, stats, trade = lax.cond(
+        )()
+
+    stats, trade = lax.cond(
         core == 1, upper, lower,
-        blocks, far_up, far_query, lengths, ids, query, cache,
+        far_up, far_query, lengths, ids, query, cache,
         home_slot.reshape(1, ADAPTERS), adapter_up, base,
     )
+    far_down, trade = lax.optimization_barrier((far_down, trade))
     pieces = 4 if block % 64 == 0 else 1
 
     def upper_low(ids, got, down, far_down, trade):
         low = pl.pallas_call(
             functools.partial(low_kernel, order),
             out_shape=jax.ShapeDtypeStruct((parts, per_dev, 128), BF16),
-            in_specs=[VMEM] * 3 + [HBM],
+            in_specs=[HBM, VMEM, VMEM, HBM],
             out_specs=VMEM,
             scratch_shapes=[
+                pltpu.VMEM((1, everyone), jnp.int32),
                 pltpu.VMEM(adapter_down.shape, BF16),
-                pltpu.SemaphoreType.DMA((pieces,)),
+                pltpu.VMEM((everyone, 128), F32),
+                pltpu.SemaphoreType.DMA((pieces + 1,)),
             ],
             compiler_params=PARAMS,
-        )(ids, got, down, pin(far_down))
+        )(pin(ids), got, down, pin(far_down))
         return pl.pallas_call(
             functools.partial(total_kernel, ranks),
             out_shape=trade_shape,

time: 25.3 us -> 24 us (0.949)
  waiting for transfers between devices: 3.23 us -> 6.32 us
  starting transfers between devices: 13.4 us -> 10.6 us
  Pallas kernels: 6.98 us -> 6.07 us
  local copies, waits for them, and re-layouts: 0.63 us -> 0.02 us
    ppermute x1, starting transfers between devices: 4.41 us -> 0.89 us  [shards(): other = lax.ppermute(mine, 'tp', swap)]
    ppermute x3, waiting for transfers between devices: 0.36 us -> 3.42 us  [the longest x1 3.42 us: shards(): far_query = lax.ppermute(near_query, 'tp', swap)]
    ppermute x3, starting transfers between devices: 0.77 us -> 1.99 us  [the longest x1 1.48 us: shards(): far_down = lax.ppermute(near_down, 'tp', swap)]
    pallas_call x1, Pallas kernels: 0.94 us -> 0.09 us  [shards(): pl.pallas_call(functools.partial(rotate_kernel, order), out_shape=blocks_...]
    cond x4 -> x0, local copies, waits for them, and re-layouts: 0.61 us -> none
    all_to_all x1, starting transfers between devices: 8.19 us -> 7.68 us  [exchange(): lax.all_to_all(x, 'req', split_axis=0, concat_axis=0, tiled=True, axis_in...]
  transfers between devices with their start and end apart: 5 -> 5, of which waited for: 3 -> 3; matrix products, arithmetic and copies ran while one was open for 0% -> 0% of each run, Pallas kernels for 24% -> 21%
where the time goes in v4:
time: 24 us; the launch traced here: 23.7 us
  starting transfers between devices  10.6 us (44%)
  waiting for transfers between devices  6.32 us (26%)
  Pallas kernels  6.07 us (25%)
  between operations  0.7 us (3%)
    all_to_all x1, starting transfers between devices, exchange(): lax.all_to_all(x, 'req', split_axis=0, concat_axis=0, tiled=True, axis_in...  7.68 us
    ppermute x1, waiting for transfers between devices, shards(): far_query = lax.ppermute(near_query, 'tp', swap)  3.42 us
    pallas_call x1, Pallas kernels, lower(): pl.pallas_call(attend_kernel, out_shape=(stats_shape, stats_shape), in_sp...  3 us
    all_to_all x1, waiting for transfers between devices, exchange(): lax.all_to_all(x, 'req', split_axis=0, concat_axis=0, tiled=True, axis_in...  1.96 us
    pallas_call x1, Pallas kernels, lower(): pl.pallas_call(functools.partial(pack_kernel, order), out_shape=jax.Shape...  1.91 us
    ppermute x1, starting transfers between devices, shards(): far_down = lax.ppermute(near_down, 'tp', swap)  1.48 us
    pallas_call x1, Pallas kernels, shards(): pl.pallas_call(functools.partial(merge_kernel, ranks), out_shape=(jax.Sha...  1.03 us
    ppermute x1, waiting for transfers between devices, shards(): other = lax.ppermute(mine, 'tp', swap)  0.94 us
  transfers between devices with their start and end apart: 5, of which 3 were waited for; matrix products, arithmetic and copies ran while one was open for 0% of the time, Pallas kernels for 21%

profile of v4, /device:TPU:0, one launch (start us, length us, event | category | flops | bytes accessed | tf_op | source)
XLA Modules:
  0.0 23.7 jit_solution(5756674261175709873)
XLA Ops:
  0.6 0.0 copy-start.1
  0.6 0.1 shard_map.107
  0.7 1.5 %collective-permute-start = (bf16[2048,512]{1,0:T(8,128)(2,1)}, bf16[2048,512]{1,0:T(8,128)(2,1)}, u32[]{:S(2)}, u32[]{:S(2)}) collective-permute-start(bf16[2048,512]{1,0:T(8,128)(2,1)} %param.22), channel_id=1, source_target_pairs={{0,1},{1,0},{2,3},{3,2},{4,5},{5,4},{6,7},{7,6},{8,9},{9,8},{10,11... | collective-permute-start | bytes 6291464 | tf_op jit(solution)/shard_map/ppermute | solution.py:278
  2.2 0.1 collective-permute-start.1
  2.3 0.4 %collective-permute-start.2 = (bf16[4,1024]{1,0:T(4,128)(2,1)}, bf16[4,1024]{1,0:T(4,128)(2,1)S(1)}, u32[]{:S(2)}, u32[]{:S(2)}) collective-permute-start(bf16[4,1024]{1,0:T(4,128)(2,1)} %query_ref.1), channel_id=1, source_target_pairs={{0,1},{1,0},{2,3},{3,2},{4,5},{5,4},{6,7},{7,6},{8,9},{9,8},{10,11... | collective-permute-start | bytes 24584 | tf_op jit(solution)/shard_map/ppermute | solution.py:277
  2.7 3.4 %collective-permute-done.2 = bf16[4,1024]{1,0:T(4,128)(2,1)S(1)} collective-permute-done((bf16[4,1024]{1,0:T(4,128)(2,1)}, bf16[4,1024]{1,0:T(4,128)(2,1)S(1)}, u32[]{:S(2)}, u32[]{:S(2)}) %collective-permute-start.2) | collective-permute-done | bytes 8224 | tf_op jit(solution)/shard_map/ppermute | solution.py:277
  6.1 0.0 collective-permute-done.1
  6.2 14.6 %conditional.4 = ((f32[64,128]{1,0:T(8,128)S(1)}, f32[192,128]{1,0:T(8,128)S(1)})) conditional(s32[]{:T(128)} %convert_element_type.2, (s32[4]{0:T(128)}, bf16[4,1024]{1,0:T(4,128)(2,1)}, bf16[4,1024]{1,0:T(4,128)(2,1)S(1)}, bf16[4,512,256]{2,1,0:T(8,128)(2,1)}, s32[]{:T(128)}, /*index=5*/s32[64]{0:T(128)}, s32[1,32]{1,0:T(1,128)}, ...), branch_computations={%region_2.0_spmd, %region_3.0_spmd} | conditional | flops 1 | bytes 786500 | solution.py:330
  6.2 1.9 %branch_0_fun.4 = bf16[8,4,4096]{2,1,0:T(4,128)(2,1)} custom-call(s32[1]{0:T(128)} %bitcast.base_ref, s32[1,32]{1,0:T(1,128)} %get-tuple-element.46.ids_hbm, s32[1,64]{1,0:T(1,128)} %bitcast.5, bf16[8,8,256]{2,1,0:T(8,128)(2,1)} %get-tuple-element.48.up_hbm, bf16[8,8,256]{2,1,0:T(8,128)(2,1)S(1)} %get-tuple-element.49.far_ref), custom_call_target="tpu_custom_call" | custom-call | tf_op jit(solution)/shard_map/cond/branch_0_fun/pallas_call | solution.py:283
  8.1 7.7 %all-to-all-start.1 = ((bf16[8,4,4096]{2,1,0:T(4,128)(2,1)}), bf16[8,4,4096]{2,1,0:T(4,128)(2,1)S(1)}, u32[]{:S(2)}, u32[]{:S(2)}) async-start(bf16[8,4,4096]{2,1,0:T(4,128)(2,1)} %branch_0_fun.4), calls=%async_computation.1 | async-start | bytes 524288 | tf_op jit(solution)/shard_map/cond/branch_0_fun/all_to_all | solution.py:259
  15.8 3.0 %branch_0_fun.3 = (f32[64,128]{1,0:T(8,128)S(1)}, f32[64,128]{1,0:T(8,128)S(1)}) custom-call(s32[4]{0:T(128)} %get-tuple-element.82.lengths_ref, bf16[4,1024]{1,0:T(4,128)(2,1)} %get-tuple-element.41.query_hbm, bf16[4,1024]{1,0:T(4,128)(2,1)S(1)} %get-tuple-element.42.far_query_ref, bf16[4,512,256]{2,1,0:T(8,128)(2,1)} %get-tuple-element.83.cache_hbm), custom_call_target="tpu_custom_call" | custom-call | tf_op jit(solution)/shard_map/cond/branch_0_fun/pallas_call | solution.py:299
  18.8 2.0 %all-to-all-done.1.got_ref = bf16[8,4,4096]{2,1,0:T(4,128)(2,1)S(1)} async-done(((bf16[8,4,4096]{2,1,0:T(4,128)(2,1)}), bf16[8,4,4096]{2,1,0:T(4,128)(2,1)S(1)}, u32[]{:S(2)}, u32[]{:S(2)}) %all-to-all-start.1) | async-done | bytes 262176 | tf_op jit(solution)/shard_map/cond/branch_0_fun/all_to_all | solution.py:259
  20.8 0.0 collective-permute-done
  20.8 0.0 copy-done.1
  20.8 0.0 copy-start
  20.8 0.0 copy-start.2
  20.8 0.9 %collective-permute-start.3 = (f32[192,128]{1,0:T(8,128)S(1)}, f32[192,128]{1,0:T(8,128)S(1)}, u32[]{:S(2)}, u32[]{:S(2)}) collective-permute-start(f32[192,128]{1,0:T(8,128)S(1)} %get-tuple-element.91.mine_ref), channel_id=1, source_target_pairs={{0,1},{1,0},{2,3},{3,2},{4,5},{5,4},{6,7},{7,6},{8,9},{9,8},{10,11... | collective-permute-start | bytes 294920 | tf_op jit(solution)/shard_map/ppermute | solution.py:367
  21.7 0.9 %collective-permute-done.3.other_ref = f32[192,128]{1,0:T(8,128)S(1)} collective-permute-done((f32[192,128]{1,0:T(8,128)S(1)}, f32[192,128]{1,0:T(8,128)S(1)}, u32[]{:S(2)}, u32[]{:S(2)}) %collective-permute-start.3) | collective-permute-done | bytes 98336 | tf_op jit(solution)/shard_map/ppermute | solution.py:367
  22.7 0.0 copy-done
  22.7 0.0 copy-done.2
  22.7 1.0 %shard_map.108 = (bf16[4,256]{1,0:T(4,128)(2,1)}, bf16[4,1024]{1,0:T(4,128)(2,1)}) custom-call(f32[192,128]{1,0:T(8,128)S(1)} %get-tuple-element.91.mine_ref, f32[192,128]{1,0:T(8,128)S(1)} %collective-permute-done.3.other_ref, f32[64,128]{1,0:T(8,128)S(1)} %get-tuple-element.78.stats_ref, bf16[4,256]{1,0:T(4,128)(2,1)S(1)} %copy-done, ...), custom_call_target="tpu_custom_call" | custom-call | tf_op jit(solution)/shard_map/pallas_call | solution.py:368
  (3 shorter events, 0.0 us)
Async XLA Ops:
  0.6 20.2 %copy-start.1 = (bf16[2048,512]{1,0:T(8,128)(2,1)S(1)}, bf16[2048,512]{1,0:T(8,128)(2,1)}, u32[]{:S(2)}) copy-start(bf16[2048,512]{1,0:T(8,128)(2,1)} %param.22) | copy-start | bytes 6291460
  0.7 20.0 %collective-permute-start = (bf16[2048,512]{1,0:T(8,128)(2,1)}, bf16[2048,512]{1,0:T(8,128)(2,1)}, u32[]{:S(2)}, u32[]{:S(2)}) collective-permute-start(bf16[2048,512]{1,0:T(8,128)(2,1)} %param.22), channel_id=1, source_target_pairs={{0,1},{1,0},{2,3},{3,2},{4,5},{5,4},{6,7},{7,6},{8,9},{9,8},{10,11... | collective-permute-start | bytes 6291464 | tf_op jit(solution)/shard_map/ppermute | solution.py:278
  2.2 3.9 %collective-permute-start.1 = (bf16[8,8,256]{2,1,0:T(8,128)(2,1)}, bf16[8,8,256]{2,1,0:T(8,128)(2,1)S(1)}, u32[]{:S(2)}, u32[]{:S(2)}) collective-permute-start(bf16[8,8,256]{2,1,0:T(8,128)(2,1)} %param.23), channel_id=1, source_target_pairs={{0,1},{1,0},{2,3},{3,2},{4,5},{5,4},{6,7},{7,6},{8,9},{9,8},{10,11... | collective-permute-start | bytes 98312 | tf_op jit(solution)/shard_map/ppermute | solution.py:276
  2.3 3.8 %collective-permute-start.2 = (bf16[4,1024]{1,0:T(4,128)(2,1)}, bf16[4,1024]{1,0:T(4,128)(2,1)S(1)}, u32[]{:S(2)}, u32[]{:S(2)}) collective-permute-start(bf16[4,1024]{1,0:T(4,128)(2,1)} %query_ref.1), channel_id=1, source_target_pairs={{0,1},{1,0},{2,3},{3,2},{4,5},{5,4},{6,7},{7,6},{8,9},{9,8},{10,11... | collective-permute-start | bytes 24584 | tf_op jit(solution)/shard_map/ppermute | solution.py:277
  8.1 12.6 %all-to-all-start.1 = ((bf16[8,4,4096]{2,1,0:T(4,128)(2,1)}), bf16[8,4,4096]{2,1,0:T(4,128)(2,1)S(1)}, u32[]{:S(2)}, u32[]{:S(2)}) async-start(bf16[8,4,4096]{2,1,0:T(4,128)(2,1)} %branch_0_fun.4), calls=%async_computation.1 | async-start | bytes 524288 | tf_op jit(solution)/shard_map/cond/branch_0_fun/all_to_all | solution.py:259
  20.8 1.9 %copy-start = (bf16[4,256]{1,0:T(4,128)(2,1)S(1)}, bf16[4,256]{1,0:T(4,128)(2,1)}, u32[]{:S(2)}) copy-start(bf16[4,256]{1,0:T(4,128)(2,1)} %base_ref.1) | copy-start | bytes 6148
  20.8 1.9 %copy-start.2 = (bf16[4,1024]{1,0:T(4,128)(2,1)S(1)}, bf16[4,1024]{1,0:T(4,128)(2,1)}, u32[]{:S(2)}) copy-start(bf16[4,1024]{1,0:T(4,128)(2,1)} %query_ref.1) | copy-start | bytes 24580
  20.8 1.8 %collective-permute-start.3 = (f32[192,128]{1,0:T(8,128)S(1)}, f32[192,128]{1,0:T(8,128)S(1)}, u32[]{:S(2)}, u32[]{:S(2)}) collective-permute-start(f32[192,128]{1,0:T(8,128)S(1)} %get-tuple-element.91.mine_ref), channel_id=1, source_target_pairs={{0,1},{1,0},{2,3},{3,2},{4,5},{5,4},{6,7},{7,6},{8,9},{9,8},{10,11... | collective-permute-start | bytes 294920 | tf_op jit(solution)/shard_map/ppermute | solution.py:367

commit v5 on v4

--- a/solution.py
+++ b/solution.py
@@ -77,7 +77,7 @@
 
 
 def attend_kernel(
-    lengths_ref, query_hbm, far_query_ref, cache_hbm, mine_ref, far_ref,
+    lengths_ref, query_hbm, far_query_ref, cache_hbm, q_out_ref, mine_ref, far_ref, level_ref,
     query_ref, cache_ref, q_ref, sems
 ):
     pairs = ((query_hbm, query_ref), (cache_hbm, cache_ref))
@@ -96,8 +96,9 @@
                 :, h * HD : (h + 1) * HD
             ]
     for b in range(count):
+        queries = q_ref[b * 2 * heads : (b + 1) * 2 * heads, :]
         scores = lax.dot_general(
-            q_ref[b * 2 * heads : (b + 1) * 2 * heads, :].astype(BF16),
+            queries.astype(BF16),
             cache_ref[b, :, :HD],
             (((1,), (1,)), ((), ())),
             preferred_element_type=F32,
@@ -108,22 +109,44 @@
         weights = jnp.exp(scores - top)
         total = jnp.sum(weights, axis=1, keepdims=True)
         acc = jnp.dot(weights.astype(BF16), cache_ref[b, :, HD:], preferred_element_type=F32)
-        both = jnp.where(iota(acc.shape, 1) < HD // 2, top, total)
-        at = b * heads
-        for half, ref in enumerate((mine_ref, far_ref)):
-            part = slice(half * heads, (half + 1) * heads)
-            ref[at : at + heads, :] = acc[part]
-            ref[(count + b) * heads : (count + b + 1) * heads, :] = both[part]
-
-
-def gather_kernel(got_ref, stats_ref, out_ref):
+        mean = acc / total
+        level = jnp.broadcast_to(top + jnp.log(total), mean.shape)
+        part = slice(b * heads, (b + 1) * heads)
+        q_out_ref[part, :] = queries[:heads]
+        mine_ref[part, :] = mean[:heads]
+        far_ref[part, :] = mean[heads:]
+        after = slice((count + b) * heads, (count + b + 1) * heads)
+        mine_ref[after, :] = level[:heads]
+        far_ref[after, :] = queries[heads:]
+        level_ref[part, :] = level[heads:]
+
+
+def thirds(values):
+    lane = iota(values.shape, 1)
+    high = values.astype(BF16).astype(F32)
+    rest = values - high
+    middle = rest.astype(BF16).astype(F32)
+    low = rest - middle
+    return jnp.where(lane < 32, high, jnp.where(lane < 64, middle, low)).astype(BF16)
+
+
+def whole(values):
+    values = values.astype(F32)
+    return values[:, 0:1] + values[:, 32:33] + values[:, 64:65]
+
+
+def gather_kernel(got_ref, stats_ref, level_ref, out_ref, wide_ref):
     total = got_ref[0].astype(F32)
     for p in range(1, got_ref.shape[0]):
         total = total + got_ref[p].astype(F32)
     count, span = total.shape
+    rows = level_ref.shape[0]
+    tall = span // HD * count
     for j in range(span // HD):
-        out_ref[j * count : (j + 1) * count, :] = total[:, j * HD : (j + 1) * HD]
-    out_ref[span // HD * count :, :] = stats_ref[...]
+        wide_ref[j * count : (j + 1) * count, :] = total[:, j * HD : (j + 1) * HD]
+    out_ref[:tall, :] = wide_ref[...].astype(BF16)
+    out_ref[tall : tall + 2 * rows, :] = stats_ref[...].astype(BF16)
+    out_ref[tall + 2 * rows :, :] = thirds(level_ref[...])
 
 
 def spare_kernel(*refs):
@@ -183,51 +206,47 @@
     for p in range(1, got_ref.shape[0]):
         total = total + got_ref[p].astype(F32)
     total = total + pltpu.roll(total, 128 - 2 * ranks, 1)
-    out_ref[: total.shape[0], :] = total.astype(BF16).astype(F32)
+    out_ref[:16, :] = jnp.concatenate([total] * (16 // total.shape[0]), axis=0).astype(BF16)
 
 
 def merge_kernel(
-    ranks, mine_ref, other_ref, stats_ref, base_ref, query_ref,
-    kv_ref, out_ref, q_ref, wide_ref
+    ranks, mine_ref, other_ref, q_ref, stats_ref, base_ref, kv_ref, out_ref, wide_ref
 ):
     count, width = base_ref.shape
-    heads = query_ref.shape[1] // HD
+    rows = q_ref.shape[0]
+    heads = rows // count
     halves = width // HD
-    scale = HD ** (-0.5)
-    lower = lax.axis_index("tp") == 0
     tile = halves * count
     span = 2 * ranks * tile
-    query = query_ref[...].astype(F32)
-    for h in range(heads):
-        q_ref[pl.ds(h, count, stride=heads), :] = query[:, h * HD : (h + 1) * HD]
-    low = jnp.where(lower, other_ref[:count, :], mine_ref[:count, :])
-    low = jnp.concatenate([low] * halves, axis=0)
+    lower = lax.axis_index("tp") == 0
     base = base_ref[...].astype(F32)
     fresh = jnp.concatenate([base[:, j * HD : (j + 1) * HD] for j in range(halves)], axis=0)
-    for r in range(2 * ranks):
-        part = slice(r * tile, (r + 1) * tile)
-        row = jnp.where(lower, mine_ref[part, :], other_ref[part, :])
-        fresh = fresh + low[:, r : r + 1] * row
+    low = jnp.where(lower, other_ref[:16, :], mine_ref[:16, :]).astype(F32)[:tile]
+    for r in range(0, 2 * ranks, 16 // tile):
+        part = slice(r * tile, r * tile + 16)
+        pair = jnp.where(lower, mine_ref[part, :], other_ref[part, :]).astype(F32)
+        for i in range(16 // tile):
+            fresh = fresh + low[:, r + i : r + i + 1] * pair[i * tile : (i + 1) * tile]
     fresh = fresh.astype(BF16).astype(F32)
     for j in range(halves):
         kv_ref[:, j * HD : (j + 1) * HD] = fresh[j * count : (j + 1) * count].astype(BF16)
-    for b in range(count):
-        part = slice(b * heads, (b + 1) * heads)
-        far = slice(span + b * heads, span + (b + 1) * heads)
-        key = fresh[b : b + 1]
-        value = fresh[count + b : count + b + 1]
-        own = jnp.sum(q_ref[part, :] * key, axis=1, keepdims=True) * scale
-        acc = jnp.where(lower, stats_ref[part, :], other_ref[far, :])
-        part = slice((count + b) * heads, (count + b + 1) * heads)
-        far = slice(span + (count + b) * heads, span + (count + b + 1) * heads)
-        both = jnp.where(lower, stats_ref[part, :], other_ref[far, :])
-        top = both[:, :1]
-        high = jnp.maximum(top, own)
-        keep = jnp.exp(top - high)
-        weight = jnp.exp(own - high)
-        norm = 1.0 / (both[:, HD - 1 :] * keep + weight)
-        part = slice(b * heads, (b + 1) * heads)
-        wide_ref[part, :] = acc * (keep * norm) + (weight * norm) * value
+    far = other_ref[span:, :].astype(F32)
+    mean = jnp.where(lower, stats_ref[:rows, :], far[:rows])
+    query = jnp.where(lower, q_ref[...], far[rows : 2 * rows])
+    level = jnp.where(lower, stats_ref[rows:, :1], whole(far[2 * rows :]))
+    spread = [
+        jnp.concatenate(
+            [
+                jnp.broadcast_to(fresh[j * count + b : j * count + b + 1], (heads, HD))
+                for b in range(count)
+            ],
+            axis=0,
+        )
+        for j in range(halves)
+    ]
+    own = jnp.sum(query * spread[0], axis=1, keepdims=True) * HD ** (-0.5)
+    share = 1.0 / (1.0 + jnp.exp(level - own))
+    wide_ref[...] = mean + share * (spread[1] - mean)
     for h in range(heads):
         out_ref[:, h * HD : (h + 1) * HD] = wide_ref[pl.ds(h, count, stride=heads), :].astype(BF16)
 
@@ -249,7 +268,8 @@
     core = lax.axis_index("tp").astype(jnp.int32)
     swap = [(0, 1), (1, 0)]
     stats_shape = jax.ShapeDtypeStruct((2 * per_dev * heads, HD), F32)
-    trade_shape = jax.ShapeDtypeStruct((span // HD * per_dev + 2 * per_dev * heads, HD), F32)
+    heads_shape = jax.ShapeDtypeStruct((per_dev * heads, HD), F32)
+    trade_shape = jax.ShapeDtypeStruct((span // HD * per_dev + 3 * per_dev * heads, HD), BF16)
     blocks_shape = jax.ShapeDtypeStruct((parts, per_dev, block), BF16)
 
     def pin(x):
@@ -296,11 +316,11 @@
             compiler_params=PARAMS,
         )(base, pin(ids), pin(home), pin(up), far_up)
         got = exchange(packed)
-        mine, far = pl.pallas_call(
+        near_q, mine, far, level = pl.pallas_call(
             attend_kernel,
-            out_shape=(stats_shape, stats_shape),
+            out_shape=(heads_shape, stats_shape, stats_shape, heads_shape),
             in_specs=[SMEM, HBM, VMEM, HBM],
-            out_specs=(VMEM, VMEM),
+            out_specs=(VMEM,) * 4,
             scratch_shapes=[
                 pltpu.VMEM(query.shape, BF16),
                 pltpu.VMEM(cache.shape, BF16),
@@ -312,22 +332,23 @@
         trade = pl.pallas_call(
             gather_kernel,
             out_shape=trade_shape,
-            in_specs=[VMEM, VMEM],
+            in_specs=[VMEM] * 3,
             out_specs=VMEM,
-            compiler_params=PARAMS,
-        )(got, far)
-        return mine, trade
+            scratch_shapes=[pltpu.VMEM((span // HD * per_dev, HD), F32)],
+            compiler_params=PARAMS,
+        )(got, far, level)
+        return near_q, mine, trade
 
     def upper(far_up, far_query, lengths, ids, query, cache, home, up, base):
         return pl.pallas_call(
             spare_kernel,
-            out_shape=(stats_shape, trade_shape),
+            out_shape=(heads_shape, stats_shape, trade_shape),
             in_specs=[],
-            out_specs=(VMEM, VMEM),
+            out_specs=(VMEM,) * 3,
             compiler_params=PARAMS,
         )()
 
-    stats, trade = lax.cond(
+    near_q, stats, trade = lax.cond(
         core == 1, upper, lower,
         far_up, far_query, lengths, ids, query, cache,
         home_slot.reshape(1, ADAPTERS), adapter_up, base,
@@ -373,12 +394,9 @@
         ),
         in_specs=[VMEM] * 5,
         out_specs=(VMEM, VMEM),
-        scratch_shapes=[
-            pltpu.VMEM((per_dev * heads, HD), F32),
-            pltpu.VMEM((per_dev * heads, HD), F32),
-        ],
+        scratch_shapes=[pltpu.VMEM((per_dev * heads, HD), F32)],
         compiler_params=PARAMS,
-    )(mine, other, stats, kv_base, query)
+    )(mine, other, near_q, stats, kv_base)
     return (new_kv, attended)
 
 

time: 24 us -> 23.8 us (level)
  no operation moved by 1% of the time
where the time goes in v5:
time: 23.8 us; the launch traced here: 23.5 us
  starting transfers between devices  10.5 us (44%)
  waiting for transfers between devices  6.27 us (26%)
  Pallas kernels  5.95 us (25%)
  between operations  0.69 us (3%)
    all_to_all x1, starting transfers between devices, exchange(): lax.all_to_all(x, 'req', split_axis=0, concat_axis=0, tiled=True, axis_in...  7.68 us
    ppermute x1, waiting for transfers between devices, shards(): far_query = lax.ppermute(near_query, 'tp', swap)  3.42 us
    pallas_call x1, Pallas kernels, lower(): pl.pallas_call(attend_kernel, out_shape=(heads_shape, stats_shape, stats_...  3 us
    all_to_all x1, waiting for transfers between devices, exchange(): lax.all_to_all(x, 'req', split_axis=0, concat_axis=0, tiled=True, axis_in...  1.96 us
    pallas_call x1, Pallas kernels, lower(): pl.pallas_call(functools.partial(pack_kernel, order), out_shape=jax.Shape...  1.92 us
    ppermute x1, starting transfers between devices, shards(): far_down = lax.ppermute(near_down, 'tp', swap)  1.48 us
    ppermute x1, waiting for transfers between devices, shards(): other = lax.ppermute(mine, 'tp', swap)  0.89 us
    pallas_call x1, Pallas kernels, shards(): pl.pallas_call(functools.partial(merge_kernel, ranks), out_shape=(jax.Sha...  0.89 us
  transfers between devices with their start and end apart: 5, of which 3 were waited for; matrix products, arithmetic and copies ran while one was open for 0% of the time, Pallas kernels for 21%

profile of v5, /device:TPU:0, one launch (start us, length us, event | category | flops | bytes accessed | tf_op | source)
XLA Modules:
  0.0 23.5 jit_solution(2533609096593029044)
XLA Ops:
  0.6 0.0 copy-start.1
  0.6 0.1 shard_map.107
  0.7 1.5 %collective-permute-start = (bf16[2048,512]{1,0:T(8,128)(2,1)}, bf16[2048,512]{1,0:T(8,128)(2,1)}, u32[]{:S(2)}, u32[]{:S(2)}) collective-permute-start(bf16[2048,512]{1,0:T(8,128)(2,1)} %param.22), channel_id=1, source_target_pairs={{0,1},{1,0},{2,3},{3,2},{4,5},{5,4},{6,7},{7,6},{8,9},{9,8},{10,11... | collective-permute-start | bytes 6291464 | tf_op jit(solution)/shard_map/ppermute | solution.py:298
  2.2 0.1 collective-permute-start.1
  2.3 0.4 %collective-permute-start.2 = (bf16[4,1024]{1,0:T(4,128)(2,1)}, bf16[4,1024]{1,0:T(4,128)(2,1)S(1)}, u32[]{:S(2)}, u32[]{:S(2)}) collective-permute-start(bf16[4,1024]{1,0:T(4,128)(2,1)} %param.19), channel_id=1, source_target_pairs={{0,1},{1,0},{2,3},{3,2},{4,5},{5,4},{6,7},{7,6},{8,9},{9,8},{10,11... | collective-permute-start | bytes 24584 | tf_op jit(solution)/shard_map/ppermute | solution.py:297
  2.7 3.4 %collective-permute-done.2 = bf16[4,1024]{1,0:T(4,128)(2,1)S(1)} collective-permute-done((bf16[4,1024]{1,0:T(4,128)(2,1)}, bf16[4,1024]{1,0:T(4,128)(2,1)S(1)}, u32[]{:S(2)}, u32[]{:S(2)}) %collective-permute-start.2) | collective-permute-done | bytes 8224 | tf_op jit(solution)/shard_map/ppermute | solution.py:297
  6.1 0.0 collective-permute-done.1
  6.2 14.6 %conditional.4 = ((f32[32,128]{1,0:T(8,128)S(1)}, f32[64,128]{1,0:T(8,128)S(1)}, bf16[224,128]{1,0:T(8,128)(2,1)S(1)})) conditional(s32[]{:T(128)} %convert_element_type.2, (s32[4]{0:T(128)}, bf16[4,1024]{1,0:T(4,128)(2,1)}, bf16[4,1024]{1,0:T(4,128)(2,1)S(1)}, bf16[4,512,256]{2,1,0:T(8,128)(2,1)}, s32[]{:T(128)}, /*index=5*/s32[64]{0:T(128)}, ...), branch_computations={%region_2.0_spmd, %region_3.0_spmd} | conditional | flops 1 | bytes 786508 | solution.py:351
  6.2 1.9 %branch_0_fun.4 = bf16[8,4,4096]{2,1,0:T(4,128)(2,1)} custom-call(s32[1]{0:T(128)} %bitcast.base_ref, s32[1,32]{1,0:T(1,128)} %get-tuple-element.47.ids_hbm, s32[1,64]{1,0:T(1,128)} %bitcast.5, bf16[8,8,256]{2,1,0:T(8,128)(2,1)} %get-tuple-element.49.up_hbm, bf16[8,8,256]{2,1,0:T(8,128)(2,1)S(1)} %get-tuple-element.50.far_ref), custom_call_target="tpu_custom_call" | custom-call | tf_op jit(solution)/shard_map/cond/branch_0_fun/pallas_call | solution.py:303
  8.1 7.7 %all-to-all-start.1 = ((bf16[8,4,4096]{2,1,0:T(4,128)(2,1)}), bf16[8,4,4096]{2,1,0:T(4,128)(2,1)S(1)}, u32[]{:S(2)}, u32[]{:S(2)}) async-start(bf16[8,4,4096]{2,1,0:T(4,128)(2,1)} %branch_0_fun.4), calls=%async_computation.1 | async-start | bytes 524288 | tf_op jit(solution)/shard_map/cond/branch_0_fun/all_to_all | solution.py:279
  15.8 3.0 %branch_0_fun.3 = (f32[32,128]{1,0:T(8,128)S(1)}, f32[64,128]{1,0:T(8,128)S(1)}, f32[64,128]{1,0:T(8,128)S(1)}, f32[32,128]{1,0:T(8,128)S(1)}) custom-call(s32[4]{0:T(128)} %get-tuple-element.86.lengths_ref, bf16[4,1024]{1,0:T(4,128)(2,1)} %get-tuple-element.41.query_hbm, bf16[4,1024]{1,0:T(4,128)(2,1)S(1)} %get-tuple-element.42.far_query_ref, ...), custom_call_target="tpu_custom_call" | custom-call | tf_op jit(solution)/shard_map/cond/branch_0_fun/pallas_call | solution.py:319
  18.8 2.0 %all-to-all-done.1.got_ref = bf16[8,4,4096]{2,1,0:T(4,128)(2,1)S(1)} async-done(((bf16[8,4,4096]{2,1,0:T(4,128)(2,1)}), bf16[8,4,4096]{2,1,0:T(4,128)(2,1)S(1)}, u32[]{:S(2)}, u32[]{:S(2)}) %all-to-all-start.1) | async-done | bytes 262176 | tf_op jit(solution)/shard_map/cond/branch_0_fun/all_to_all | solution.py:279
  20.8 0.0 collective-permute-done
  20.8 0.0 copy-done.1
  20.8 0.0 copy-start
  20.8 0.9 %collective-permute-start.3 = (bf16[224,128]{1,0:T(8,128)(2,1)S(1)}, bf16[224,128]{1,0:T(8,128)(2,1)S(1)}, u32[]{:S(2)}, u32[]{:S(2)}) collective-permute-start(bf16[224,128]{1,0:T(8,128)(2,1)S(1)} %get-tuple-element.97.mine_ref), channel_id=1, source_target_pairs={{0,1},{1,0},{2,3},{3,2},{4,5},{5,4},{6,7},{7,6},{8,9},{9,8},{10,11... | collective-permute-start | bytes 172040 | tf_op jit(solution)/shard_map/ppermute | solution.py:388
  21.7 0.9 %collective-permute-done.3.other_ref = bf16[224,128]{1,0:T(8,128)(2,1)S(1)} collective-permute-done((bf16[224,128]{1,0:T(8,128)(2,1)S(1)}, bf16[224,128]{1,0:T(8,128)(2,1)S(1)}, u32[]{:S(2)}, u32[]{:S(2)}) %collective-permute-start.3) | collective-permute-done | bytes 57376 | tf_op jit(solution)/shard_map/ppermute | solution.py:388
  22.6 0.0 copy-done
  22.6 0.9 %shard_map.108 = (bf16[4,256]{1,0:T(4,128)(2,1)}, bf16[4,1024]{1,0:T(4,128)(2,1)}) custom-call(bf16[224,128]{1,0:T(8,128)(2,1)S(1)} %get-tuple-element.97.mine_ref, bf16[224,128]{1,0:T(8,128)(2,1)S(1)} %collective-permute-done.3.other_ref, f32[32,128]{1,0:T(8,128)S(1)} %get-tuple-element.81.q_ref, f32[64,128]{1,0:T(8,128)S(1)} %get-tuple-element.82.stats_ref, ...), custom_call_target="tpu_custom_call" | custom-call | tf_op jit(solution)/shard_map/pallas_call | solution.py:389
  (3 shorter events, 0.1 us)
Async XLA Ops:
  0.6 20.2 %copy-start.1 = (bf16[2048,512]{1,0:T(8,128)(2,1)S(1)}, bf16[2048,512]{1,0:T(8,128)(2,1)}, u32[]{:S(2)}) copy-start(bf16[2048,512]{1,0:T(8,128)(2,1)} %param.22) | copy-start | bytes 6291460
  0.7 20.0 %collective-permute-start = (bf16[2048,512]{1,0:T(8,128)(2,1)}, bf16[2048,512]{1,0:T(8,128)(2,1)}, u32[]{:S(2)}, u32[]{:S(2)}) collective-permute-start(bf16[2048,512]{1,0:T(8,128)(2,1)} %param.22), channel_id=1, source_target_pairs={{0,1},{1,0},{2,3},{3,2},{4,5},{5,4},{6,7},{7,6},{8,9},{9,8},{10,11... | collective-permute-start | bytes 6291464 | tf_op jit(solution)/shard_map/ppermute | solution.py:298
  2.2 3.9 %collective-permute-start.1 = (bf16[8,8,256]{2,1,0:T(8,128)(2,1)}, bf16[8,8,256]{2,1,0:T(8,128)(2,1)S(1)}, u32[]{:S(2)}, u32[]{:S(2)}) collective-permute-start(bf16[8,8,256]{2,1,0:T(8,128)(2,1)} %param.23), channel_id=1, source_target_pairs={{0,1},{1,0},{2,3},{3,2},{4,5},{5,4},{6,7},{7,6},{8,9},{9,8},{10,11... | collective-permute-start | bytes 98312 | tf_op jit(solution)/shard_map/ppermute | solution.py:296
  2.3 3.8 %collective-permute-start.2 = (bf16[4,1024]{1,0:T(4,128)(2,1)}, bf16[4,1024]{1,0:T(4,128)(2,1)S(1)}, u32[]{:S(2)}, u32[]{:S(2)}) collective-permute-start(bf16[4,1024]{1,0:T(4,128)(2,1)} %param.19), channel_id=1, source_target_pairs={{0,1},{1,0},{2,3},{3,2},{4,5},{5,4},{6,7},{7,6},{8,9},{9,8},{10,11... | collective-permute-start | bytes 24584 | tf_op jit(solution)/shard_map/ppermute | solution.py:297
  8.1 12.6 %all-to-all-start.1 = ((bf16[8,4,4096]{2,1,0:T(4,128)(2,1)}), bf16[8,4,4096]{2,1,0:T(4,128)(2,1)S(1)}, u32[]{:S(2)}, u32[]{:S(2)}) async-start(bf16[8,4,4096]{2,1,0:T(4,128)(2,1)} %branch_0_fun.4), calls=%async_computation.1 | async-start | bytes 524288 | tf_op jit(solution)/shard_map/cond/branch_0_fun/all_to_all | solution.py:279
  20.8 1.8 %copy-start = (bf16[4,256]{1,0:T(4,128)(2,1)S(1)}, bf16[4,256]{1,0:T(4,128)(2,1)}, u32[]{:S(2)}) copy-start(bf16[4,256]{1,0:T(4,128)(2,1)} %base_ref.1) | copy-start | bytes 6148
  20.8 1.8 %collective-permute-start.3 = (bf16[224,128]{1,0:T(8,128)(2,1)S(1)}, bf16[224,128]{1,0:T(8,128)(2,1)S(1)}, u32[]{:S(2)}, u32[]{:S(2)}) collective-permute-start(bf16[224,128]{1,0:T(8,128)(2,1)S(1)} %get-tuple-element.97.mine_ref), channel_id=1, source_target_pairs={{0,1},{1,0},{2,3},{3,2},{4,5},{5,4},{6,7},{7,6},{8,9},{9,8},{10,11... | collective-permute-start | bytes 172040 | tf_op jit(solution)/shard_map/ppermute | solution.py:388

commit v6 on v0

v6 whole, which is shorter than its diff:
```python
import functools

import jax
import jax.numpy as jnp
from jax import lax
from jax.experimental import pallas as pl
from jax.experimental.pallas import tpu as pltpu
from jax.sharding import PartitionSpec as P

HD = 128
ADAPTERS = 64
F32 = jnp.float32
BF16 = jnp.bfloat16
VMEM = pl.BlockSpec(memory_space=pltpu.VMEM)
SMEM = pl.BlockSpec(memory_space=pltpu.SMEM)
HBM = pl.BlockSpec(memory_space=pltpu.HBM)
PARAMS = pltpu.CompilerParams(vmem_limit_bytes=8 * 1024 * 1024)


def iota(shape, dim):
    return lax.broadcasted_iota(jnp.int32, shape, dim)


def one_hot_ids(ids):
    shape = (ADAPTERS, ids.shape[1])
    return (iota(shape, 0) == jnp.broadcast_to(ids, shape)).astype(BF16)


def across(a, b):
    return lax.dot_general(a, b, (((0,), (0,)), ((), ())), preferred_element_type=F32)


def start_kernel(
    hidden_ref, ids_hbm, home_hbm, up_hbm, out_ref, ids_ref, home_ref, up_ref, sems
):
    parts, _, block = hidden_ref.shape
    center = (parts // 2 + 1) % parts

    @pl.when(lax.axis_index("tp") == 1)
    def _():
        copies = [
            pltpu.make_async_copy(
                hidden_ref.at[pl.ds(center, parts - center)],
                out_ref.at[pl.ds(0, parts - center), :, pl.ds(0, block)],
                sems.at[0],
            ),
            pltpu.make_async_copy(
                hidden_ref.at[pl.ds(0, center)],
                out_ref.at[pl.ds(parts - center, center), :, pl.ds(0, block)],
                sems.at[1],
            ),
            pltpu.make_async_copy(ids_hbm, ids_ref, sems.at[2]),
            pltpu.make_async_copy(home_hbm, home_ref, sems.at[3]),
            pltpu.make_async_copy(up_hbm, up_ref, sems.at[4]),
        ]
        for copy in copies:
            copy.start()
        for copy in copies:
            copy.wait()


def needed_rows(ids, home, up_ref, flat_ref, wide_ref):
    slots, ranks, width = up_ref.shape
    depth = flat_ref.shape[0]
    if depth > slots:
        flat_ref[...] = jnp.zeros_like(flat_ref)
    wide_ref[...] = up_ref[...].astype(F32)
    for r in range(ranks):
        flat_ref[:slots, r * width : (r + 1) * width] = wide_ref[:, r, :]
    shape = (depth, ADAPTERS)
    base = lax.axis_index("req").astype(jnp.int32) * slots
    here = jnp.broadcast_to(home, shape) - base == iota(shape, 0)
    held = here & (iota(shape, 0) < slots)
    match = jnp.dot(held.astype(BF16), one_hot_ids(ids), preferred_element_type=F32)
    return across(match.astype(BF16), flat_ref[...].astype(BF16)).astype(BF16)


def pack_kernel(
    order, blocks_ref, ids_hbm, home_hbm, up_hbm, cache_hbm, down_hbm, out_ref,
    ids_ref, home_ref, up_ref, flat_ref, wide_ref, sems
):
    count = out_ref.shape[1]
    span = flat_ref.shape[1]
    lower = lax.axis_index("tp") == 0

    @pl.when(lower)
    def _():
        pairs = ((ids_hbm, ids_ref), (home_hbm, home_ref), (up_hbm, up_ref))
        copies = [pltpu.make_async_copy(a, b, sems.at[i]) for i, (a, b) in enumerate(pairs)]
        for copy in copies:
            copy.start()
        for copy in copies:
            copy.wait()
        rows = needed_rows(ids_ref[...], home_ref[...], up_ref, flat_ref, wide_ref)
        for p, q in enumerate(order):
            out_ref[p, :, :span] = rows[q * count : (q + 1) * count]

    @pl.when(jnp.logical_not(lower))
    def _():
        out_ref[...] = blocks_ref[...]


def low_kernel(
    order, ids_ref, home_ref, up_ref, got_ref, down_ref, far_ref, out_ref, flat_ref, wide_ref
):
    parts, per_dev, _ = out_ref.shape
    block, columns = down_ref.shape
    ranks = columns // ADAPTERS
    span = flat_ref.shape[1]

    @pl.when(lax.axis_index("tp") == 1)
    def _():
        pieces = [got_ref[p].astype(F32)[:, :block] for p in range(parts)]
        blocks = jnp.concatenate(pieces, axis=0).astype(BF16)
        names = across(one_hot_ids(ids_ref[...]), iota((ADAPTERS, 128), 0).astype(BF16))
        names = names.astype(jnp.int32)
        shift = order[0] * per_dev
        if shift:
            names = jnp.concatenate([names[shift:], names[:shift]], axis=0)
        lane = iota(names.shape, 1)
        spot = names + lane % 2 * ADAPTERS
        rank = lane % (2 * ranks)
        low = jnp.zeros(names.shape, F32)
        for half, ref in enumerate((far_ref, down_ref)):
            values = jnp.dot(blocks, ref[...], preferred_element_type=F32)
            for j in range(columns // 128):
                got = jnp.take_along_axis(values[:, j * 128 : (j + 1) * 128], spot, axis=1)
                low = jnp.where(rank // 2 == j + half * ranks // 2, got, low)
        high = low.astype(BF16).astype(F32)
        low = jnp.where(lane < 2 * ranks, high, low - high).astype(BF16)
        rows = needed_rows(ids_ref[...], home_ref[...], up_ref, flat_ref, wide_ref)
        for p, q in enumerate(order):
            out_ref[p, :, :span] = rows[q * per_dev : (q + 1) * per_dev]
            out_ref[p, :, span:] = low[p * per_dev : (p + 1) * per_dev]


def fold_kernel(ranks, span, got_ref, out_ref, wide_ref):
    total = got_ref[0].astype(F32)
    for p in range(1, got_ref.shape[0]):
        total = total + got_ref[p].astype(F32)
    count = total.shape[0]
    tall = span // HD * count
    for j in range(span // HD):
        wide_ref[j * count : (j + 1) * count, :] = total[:, j * HD : (j + 1) * HD]
    out_ref[:tall, :] = wide_ref[...].astype(BF16)
    if total.shape[1] == span + 128:
        low = total[:, span:]
        low = low + pltpu.roll(low, 128 - 2 * ranks, 1)
        out_ref[tall:, :] = jnp.concatenate([low] * (16 // count), axis=0).astype(BF16)


def attend_kernel(lengths_ref, query_ref, cache_ref, q_ref, stats_ref):
    count = cache_ref.shape[0]
    heads = query_ref.shape[1] // HD
    scale = HD ** (-0.5)
    query = query_ref[...].astype(F32)
    lengths = lengths_ref[...]
    for h in range(heads):
        q_ref[pl.ds(h, count, stride=heads), :] = query[:, h * HD : (h + 1) * HD]
    for b in range(count):
        part = slice(b * heads, (b + 1) * heads)
        scores = lax.dot_general(
            q_ref[part, :].astype(BF16),
            cache_ref[b, :, :HD],
            (((1,), (1,)), ((), ())),
            preferred_element_type=F32,
        )
        valid = iota(scores.shape, 1) < lengths[:, b : b + 1]
        scores = jnp.where(valid, scores * scale, -jnp.inf)
        top = jnp.max(scores, axis=1, keepdims=True)
        weights = jnp.exp(scores - top)
        total = jnp.sum(weights, axis=1, keepdims=True)
        acc = jnp.dot(weights.astype(BF16), cache_ref[b, :, HD:], preferred_element_type=F32)
        stats_ref[part, :] = acc / total
        after = slice((count + b) * heads, (count + b + 1) * heads)
        stats_ref[after, :] = jnp.broadcast_to(top + jnp.log(total), acc.shape)


def merge_kernel(
    ranks, mine_ref, other_ref, q_ref, stats_ref, base_ref, kv_ref, out_ref, wide_ref
):
    count, width = base_ref.shape
    rows = q_ref.shape[0]
    heads = rows // count
    halves = width // HD
    tile = halves * count
    span = ranks * tile
    lower = lax.axis_index("tp") == 0
    base = base_ref[...].astype(F32)
    fresh = jnp.concatenate([base[:, j * HD : (j + 1) * HD] for j in range(halves)], axis=0)
    low = jnp.where(lower, other_ref[span:, :], mine_ref[span:, :]).astype(F32)[:tile]
    for r in range(0, ranks, 16 // tile):
        part = slice(r * tile, r * tile + 16)
        mine = mine_ref[part, :]
        other = other_ref[part, :]
        for half, pair in ((0, jnp.where(lower, mine, other)), (1, jnp.where(lower, other, mine))):
            pair = pair.astype(F32)
            for i in range(16 // tile):
                at = half * ranks + r + i
                fresh = fresh + low[:, at : at + 1] * pair[i * tile : (i + 1) * tile]
    fresh = fresh.astype(BF16).astype(F32)
    for j in range(halves):
        kv_ref[:, j * HD : (j + 1) * HD] = fresh[j * count : (j + 1) * count].astype(BF16)
    mean = stats_ref[:rows, :]
    level = stats_ref[rows:, :1]
    spread = [
        jnp.concatenate(
            [
                jnp.broadcast_to(fresh[j * count + b : j * count + b + 1], (heads, HD))
                for b in range(count)
            ],
            axis=0,
        )
        for j in range(halves)
    ]
    own = jnp.sum(q_ref[...] * spread[0], axis=1, keepdims=True) * HD ** (-0.5)
    share = 1.0 / (1.0 + jnp.exp(level - own))
    wide_ref[...] = mean + share * (spread[1] - mean)
    for h in range(heads):
        out_ref[:, h * HD : (h + 1) * HD] = wide_ref[pl.ds(h, count, stride=heads), :].astype(BF16)


def shards(
    hidden, adapter_ids, home_slot, lengths, query, kv_base, cache, adapter_down, adapter_up
):
    per_dev = hidden.shape[0]
    slots, ranks, width = adapter_up.shape
    parts = lax.axis_size("req")
    everyone = per_dev * parts
    block = hidden.shape[1] // parts
    heads = query.shape[1] // HD
    span = ranks * width
    wide = max(block, span)
    center = (parts // 2 + 1) % parts
    order = [(center + p) % parts for p in range(parts)]
    depth = -(-slots // 8) * 8
    core = lax.axis_index("tp").astype(jnp.int32)
    swap = [(0, 1), (1, 0)]
    blocks_shape = jax.ShapeDtypeStruct((parts, per_dev, wide), BF16)
    tall = span // HD * per_dev
    trade_shape = jax.ShapeDtypeStruct((tall + 16, HD), BF16)

    def pin(x):
        return pltpu.with_memory_space_constraint(x, pltpu.HBM)

    def exchange(x):
        return lax.all_to_all(
            x, "req", split_axis=0, concat_axis=0, tiled=True, axis_index_groups=[order]
        )

    ids = adapter_ids.reshape(1, everyone)
    home = home_slot.reshape(1, ADAPTERS)
    like = lambda x: jax.ShapeDtypeStruct(x.shape, x.dtype)
    blocks, near_ids, near_home, near_up = pl.pallas_call(
        start_kernel,
        out_shape=(blocks_shape, like(ids), like(home), like(adapter_up)),
        in_specs=[HBM] * 4,
        out_specs=(VMEM,) * 4,
        scratch_shapes=[pltpu.SemaphoreType.DMA((5,))],
        compiler_params=PARAMS,
    )(
        pin(jnp.swapaxes(hidden.reshape(per_dev, parts, block), 0, 1)),
        pin(ids),
        pin(home),
        pin(adapter_up),
    )
    blocks, near_down, lower = lax.optimization_barrier((blocks, adapter_down, core == 0))
    far_down = lax.ppermute(near_down, "tp", swap)
    blocks = pl.pallas_call(
        functools.partial(pack_kernel, order),
        out_shape=blocks_shape,
        in_specs=[VMEM] + [HBM] * 5,
        out_specs=VMEM,
        scratch_shapes=[
            pltpu.VMEM(ids.shape, ids.dtype),
            pltpu.VMEM(home.shape, home.dtype),
            pltpu.VMEM(adapter_up.shape, BF16),
            pltpu.VMEM((depth, span), F32),
            pltpu.VMEM((slots, ranks, width), F32),
            pltpu.SemaphoreType.DMA((3,)),
        ],
        compiler_params=PARAMS,
    )(blocks, pin(ids), pin(home), pin(adapter_up), pin(cache), pin(near_down))
    got = exchange(blocks)
    packed = pl.pallas_call(
        functools.partial(low_kernel, order),
        out_shape=jax.ShapeDtypeStruct((parts, per_dev, span + 128), BF16),
        in_specs=[VMEM] * 6,
        out_specs=VMEM,
        scratch_shapes=[
            pltpu.VMEM((depth, span), F32),
            pltpu.VMEM((slots, ranks, width), F32),
        ],
        compiler_params=PARAMS,
    )(near_ids, near_home, near_up, got, near_down, far_down)

    packed, got, lower = lax.optimization_barrier((packed, got, lower))

    def fold(x):
        return pl.pallas_call(
            functools.partial(fold_kernel, ranks, span),
            out_shape=trade_shape,
            in_specs=[VMEM],
            out_specs=VMEM,
            scratch_shapes=[pltpu.VMEM((tall, HD), F32)],
            compiler_params=PARAMS,
        )(x)

    mine = lax.cond(
        lower,
        lambda packed, got: fold(got[:, :, :span]),
        lambda packed, got: fold(exchange(packed)),
        packed, got,
    )
    mine, lengths, query, cache = lax.optimization_barrier((mine, lengths, query, cache))
    other = lax.ppermute(mine, "tp", swap)
    q_rows, stats = pl.pallas_call(
        attend_kernel,
        out_shape=(
            jax.ShapeDtypeStruct((per_dev * heads, HD), F32),
            jax.ShapeDtypeStruct((2 * per_dev * heads, HD), F32),
        ),
        in_specs=[VMEM] * 3,
        out_specs=(VMEM, VMEM),
        cost_estimate=pl.CostEstimate(flops=0, transcendentals=0, bytes_accessed=1 << 22),
        compiler_params=PARAMS,
    )(lengths.reshape(1, per_dev), query, cache)
    new_kv, attended = pl.pallas_call(
        functools.partial(merge_kernel, ranks),
        out_shape=(
            jax.ShapeDtypeStruct(kv_base.shape, BF16),
            jax.ShapeDtypeStruct(query.shape, BF16),
        ),
        in_specs=[VMEM] * 5,
        out_specs=(VMEM, VMEM),
        scratch_shapes=[pltpu.VMEM((per_dev * heads, HD), F32)],
        compiler_params=PARAMS,
    )(mine, other, q_rows, stats, kv_base)
    return (new_kv, attended)


def solution(mesh):
    placed = (
        P(("group", "req"), None),
        P("group"),
        P(),
        P(("group", "req")),
        P(("group", "req"), "tp"),
        P(("group", "req"), None),
        P(("group", "req"), None, None),
        P("req", "tp"),
        P("req", "tp", None),
    )
    return jax.shard_map(
        shards,
        mesh=mesh,
        in_specs=placed,
        out_specs=(P(("group", "req"), None), P(("group", "req"), "tp")),
        check_vma=False,
    )
```

time: 78.4 us -> 23.1 us (0.29)
  blocking collectives: 57.3 us -> 11.1 us
  local copies, waits for them, and re-layouts: 5.86 us -> 0.03 us
  matrix products: 4.2 us -> 0 us
  Pallas kernels: 0 us -> 3.22 us
  other arithmetic: 1.91 us -> 0 us
    all_gather x1 -> x0, blocking collectives: 33.5 us -> none  [shards(): lax.all_gather(adapter_up, 'req', axis=0, tiled=True)]
    unnamed x1 -> x0, blocking collectives: 21.3 us -> none
    all_to_all x0 -> x1, blocking collectives: none -> 11.1 us  [exchange(): lax.all_to_all(x, 'req', split_axis=0, concat_axis=0, tiled=True, axis_in...]
    ppermute x0 -> x2, starting transfers between devices: none -> 7.82 us  [the longest x1 6.25 us: shards(): other = lax.ppermute(mine, 'tp', swap)]
    all_to_all x1 -> x0, starting transfers between devices: 7.26 us -> none  [shards(): lax.all_to_all(hidden, 'req', split_axis=1, concat_axis=0, tiled=True)]
    unnamed x16 -> x10, local copies, waits for them, and re-layouts: 4.96 us -> 0.03 us
    dot_general x6 -> x0, matrix products: 4.2 us -> none  [the longest x1 1.38 us: attend(): jnp.einsum('bhd,bld->bhl', q_rows, keys, preferred_element_type=jnp.float32)]
    pallas_call x0 -> x6, Pallas kernels: none -> 3.22 us  [the longest x1 1.17 us: shards(): pl.pallas_call(functools.partial(pack_kernel, order), out_shape=blocks_sh...]
  transfers between devices with their start and end apart: 1 -> 2, of which waited for: 0 -> 0; matrix products, arithmetic and copies ran while one was open for 10% -> 0% of each run, Pallas kernels for 0% -> 10%
where the time goes in v6:
time: 23.1 us; the launch traced here: 22.9 us
  blocking collectives  11.1 us (48%)
  starting transfers between devices  7.82 us (34%)
  Pallas kernels  3.22 us (14%)
  between operations  0.71 us (3%)
    all_to_all x1, blocking collectives, exchange(): lax.all_to_all(x, 'req', split_axis=0, concat_axis=0, tiled=True, axis_in...  11.1 us
    ppermute x1, starting transfers between devices, shards(): other = lax.ppermute(mine, 'tp', swap)  6.25 us
    ppermute x1, starting transfers between devices, shards(): far_down = lax.ppermute(near_down, 'tp', swap)  1.57 us
    pallas_call x1, Pallas kernels, shards(): pl.pallas_call(functools.partial(pack_kernel, order), out_shape=blocks_sh...  1.17 us
    pallas_call x1, Pallas kernels, shards(): pl.pallas_call(attend_kernel, out_shape=(jax.ShapeDtypeStruct((per_dev *...  1.06 us
    pallas_call x1, Pallas kernels, shards(): pl.pallas_call(functools.partial(merge_kernel, ranks), out_shape=(jax.Sha...  0.88 us
  transfers between devices with their start and end apart: 2, of which 0 were waited for; matrix products, arithmetic and copies ran while one was open for 0% of the time, Pallas kernels for 10%

profile of v6, /device:TPU:0, one launch (start us, length us, event | category | flops | bytes accessed | tf_op | source)
XLA Modules:
  0.0 22.9 jit_solution(10974584352318432450)
XLA Ops:
  0.6 0.0 copy-start
  0.6 0.1 shard_map.104
  0.7 1.6 %collective-permute-start = (bf16[2048,512]{1,0:T(8,128)(2,1)}, bf16[2048,512]{1,0:T(8,128)(2,1)S(1)}, u32[]{:S(2)}, u32[]{:S(2)}) collective-permute-start(bf16[2048,512]{1,0:T(8,128)(2,1)} %down_ref), channel_id=1, source_target_pairs={{0,1},{1,0},{2,3},{3,2},{4,5},{5,4},{6,7},{7,6},{8,9},{9,8},{10,11... | collective-permute-start | bytes 6291464 | tf_op jit(solution)/shard_map/ppermute | solution.py:268
  2.3 1.2 %shard_map.105 = bf16[8,4,2048]{2,1,0:T(4,128)(2,1)S(1)} custom-call(bf16[8,4,2048]{2,1,0:T(4,128)(2,1)S(1)} %get-tuple-element.27.blocks_ref, s32[1,32]{1,0:T(1,128)} %bitcast.9, s32[1,64]{1,0:T(1,128)} %bitcast.11, bf16[8,8,256]{2,1,0:T(8,128)(2,1)} %up_hbm.3, bf16[4,512,256]{2,1,0:T(8,128)(2,1)} %cache_ref, bf16[2048,512]{1,0:T(8,128)(2,1)} %down_ref), custom_call_target="tpu_custom_call" | custom-call | tf_op jit(solution)/shard_map/pallas_call | solution.py:269
  3.5 11.1 %all_to_all.10.got_ref = bf16[8,4,2048]{2,1,0:T(4,128)(2,1)S(1)} all-to-all(bf16[8,4,2048]{2,1,0:T(4,128)(2,1)S(1)} %shard_map.105), channel_id=1, replica_groups={{10,12,14,0,2,4,6,8},{11,13,15,1,3,5,7,9},{26,28,30,16,18,20,22,24},{27..., dimensions={0} | all-to-all | bytes 262144 | tf_op jit(solution)/shard_map/all_to_all | solution.py:247
  14.5 0.0 collective-permute-done.far_ref
  14.5 0.0 copy-done
  14.5 0.0 copy-start.1
  14.5 0.0 copy-start.2
  14.6 0.0 copy-start.4
  14.6 0.0 copy-start.3
  14.7 6.3 %collective-permute-start.1 = (bf16[80,128]{1,0:T(8,128)(2,1)S(1)}, bf16[80,128]{1,0:T(8,128)(2,1)S(1)}, u32[]{:S(2)}, u32[]{:S(2)}) collective-permute-start(bf16[80,128]{1,0:T(8,128)(2,1)S(1)} %get-tuple-element.39.mine_ref), channel_id=1, source_target_pairs={{0,1},{1,0},{2,3},{3,2},{4,5},{5,4},{6,7},{7,6},{8,9},{9,8},{10,11... | collective-permute-start | bytes 61448 | tf_op jit(solution)/shard_map/ppermute | solution.py:316
  20.9 0.0 copy-done.1
  20.9 0.0 copy-done.2
  20.9 0.0 copy-done.4
  20.9 1.1 %shard_map.107 = (f32[32,128]{1,0:T(8,128)S(1)}, f32[64,128]{1,0:T(8,128)S(1)}) custom-call(s32[1,4]{1,0:T(1,128)S(1)} %bitcast.6, bf16[4,1024]{1,0:T(4,128)(2,1)S(1)} %copy-done.2, bf16[4,512,256]{2,1,0:T(8,128)(2,1)S(1)} %copy-done.1), custom_call_target="tpu_custom_call" | custom-call | bytes 4194304 | tf_op jit(solution)/shard_map/pallas_call | solution.py:317
  22.0 0.0 collective-permute-done.1.other_ref
  22.0 0.0 copy-done.3
  22.0 0.9 %shard_map.108 = (bf16[4,256]{1,0:T(4,128)(2,1)}, bf16[4,1024]{1,0:T(4,128)(2,1)}) custom-call(bf16[80,128]{1,0:T(8,128)(2,1)S(1)} %get-tuple-element.39.mine_ref, bf16[80,128]{1,0:T(8,128)(2,1)S(1)} %collective-permute-done.1.other_ref, f32[32,128]{1,0:T(8,128)S(1)} %get-tuple-element.37.q_ref, f32[64,128]{1,0:T(8,128)S(1)} %get-tuple-element.38.stats_ref, ...), custom_call_target="tpu_custom_call" | custom-call | tf_op jit(solution)/shard_map/pallas_call | solution.py:328
  (3 shorter events, 0.1 us)
Async XLA Ops:
  0.6 13.9 %copy-start = (bf16[2048,512]{1,0:T(8,128)(2,1)S(1)}, bf16[2048,512]{1,0:T(8,128)(2,1)}, u32[]{:S(2)}) copy-start(bf16[2048,512]{1,0:T(8,128)(2,1)} %down_ref) | copy-start | bytes 6291460
  0.7 13.8 %collective-permute-start = (bf16[2048,512]{1,0:T(8,128)(2,1)}, bf16[2048,512]{1,0:T(8,128)(2,1)S(1)}, u32[]{:S(2)}, u32[]{:S(2)}) collective-permute-start(bf16[2048,512]{1,0:T(8,128)(2,1)} %down_ref), channel_id=1, source_target_pairs={{0,1},{1,0},{2,3},{3,2},{4,5},{5,4},{6,7},{7,6},{8,9},{9,8},{10,11... | collective-permute-start | bytes 6291464 | tf_op jit(solution)/shard_map/ppermute | solution.py:268
  14.5 6.4 %copy-start.1 = (bf16[4,512,256]{2,1,0:T(8,128)(2,1)S(1)}, bf16[4,512,256]{2,1,0:T(8,128)(2,1)}, u32[]{:S(2)}) copy-start(bf16[4,512,256]{2,1,0:T(8,128)(2,1)} %cache_ref) | copy-start | bytes 3145732
  14.5 6.4 %copy-start.2 = (bf16[4,1024]{1,0:T(4,128)(2,1)S(1)}, bf16[4,1024]{1,0:T(4,128)(2,1)}, u32[]{:S(2)}) copy-start(bf16[4,1024]{1,0:T(4,128)(2,1)} %query_ref) | copy-start | bytes 24580
  14.6 6.4 %copy-start.4 = (s32[4]{0:T(128)S(1)}, s32[4]{0:T(128)}, u32[]{:S(2)}) copy-start(s32[4]{0:T(128)} %param.14) | copy-start | bytes 52
  14.6 7.4 %copy-start.3 = (bf16[4,256]{1,0:T(4,128)(2,1)S(1)}, bf16[4,256]{1,0:T(4,128)(2,1)}, u32[]{:S(2)}) copy-start(bf16[4,256]{1,0:T(4,128)(2,1)} %base_ref.1) | copy-start | bytes 6148
  14.7 7.3 %collective-permute-start.1 = (bf16[80,128]{1,0:T(8,128)(2,1)S(1)}, bf16[80,128]{1,0:T(8,128)(2,1)S(1)}, u32[]{:S(2)}, u32[]{:S(2)}) collective-permute-start(bf16[80,128]{1,0:T(8,128)(2,1)S(1)} %get-tuple-element.39.mine_ref), channel_id=1, source_target_pairs={{0,1},{1,0},{2,3},{3,2},{4,5},{5,4},{6,7},{7,6},{8,9},{9,8},{10,11... | collective-permute-start | bytes 61448 | tf_op jit(solution)/shard_map/ppermute | solution.py:316

commit v7 on v6

--- a/solution.py
+++ b/solution.py
@@ -76,7 +76,13 @@
 
 
 def pack_kernel(
-    order, blocks_ref, ids_hbm, home_hbm, up_hbm, cache_hbm, down_hbm, out_ref,
+    order, blocks_ref, ids_hbm, home_hbm, up_hbm, cache_hbm, down_hbm, *rest
+):
+    pack(order, blocks_ref, ids_hbm, home_hbm, up_hbm, *rest[2:])
+
+
+def pack(
+    order, blocks_ref, ids_hbm, home_hbm, up_hbm, out_ref,
     ids_ref, home_ref, up_ref, flat_ref, wide_ref, sems
 ):
     count = out_ref.shape[1]
@@ -122,9 +128,11 @@
         rank = lane % (2 * ranks)
         low = jnp.zeros(names.shape, F32)
         for half, ref in enumerate((far_ref, down_ref)):
-            values = jnp.dot(blocks, ref[...], preferred_element_type=F32)
             for j in range(columns // 128):
-                got = jnp.take_along_axis(values[:, j * 128 : (j + 1) * 128], spot, axis=1)
+                values = jnp.dot(
+                    blocks, ref[:, j * 128 : (j + 1) * 128], preferred_element_type=F32
+                )
+                got = jnp.take_along_axis(values, spot, axis=1)
                 low = jnp.where(rank // 2 == j + half * ranks // 2, got, low)
         high = low.astype(BF16).astype(F32)
         low = jnp.where(lane < 2 * ranks, high, low - high).astype(BF16)
@@ -269,7 +277,7 @@
     blocks = pl.pallas_call(
         functools.partial(pack_kernel, order),
         out_shape=blocks_shape,
-        in_specs=[VMEM] + [HBM] * 5,
+        in_specs=[VMEM] + [HBM] * 7,
         out_specs=VMEM,
         scratch_shapes=[
             pltpu.VMEM(ids.shape, ids.dtype),
@@ -280,7 +288,10 @@
             pltpu.SemaphoreType.DMA((3,)),
         ],
         compiler_params=PARAMS,
-    )(blocks, pin(ids), pin(home), pin(adapter_up), pin(cache), pin(near_down))
+    )(
+        blocks, pin(ids), pin(home), pin(adapter_up),
+        pin(cache), pin(near_down), pin(cache), pin(near_down),
+    )
     got = exchange(blocks)
     packed = pl.pallas_call(
         functools.partial(low_kernel, order),

time: 23.1 us -> 23 us (level)
  no operation moved by 1% of the time
where the time goes in v7:
time: 23 us; the launch traced here: 22.8 us
  blocking collectives  11.1 us (48%)
  starting transfers between devices  7.73 us (34%)
  Pallas kernels  3.21 us (14%)
  between operations  0.71 us (3%)
    all_to_all x1, blocking collectives, exchange(): lax.all_to_all(x, 'req', split_axis=0, concat_axis=0, tiled=True, axis_in...  11.1 us
    ppermute x1, starting transfers between devices, shards(): other = lax.ppermute(mine, 'tp', swap)  6.3 us
    ppermute x1, starting transfers between devices, shards(): far_down = lax.ppermute(near_down, 'tp', swap)  1.43 us
    pallas_call x1, Pallas kernels, shards(): pl.pallas_call(functools.partial(pack_kernel, order), out_shape=blocks_sh...  1.16 us
    pallas_call x1, Pallas kernels, shards(): pl.pallas_call(attend_kernel, out_shape=(jax.ShapeDtypeStruct((per_dev *...  1.06 us
    pallas_call x1, Pallas kernels, shards(): pl.pallas_call(functools.partial(merge_kernel, ranks), out_shape=(jax.Sha...  0.88 us
  transfers between devices with their start and end apart: 2, of which 0 were waited for; matrix products, arithmetic and copies ran while one was open for 0% of the time, Pallas kernels for 10%

profile of v7, /device:TPU:0, one launch (start us, length us, event | category | flops | bytes accessed | tf_op | source)
XLA Modules:
  0.0 22.8 jit_solution(10757455009723288263)
XLA Ops:
  0.6 0.1 shard_map.104
  0.7 0.0 copy-start
  0.7 1.4 %collective-permute-start = (bf16[2048,512]{1,0:T(8,128)(2,1)}, bf16[2048,512]{1,0:T(8,128)(2,1)S(1)}, u32[]{:S(2)}, u32[]{:S(2)}) collective-permute-start(bf16[2048,512]{1,0:T(8,128)(2,1)} %down_ref), channel_id=1, source_target_pairs={{0,1},{1,0},{2,3},{3,2},{4,5},{5,4},{6,7},{7,6},{8,9},{9,8},{10,11... | collective-permute-start | bytes 6291464 | tf_op jit(solution)/shard_map/ppermute | solution.py:276
  2.1 1.2 %shard_map.105 = bf16[8,4,2048]{2,1,0:T(4,128)(2,1)S(1)} custom-call(bf16[8,4,2048]{2,1,0:T(4,128)(2,1)S(1)} %get-tuple-element.27.blocks_ref, s32[1,32]{1,0:T(1,128)} %bitcast.9, s32[1,64]{1,0:T(1,128)} %bitcast.11, bf16[8,8,256]{2,1,0:T(8,128)(2,1)} %up_hbm.3, bf16[4,512,256]{2,1,0:T(8,128)(2,1)} %cache_ref, bf16[2048,512]{1,0:T(8,128)(2,1)} %down_ref, ...), custom_call_target="tpu_custom_call" | custom-call | tf_op jit(solution)/shard_map/pallas_call | solution.py:277
  3.3 11.1 %all_to_all.10.got_ref = bf16[8,4,2048]{2,1,0:T(4,128)(2,1)S(1)} all-to-all(bf16[8,4,2048]{2,1,0:T(4,128)(2,1)S(1)} %shard_map.105), channel_id=1, replica_groups={{10,12,14,0,2,4,6,8},{11,13,15,1,3,5,7,9},{26,28,30,16,18,20,22,24},{27..., dimensions={0} | all-to-all | bytes 262144 | tf_op jit(solution)/shard_map/all_to_all | solution.py:255
  14.4 0.0 collective-permute-done.far_ref
  14.4 0.0 copy-done
  14.4 0.0 copy-start.1
  14.4 0.0 copy-start.2
  14.4 0.0 copy-start.4
  14.4 0.0 copy-start.3
  14.5 6.3 %collective-permute-start.1 = (bf16[80,128]{1,0:T(8,128)(2,1)S(1)}, bf16[80,128]{1,0:T(8,128)(2,1)S(1)}, u32[]{:S(2)}, u32[]{:S(2)}) collective-permute-start(bf16[80,128]{1,0:T(8,128)(2,1)S(1)} %get-tuple-element.39.mine_ref), channel_id=1, source_target_pairs={{0,1},{1,0},{2,3},{3,2},{4,5},{5,4},{6,7},{7,6},{8,9},{9,8},{10,11... | collective-permute-start | bytes 61448 | tf_op jit(solution)/shard_map/ppermute | solution.py:327
  20.8 0.0 copy-done.1
  20.8 0.0 copy-done.2
  20.8 0.0 copy-done.4
  20.8 1.1 %shard_map.107 = (f32[32,128]{1,0:T(8,128)S(1)}, f32[64,128]{1,0:T(8,128)S(1)}) custom-call(s32[1,4]{1,0:T(1,128)S(1)} %bitcast.6, bf16[4,1024]{1,0:T(4,128)(2,1)S(1)} %copy-done.2, bf16[4,512,256]{2,1,0:T(8,128)(2,1)S(1)} %copy-done.1), custom_call_target="tpu_custom_call" | custom-call | bytes 4194304 | tf_op jit(solution)/shard_map/pallas_call | solution.py:328
  21.9 0.0 collective-permute-done.1.other_ref
  21.9 0.0 copy-done.3
  21.9 0.9 %shard_map.108 = (bf16[4,256]{1,0:T(4,128)(2,1)}, bf16[4,1024]{1,0:T(4,128)(2,1)}) custom-call(bf16[80,128]{1,0:T(8,128)(2,1)S(1)} %get-tuple-element.39.mine_ref, bf16[80,128]{1,0:T(8,128)(2,1)S(1)} %collective-permute-done.1.other_ref, f32[32,128]{1,0:T(8,128)S(1)} %get-tuple-element.37.q_ref, f32[64,128]{1,0:T(8,128)S(1)} %get-tuple-element.38.stats_ref, ...), custom_call_target="tpu_custom_call" | custom-call | tf_op jit(solution)/shard_map/pallas_call | solution.py:339
  (3 shorter events, 0.1 us)
Async XLA Ops:
  0.7 13.7 %copy-start = (bf16[2048,512]{1,0:T(8,128)(2,1)S(1)}, bf16[2048,512]{1,0:T(8,128)(2,1)}, u32[]{:S(2)}) copy-start(bf16[2048,512]{1,0:T(8,128)(2,1)} %down_ref) | copy-start | bytes 6291460
  0.7 13.7 %collective-permute-start = (bf16[2048,512]{1,0:T(8,128)(2,1)}, bf16[2048,512]{1,0:T(8,128)(2,1)S(1)}, u32[]{:S(2)}, u32[]{:S(2)}) collective-permute-start(bf16[2048,512]{1,0:T(8,128)(2,1)} %down_ref), channel_id=1, source_target_pairs={{0,1},{1,0},{2,3},{3,2},{4,5},{5,4},{6,7},{7,6},{8,9},{9,8},{10,11... | collective-permute-start | bytes 6291464 | tf_op jit(solution)/shard_map/ppermute | solution.py:276
  14.4 6.4 %copy-start.1 = (bf16[4,512,256]{2,1,0:T(8,128)(2,1)S(1)}, bf16[4,512,256]{2,1,0:T(8,128)(2,1)}, u32[]{:S(2)}) copy-start(bf16[4,512,256]{2,1,0:T(8,128)(2,1)} %cache_ref) | copy-start | bytes 3145732
  14.4 6.4 %copy-start.2 = (bf16[4,1024]{1,0:T(4,128)(2,1)S(1)}, bf16[4,1024]{1,0:T(4,128)(2,1)}, u32[]{:S(2)}) copy-start(bf16[4,1024]{1,0:T(4,128)(2,1)} %query_ref) | copy-start | bytes 24580
  14.4 6.4 %copy-start.4 = (s32[4]{0:T(128)S(1)}, s32[4]{0:T(128)}, u32[]{:S(2)}) copy-start(s32[4]{0:T(128)} %param.14) | copy-start | bytes 52
  14.4 7.5 %copy-start.3 = (bf16[4,256]{1,0:T(4,128)(2,1)S(1)}, bf16[4,256]{1,0:T(4,128)(2,1)}, u32[]{:S(2)}) copy-start(bf16[4,256]{1,0:T(4,128)(2,1)} %base_ref.1) | copy-start | bytes 6148
  14.5 7.4 %collective-permute-start.1 = (bf16[80,128]{1,0:T(8,128)(2,1)S(1)}, bf16[80,128]{1,0:T(8,128)(2,1)S(1)}, u32[]{:S(2)}, u32[]{:S(2)}) collective-permute-start(bf16[80,128]{1,0:T(8,128)(2,1)S(1)} %get-tuple-element.39.mine_ref), channel_id=1, source_target_pairs={{0,1},{1,0},{2,3},{3,2},{4,5},{5,4},{6,7},{7,6},{8,9},{9,8},{10,11... | collective-permute-start | bytes 61448 | tf_op jit(solution)/shard_map/ppermute | solution.py:327

commit v8 on v7

--- a/solution.py
+++ b/solution.py
@@ -157,7 +157,35 @@
         out_ref[tall:, :] = jnp.concatenate([low] * (16 // count), axis=0).astype(BF16)
 
 
-def attend_kernel(lengths_ref, query_ref, cache_ref, q_ref, stats_ref):
+def early_kernel(
+    low_ref, lengths_hbm, query_hbm, cache_hbm, q_ref, stats_ref,
+    lengths_ref, query_ref, cache_ref, sems
+):
+    @pl.when(lax.axis_index("tp") == 0)
+    def _():
+        early(lengths_hbm, query_hbm, cache_hbm, q_ref, stats_ref,
+              lengths_ref, query_ref, cache_ref, sems)
+
+
+def early(
+    lengths_hbm, query_hbm, cache_hbm, q_ref, stats_ref, lengths_ref, query_ref, cache_ref, sems
+):
+    pairs = ((lengths_hbm, lengths_ref), (query_hbm, query_ref), (cache_hbm, cache_ref))
+    copies = [pltpu.make_async_copy(a, b, sems.at[i]) for i, (a, b) in enumerate(pairs)]
+    for copy in copies:
+        copy.start()
+    for copy in copies:
+        copy.wait()
+    attend(lengths_ref, query_ref, cache_ref, q_ref, stats_ref)
+
+
+def late_kernel(lengths_ref, query_ref, cache_ref, q_ref, stats_ref):
+    @pl.when(lax.axis_index("tp") == 1)
+    def _():
+        attend(lengths_ref, query_ref, cache_ref, q_ref, stats_ref)
+
+
+def attend(lengths_ref, query_ref, cache_ref, q_ref, stats_ref):
     count = cache_ref.shape[0]
     heads = query_ref.shape[1] // HD
     scale = HD ** (-0.5)
@@ -185,7 +213,8 @@
 
 
 def merge_kernel(
-    ranks, mine_ref, other_ref, q_ref, stats_ref, base_ref, kv_ref, out_ref, wide_ref
+    ranks, mine_ref, other_ref, q_ref, stats_ref, early_q_ref, early_ref, base_ref,
+    kv_ref, out_ref, wide_ref
 ):
     count, width = base_ref.shape
     rows = q_ref.shape[0]
@@ -209,8 +238,10 @@
     fresh = fresh.astype(BF16).astype(F32)
     for j in range(halves):
         kv_ref[:, j * HD : (j + 1) * HD] = fresh[j * count : (j + 1) * count].astype(BF16)
-    mean = stats_ref[:rows, :]
-    level = stats_ref[rows:, :1]
+    stats = jnp.where(lower, early_ref[...], stats_ref[...])
+    query = jnp.where(lower, early_q_ref[...], q_ref[...])
+    mean = stats[:rows]
+    level = stats[rows:, :1]
     spread = [
         jnp.concatenate(
             [
@@ -221,7 +252,7 @@
         )
         for j in range(halves)
     ]
-    own = jnp.sum(q_ref[...] * spread[0], axis=1, keepdims=True) * HD ** (-0.5)
+    own = jnp.sum(query * spread[0], axis=1, keepdims=True) * HD ** (-0.5)
     share = 1.0 / (1.0 + jnp.exp(level - own))
     wide_ref[...] = mean + share * (spread[1] - mean)
     for h in range(heads):
@@ -317,6 +348,23 @@
             compiler_params=PARAMS,
         )(x)
 
+    heads_shape = jax.ShapeDtypeStruct((per_dev * heads, HD), F32)
+    stats_shape = jax.ShapeDtypeStruct((2 * per_dev * heads, HD), F32)
+
+    early_q, early_stats = pl.pallas_call(
+        early_kernel,
+        out_shape=(heads_shape, stats_shape),
+        in_specs=[VMEM] + [HBM] * 3,
+        out_specs=(VMEM, VMEM),
+        scratch_shapes=[
+            pltpu.VMEM((1, per_dev), lengths.dtype),
+            pltpu.VMEM(query.shape, BF16),
+            pltpu.VMEM(cache.shape, BF16),
+            pltpu.SemaphoreType.DMA((3,)),
+        ],
+        compiler_params=PARAMS,
+    )(packed, pin(lengths.reshape(1, per_dev)), pin(query), pin(cache))
+    packed, got, early_q = lax.optimization_barrier((packed, got, early_q))
     mine = lax.cond(
         lower,
         lambda packed, got: fold(got[:, :, :span]),
@@ -326,11 +374,8 @@
     mine, lengths, query, cache = lax.optimization_barrier((mine, lengths, query, cache))
     other = lax.ppermute(mine, "tp", swap)
     q_rows, stats = pl.pallas_call(
-        attend_kernel,
-        out_shape=(
-            jax.ShapeDtypeStruct((per_dev * heads, HD), F32),
-            jax.ShapeDtypeStruct((2 * per_dev * heads, HD), F32),
-        ),
+        late_kernel,
+        out_shape=(heads_shape, stats_shape),
         in_specs=[VMEM] * 3,
         out_specs=(VMEM, VMEM),
         cost_estimate=pl.CostEstimate(flops=0, transcendentals=0, bytes_accessed=1 << 22),
@@ -342,11 +387,11 @@
             jax.ShapeDtypeStruct(kv_base.shape, BF16),
             jax.ShapeDtypeStruct(query.shape, BF16),
         ),
-        in_specs=[VMEM] * 5,
+        in_specs=[VMEM] * 7,
         out_specs=(VMEM, VMEM),
         scratch_shapes=[pltpu.VMEM((per_dev * heads, HD), F32)],
         compiler_params=PARAMS,
-    )(mine, other, q_rows, stats, kv_base)
+    )(mine, other, q_rows, stats, early_q, early_stats, kv_base)
     return (new_kv, attended)
 
 

time: 23 us -> 22.8 us (level)
  starting transfers between devices: 7.73 us -> 5.34 us
  Pallas kernels: 3.21 us -> 4.59 us
  waiting for transfers between devices: 0.01 us -> 0.82 us
    ppermute x1, starting transfers between devices: 6.3 us -> 3.91 us  [shards(): other = lax.ppermute(mine, 'tp', swap)]
    pallas_call x1 -> x2, Pallas kernels: 1.06 us -> 2.45 us  [the longest x1 2.44 us: shards(): pl.pallas_call(early_kernel, out_shape=(heads_shape, stats_shape), in_spe...]
    ppermute x1, waiting for transfers between devices: 0.01 us -> 0.82 us  [shards(): other = lax.ppermute(mine, 'tp', swap)]
  transfers between devices with their start and end apart: 2 -> 2, of which waited for: 0 -> 1; matrix products, arithmetic and copies ran while one was open for 0% -> 0% of each run, Pallas kernels for 10% -> 5%
where the time goes in v8:
time: 22.8 us; the launch traced here: 22.6 us
  blocking collectives  11.1 us (49%)
  starting transfers between devices  5.34 us (23%)
  Pallas kernels  4.59 us (20%)
  waiting for transfers between devices  0.82 us (4%)
  between operations  0.72 us (3%)
    all_to_all x1, blocking collectives, exchange(): lax.all_to_all(x, 'req', split_axis=0, concat_axis=0, tiled=True, axis_in...  11.1 us
    ppermute x1, starting transfers between devices, shards(): other = lax.ppermute(mine, 'tp', swap)  3.91 us
    pallas_call x1, Pallas kernels, shards(): pl.pallas_call(early_kernel, out_shape=(heads_shape, stats_shape), in_spe...  2.44 us
    ppermute x1, starting transfers between devices, shards(): far_down = lax.ppermute(near_down, 'tp', swap)  1.43 us
    pallas_call x1, Pallas kernels, shards(): pl.pallas_call(functools.partial(pack_kernel, order), out_shape=blocks_sh...  1.16 us
    pallas_call x1, Pallas kernels, shards(): pl.pallas_call(functools.partial(merge_kernel, ranks), out_shape=(jax.Sha...  0.88 us
    ppermute x1, waiting for transfers between devices, shards(): other = lax.ppermute(mine, 'tp', swap)  0.82 us
  transfers between devices with their start and end apart: 2, of which 1 were waited for; matrix products, arithmetic and copies ran while one was open for 0% of the time, Pallas kernels for 5%

profile of v8, /device:TPU:0, one launch (start us, length us, event | category | flops | bytes accessed | tf_op | source)
XLA Modules:
  0.0 22.6 jit_solution(9820162090397124663)
XLA Ops:
  0.6 0.1 shard_map.104
  0.7 0.0 copy-start
  0.7 1.4 %collective-permute-start = (bf16[2048,512]{1,0:T(8,128)(2,1)}, bf16[2048,512]{1,0:T(8,128)(2,1)S(1)}, u32[]{:S(2)}, u32[]{:S(2)}) collective-permute-start(bf16[2048,512]{1,0:T(8,128)(2,1)} %down_ref), channel_id=1, source_target_pairs={{0,1},{1,0},{2,3},{3,2},{4,5},{5,4},{6,7},{7,6},{8,9},{9,8},{10,11... | collective-permute-start | bytes 6291464 | tf_op jit(solution)/shard_map/ppermute | solution.py:307
  2.1 1.2 %shard_map.105 = bf16[8,4,2048]{2,1,0:T(4,128)(2,1)S(1)} custom-call(bf16[8,4,2048]{2,1,0:T(4,128)(2,1)S(1)} %get-tuple-element.32.blocks_ref, s32[1,32]{1,0:T(1,128)} %bitcast.11, s32[1,64]{1,0:T(1,128)} %bitcast.13, bf16[8,8,256]{2,1,0:T(8,128)(2,1)} %up_hbm.3, bf16[4,512,256]{2,1,0:T(8,128)(2,1)} %cache_ref, bf16[2048,512]{1,0:T(8,128)(2,1)} %down_ref, ...), custom_call_target="tpu_custom_call" | custom-call | tf_op jit(solution)/shard_map/pallas_call | solution.py:308
  3.3 11.1 %all_to_all.10.got_ref = bf16[8,4,2048]{2,1,0:T(4,128)(2,1)S(1)} all-to-all(bf16[8,4,2048]{2,1,0:T(4,128)(2,1)S(1)} %shard_map.105), channel_id=1, replica_groups={{10,12,14,0,2,4,6,8},{11,13,15,1,3,5,7,9},{26,28,30,16,18,20,22,24},{27..., dimensions={0} | all-to-all | bytes 262144 | tf_op jit(solution)/shard_map/all_to_all | solution.py:286
  14.4 0.0 collective-permute-done.far_ref
  14.4 0.0 copy-done
  14.4 0.0 copy-start.1
  14.4 0.0 copy-start.2
  14.4 0.0 copy-start.4
  14.5 0.0 copy-start.3
  14.5 2.4 %shard_map.107 = (f32[32,128]{1,0:T(8,128)S(1)}, f32[64,128]{1,0:T(8,128)S(1)}) custom-call(bf16[8,4,2176]{2,1,0:T(4,128)(2,1)S(1)} %shard_map.106.low_ref, s32[1,4]{1,0:T(1,128)} %bitcast.7, bf16[4,1024]{1,0:T(4,128)(2,1)} %query_ref, bf16[4,512,256]{2,1,0:T(8,128)(2,1)} %cache_ref), custom_call_target="tpu_custom_call" | custom-call | tf_op jit(solution)/shard_map/pallas_call | solution.py:354
  16.9 0.1 conditional.1
  17.0 3.9 %collective-permute-start.1 = (bf16[80,128]{1,0:T(8,128)(2,1)S(1)}, bf16[80,128]{1,0:T(8,128)(2,1)S(1)}, u32[]{:S(2)}, u32[]{:S(2)}) collective-permute-start(bf16[80,128]{1,0:T(8,128)(2,1)S(1)} %get-tuple-element.49.mine_ref), channel_id=1, source_target_pairs={{0,1},{1,0},{2,3},{3,2},{4,5},{5,4},{6,7},{7,6},{8,9},{9,8},{10,11... | collective-permute-start | bytes 61448 | tf_op jit(solution)/shard_map/ppermute | solution.py:375
  20.9 0.0 copy-done.1
  20.9 0.0 copy-done.2
  20.9 0.0 copy-done.4
  20.9 0.8 %collective-permute-done.1.other_ref = bf16[80,128]{1,0:T(8,128)(2,1)S(1)} collective-permute-done((bf16[80,128]{1,0:T(8,128)(2,1)S(1)}, bf16[80,128]{1,0:T(8,128)(2,1)S(1)}, u32[]{:S(2)}, u32[]{:S(2)}) %collective-permute-start.1) | collective-permute-done | bytes 20512 | tf_op jit(solution)/shard_map/ppermute | solution.py:375
  21.7 0.0 copy-done.3
  21.7 0.9 %shard_map.109 = (bf16[4,256]{1,0:T(4,128)(2,1)}, bf16[4,1024]{1,0:T(4,128)(2,1)}) custom-call(bf16[80,128]{1,0:T(8,128)(2,1)S(1)} %get-tuple-element.49.mine_ref, bf16[80,128]{1,0:T(8,128)(2,1)S(1)} %collective-permute-done.1.other_ref, f32[32,128]{1,0:T(8,128)S(1)} %get-tuple-element.45.q_ref, f32[64,128]{1,0:T(8,128)S(1)} %get-tuple-element.46.stats_ref, ...), custom_call_target="tpu_custom_call" | custom-call | tf_op jit(solution)/shard_map/pallas_call | solution.py:384
  (3 shorter events, 0.1 us)
Async XLA Ops:
  0.7 13.7 %copy-start = (bf16[2048,512]{1,0:T(8,128)(2,1)S(1)}, bf16[2048,512]{1,0:T(8,128)(2,1)}, u32[]{:S(2)}) copy-start(bf16[2048,512]{1,0:T(8,128)(2,1)} %down_ref) | copy-start | bytes 6291460
  0.7 13.7 %collective-permute-start = (bf16[2048,512]{1,0:T(8,128)(2,1)}, bf16[2048,512]{1,0:T(8,128)(2,1)S(1)}, u32[]{:S(2)}, u32[]{:S(2)}) collective-permute-start(bf16[2048,512]{1,0:T(8,128)(2,1)} %down_ref), channel_id=1, source_target_pairs={{0,1},{1,0},{2,3},{3,2},{4,5},{5,4},{6,7},{7,6},{8,9},{9,8},{10,11... | collective-permute-start | bytes 6291464 | tf_op jit(solution)/shard_map/ppermute | solution.py:307
  14.4 6.5 %copy-start.1 = (bf16[4,512,256]{2,1,0:T(8,128)(2,1)S(1)}, bf16[4,512,256]{2,1,0:T(8,128)(2,1)}, u32[]{:S(2)}) copy-start(bf16[4,512,256]{2,1,0:T(8,128)(2,1)} %cache_ref) | copy-start | bytes 3145732
  14.4 6.5 %copy-start.2 = (bf16[4,1024]{1,0:T(4,128)(2,1)S(1)}, bf16[4,1024]{1,0:T(4,128)(2,1)}, u32[]{:S(2)}) copy-start(bf16[4,1024]{1,0:T(4,128)(2,1)} %query_ref) | copy-start | bytes 24580
  14.4 6.5 %copy-start.4 = (s32[4]{0:T(128)S(1)}, s32[4]{0:T(128)}, u32[]{:S(2)}) copy-start(s32[4]{0:T(128)} %param.14) | copy-start | bytes 52
  14.5 7.3 %copy-start.3 = (bf16[4,256]{1,0:T(4,128)(2,1)S(1)}, bf16[4,256]{1,0:T(4,128)(2,1)}, u32[]{:S(2)}) copy-start(bf16[4,256]{1,0:T(4,128)(2,1)} %base_ref.1) | copy-start | bytes 6148
  17.0 4.8 %collective-permute-start.1 = (bf16[80,128]{1,0:T(8,128)(2,1)S(1)}, bf16[80,128]{1,0:T(8,128)(2,1)S(1)}, u32[]{:S(2)}, u32[]{:S(2)}) collective-permute-start(bf16[80,128]{1,0:T(8,128)(2,1)S(1)} %get-tuple-element.49.mine_ref), channel_id=1, source_target_pairs={{0,1},{1,0},{2,3},{3,2},{4,5},{5,4},{6,7},{7,6},{8,9},{9,8},{10,11... | collective-permute-start | bytes 61448 | tf_op jit(solution)/shard_map/ppermute | solution.py:375

commit v9 on v8

--- a/solution.py
+++ b/solution.py
@@ -30,24 +30,31 @@
     return lax.dot_general(a, b, (((0,), (0,)), ((), ())), preferred_element_type=F32)
 
 
+def runs(order):
+    found = []
+    for p, q in enumerate(order):
+        if p and q == order[p - 1] + 1:
+            found[-1] = (found[-1][0], found[-1][1] + 1)
+        else:
+            found.append((p, 1))
+    return found
+
+
 def start_kernel(
-    hidden_ref, ids_hbm, home_hbm, up_hbm, out_ref, ids_ref, home_ref, up_ref, sems
+    order, hidden_ref, ids_hbm, home_hbm, up_hbm, out_ref, ids_ref, home_ref, up_ref, sems
 ):
     parts, _, block = hidden_ref.shape
-    center = (parts // 2 + 1) % parts
 
     @pl.when(lax.axis_index("tp") == 1)
     def _():
         copies = [
-            pltpu.make_async_copy(
-                hidden_ref.at[pl.ds(center, parts - center)],
-                out_ref.at[pl.ds(0, parts - center), :, pl.ds(0, block)],
-                sems.at[0],
-            ),
-            pltpu.make_async_copy(
-                hidden_ref.at[pl.ds(0, center)],
-                out_ref.at[pl.ds(parts - center, center), :, pl.ds(0, block)],
-                sems.at[1],
+            *(
+                pltpu.make_async_copy(
+                    hidden_ref.at[pl.ds(order[at], count)],
+                    out_ref.at[pl.ds(at, count), :, pl.ds(0, block)],
+                    sems.at[5 + i],
+                )
+                for i, (at, count) in enumerate(runs(order))
             ),
             pltpu.make_async_copy(ids_hbm, ids_ref, sems.at[2]),
             pltpu.make_async_copy(home_hbm, home_ref, sems.at[3]),
@@ -120,9 +127,13 @@
         blocks = jnp.concatenate(pieces, axis=0).astype(BF16)
         names = across(one_hot_ids(ids_ref[...]), iota((ADAPTERS, 128), 0).astype(BF16))
         names = names.astype(jnp.int32)
-        shift = order[0] * per_dev
-        if shift:
-            names = jnp.concatenate([names[shift:], names[:shift]], axis=0)
+        names = jnp.concatenate(
+            [
+                names[order[at] * per_dev : (order[at] + count) * per_dev]
+                for at, count in runs(order)
+            ],
+            axis=0,
+        )
         lane = iota(names.shape, 1)
         spot = names + lane % 2 * ADAPTERS
         rank = lane % (2 * ranks)
@@ -271,7 +282,7 @@
     span = ranks * width
     wide = max(block, span)
     center = (parts // 2 + 1) % parts
-    order = [(center + p) % parts for p in range(parts)]
+    order = [center, 0, *range(center + 1, parts), *range(1, center)] if center else [*range(parts)]
     depth = -(-slots // 8) * 8
     core = lax.axis_index("tp").astype(jnp.int32)
     swap = [(0, 1), (1, 0)]
@@ -291,11 +302,11 @@
     home = home_slot.reshape(1, ADAPTERS)
     like = lambda x: jax.ShapeDtypeStruct(x.shape, x.dtype)
     blocks, near_ids, near_home, near_up = pl.pallas_call(
-        start_kernel,
+        functools.partial(start_kernel, order),
         out_shape=(blocks_shape, like(ids), like(home), like(adapter_up)),
         in_specs=[HBM] * 4,
         out_specs=(VMEM,) * 4,
-        scratch_shapes=[pltpu.SemaphoreType.DMA((5,))],
+        scratch_shapes=[pltpu.SemaphoreType.DMA((5 + len(runs(order)),))],
         compiler_params=PARAMS,
     )(
         pin(jnp.swapaxes(hidden.reshape(per_dev, parts, block), 0, 1)),

time: 22.8 us -> 22.2 us (0.974)
  blocking collectives: 11.1 us -> 10.6 us
    all_to_all x1, blocking collectives: 11.1 us -> 10.6 us  [exchange(): lax.all_to_all(x, 'req', split_axis=0, concat_axis=0, tiled=True, axis_in...]
where the time goes in v9:
time: 22.2 us; the launch traced here: 21.9 us
  blocking collectives  10.6 us (48%)
  starting transfers between devices  5.14 us (23%)
  Pallas kernels  4.64 us (21%)
  waiting for transfers between devices  0.82 us (4%)
  between operations  0.72 us (3%)
    all_to_all x1, blocking collectives, exchange(): lax.all_to_all(x, 'req', split_axis=0, concat_axis=0, tiled=True, axis_in...  10.6 us
    ppermute x1, starting transfers between devices, shards(): other = lax.ppermute(mine, 'tp', swap)  3.74 us
    pallas_call x1, Pallas kernels, shards(): pl.pallas_call(early_kernel, out_shape=(heads_shape, stats_shape), in_spe...  2.44 us
    ppermute x1, starting transfers between devices, shards(): far_down = lax.ppermute(near_down, 'tp', swap)  1.4 us
    pallas_call x1, Pallas kernels, shards(): pl.pallas_call(functools.partial(pack_kernel, order), out_shape=blocks_sh...  1.17 us
    pallas_call x1, Pallas kernels, shards(): pl.pallas_call(functools.partial(merge_kernel, ranks), out_shape=(jax.Sha...  0.88 us
    ppermute x1, waiting for transfers between devices, shards(): other = lax.ppermute(mine, 'tp', swap)  0.82 us
  transfers between devices with their start and end apart: 2, of which 1 were waited for; matrix products, arithmetic and copies ran while one was open for 0% of the time, Pallas kernels for 5%

profile of v9, /device:TPU:0, one launch (start us, length us, event | category | flops | bytes accessed | tf_op | source)
XLA Modules:
  0.0 21.9 jit_solution(10352180029373509456)
XLA Ops:
  0.6 0.1 shard_map.104
  0.7 0.0 copy-start
  0.8 1.4 %collective-permute-start = (bf16[2048,512]{1,0:T(8,128)(2,1)}, bf16[2048,512]{1,0:T(8,128)(2,1)S(1)}, u32[]{:S(2)}, u32[]{:S(2)}) collective-permute-start(bf16[2048,512]{1,0:T(8,128)(2,1)} %down_ref), channel_id=1, source_target_pairs={{0,1},{1,0},{2,3},{3,2},{4,5},{5,4},{6,7},{7,6},{8,9},{9,8},{10,11... | collective-permute-start | bytes 6291464 | tf_op jit(solution)/shard_map/ppermute | solution.py:318
  2.2 1.2 %shard_map.105 = bf16[8,4,2048]{2,1,0:T(4,128)(2,1)S(1)} custom-call(bf16[8,4,2048]{2,1,0:T(4,128)(2,1)S(1)} %get-tuple-element.32.blocks_ref, s32[1,32]{1,0:T(1,128)} %bitcast.11, s32[1,64]{1,0:T(1,128)} %bitcast.13, bf16[8,8,256]{2,1,0:T(8,128)(2,1)} %up_hbm.3, bf16[4,512,256]{2,1,0:T(8,128)(2,1)} %cache_ref, bf16[2048,512]{1,0:T(8,128)(2,1)} %down_ref, ...), custom_call_target="tpu_custom_call" | custom-call | tf_op jit(solution)/shard_map/pallas_call | solution.py:319
  3.3 10.6 %all_to_all.10.got_ref = bf16[8,4,2048]{2,1,0:T(4,128)(2,1)S(1)} all-to-all(bf16[8,4,2048]{2,1,0:T(4,128)(2,1)S(1)} %shard_map.105), channel_id=1, replica_groups={{10,0,12,14,2,4,6,8},{11,1,13,15,3,5,7,9},{26,16,28,30,18,20,22,24},{27..., dimensions={0} | all-to-all | bytes 262144 | tf_op jit(solution)/shard_map/all_to_all | solution.py:297
  13.9 0.0 collective-permute-done.far_ref
  13.9 0.0 copy-done
  13.9 0.0 copy-start.1
  13.9 0.0 copy-start.2
  13.9 0.0 copy-start.4
  13.9 0.0 copy-start.3
  14.0 2.4 %shard_map.107 = (f32[32,128]{1,0:T(8,128)S(1)}, f32[64,128]{1,0:T(8,128)S(1)}) custom-call(bf16[8,4,2176]{2,1,0:T(4,128)(2,1)S(1)} %shard_map.106.low_ref, s32[1,4]{1,0:T(1,128)} %bitcast.7, bf16[4,1024]{1,0:T(4,128)(2,1)} %query_ref, bf16[4,512,256]{2,1,0:T(8,128)(2,1)} %cache_ref), custom_call_target="tpu_custom_call" | custom-call | tf_op jit(solution)/shard_map/pallas_call | solution.py:365
  16.4 0.1 conditional.1
  16.5 3.7 %collective-permute-start.1 = (bf16[80,128]{1,0:T(8,128)(2,1)S(1)}, bf16[80,128]{1,0:T(8,128)(2,1)S(1)}, u32[]{:S(2)}, u32[]{:S(2)}) collective-permute-start(bf16[80,128]{1,0:T(8,128)(2,1)S(1)} %get-tuple-element.49.mine_ref), channel_id=1, source_target_pairs={{0,1},{1,0},{2,3},{3,2},{4,5},{5,4},{6,7},{7,6},{8,9},{9,8},{10,11... | collective-permute-start | bytes 61448 | tf_op jit(solution)/shard_map/ppermute | solution.py:386
  20.2 0.0 copy-done.1
  20.2 0.0 copy-done.2
  20.2 0.0 copy-done.4
  20.2 0.8 %collective-permute-done.1.other_ref = bf16[80,128]{1,0:T(8,128)(2,1)S(1)} collective-permute-done((bf16[80,128]{1,0:T(8,128)(2,1)S(1)}, bf16[80,128]{1,0:T(8,128)(2,1)S(1)}, u32[]{:S(2)}, u32[]{:S(2)}) %collective-permute-start.1) | collective-permute-done | bytes 20512 | tf_op jit(solution)/shard_map/ppermute | solution.py:386
  21.0 0.0 copy-done.3
  21.0 0.9 %shard_map.109 = (bf16[4,256]{1,0:T(4,128)(2,1)}, bf16[4,1024]{1,0:T(4,128)(2,1)}) custom-call(bf16[80,128]{1,0:T(8,128)(2,1)S(1)} %get-tuple-element.49.mine_ref, bf16[80,128]{1,0:T(8,128)(2,1)S(1)} %collective-permute-done.1.other_ref, f32[32,128]{1,0:T(8,128)S(1)} %get-tuple-element.45.q_ref, f32[64,128]{1,0:T(8,128)S(1)} %get-tuple-element.46.stats_ref, ...), custom_call_target="tpu_custom_call" | custom-call | tf_op jit(solution)/shard_map/pallas_call | solution.py:395
  (3 shorter events, 0.1 us)
Async XLA Ops:
  0.7 13.1 %copy-start = (bf16[2048,512]{1,0:T(8,128)(2,1)S(1)}, bf16[2048,512]{1,0:T(8,128)(2,1)}, u32[]{:S(2)}) copy-start(bf16[2048,512]{1,0:T(8,128)(2,1)} %down_ref) | copy-start | bytes 6291460
  0.8 13.1 %collective-permute-start = (bf16[2048,512]{1,0:T(8,128)(2,1)}, bf16[2048,512]{1,0:T(8,128)(2,1)S(1)}, u32[]{:S(2)}, u32[]{:S(2)}) collective-permute-start(bf16[2048,512]{1,0:T(8,128)(2,1)} %down_ref), channel_id=1, source_target_pairs={{0,1},{1,0},{2,3},{3,2},{4,5},{5,4},{6,7},{7,6},{8,9},{9,8},{10,11... | collective-permute-start | bytes 6291464 | tf_op jit(solution)/shard_map/ppermute | solution.py:318
  13.9 6.3 %copy-start.1 = (bf16[4,512,256]{2,1,0:T(8,128)(2,1)S(1)}, bf16[4,512,256]{2,1,0:T(8,128)(2,1)}, u32[]{:S(2)}) copy-start(bf16[4,512,256]{2,1,0:T(8,128)(2,1)} %cache_ref) | copy-start | bytes 3145732
  13.9 6.3 %copy-start.2 = (bf16[4,1024]{1,0:T(4,128)(2,1)S(1)}, bf16[4,1024]{1,0:T(4,128)(2,1)}, u32[]{:S(2)}) copy-start(bf16[4,1024]{1,0:T(4,128)(2,1)} %query_ref) | copy-start | bytes 24580
  13.9 6.3 %copy-start.4 = (s32[4]{0:T(128)S(1)}, s32[4]{0:T(128)}, u32[]{:S(2)}) copy-start(s32[4]{0:T(128)} %param.14) | copy-start | bytes 52
  13.9 7.1 %copy-start.3 = (bf16[4,256]{1,0:T(4,128)(2,1)S(1)}, bf16[4,256]{1,0:T(4,128)(2,1)}, u32[]{:S(2)}) copy-start(bf16[4,256]{1,0:T(4,128)(2,1)} %base_ref.1) | copy-start | bytes 6148
  16.5 4.6 %collective-permute-start.1 = (bf16[80,128]{1,0:T(8,128)(2,1)S(1)}, bf16[80,128]{1,0:T(8,128)(2,1)S(1)}, u32[]{:S(2)}, u32[]{:S(2)}) collective-permute-start(bf16[80,128]{1,0:T(8,128)(2,1)S(1)} %get-tuple-element.49.mine_ref), channel_id=1, source_target_pairs={{0,1},{1,0},{2,3},{3,2},{4,5},{5,4},{6,7},{7,6},{8,9},{9,8},{10,11... | collective-permute-start | bytes 61448 | tf_op jit(solution)/shard_map/ppermute | solution.py:386

commit v10 on v9

--- a/solution.py
+++ b/solution.py
@@ -107,10 +107,6 @@
         rows = needed_rows(ids_ref[...], home_ref[...], up_ref, flat_ref, wide_ref)
         for p, q in enumerate(order):
             out_ref[p, :, :span] = rows[q * count : (q + 1) * count]
-
-    @pl.when(jnp.logical_not(lower))
-    def _():
-        out_ref[...] = blocks_ref[...]
 
 
 def low_kernel(
@@ -329,6 +325,7 @@
             pltpu.VMEM((slots, ranks, width), F32),
             pltpu.SemaphoreType.DMA((3,)),
         ],
+        input_output_aliases={0: 0},
         compiler_params=PARAMS,
     )(
         blocks, pin(ids), pin(home), pin(adapter_up),

time: 22.2 us -> 22.2 us (level)
  no operation moved by 1% of the time
where the time goes in v10:
time: 22.2 us; the launch traced here: 21.9 us
  blocking collectives  10.6 us (48%)
  starting transfers between devices  5.14 us (23%)
  Pallas kernels  4.64 us (21%)
  waiting for transfers between devices  0.82 us (4%)
  between operations  0.72 us (3%)
    all_to_all x1, blocking collectives, exchange(): lax.all_to_all(x, 'req', split_axis=0, concat_axis=0, tiled=True, axis_in...  10.6 us
    ppermute x1, starting transfers between devices, shards(): other = lax.ppermute(mine, 'tp', swap)  3.73 us
    pallas_call x1, Pallas kernels, shards(): pl.pallas_call(early_kernel, out_shape=(heads_shape, stats_shape), in_spe...  2.44 us
    ppermute x1, starting transfers between devices, shards(): far_down = lax.ppermute(near_down, 'tp', swap)  1.4 us
    pallas_call x1, Pallas kernels, shards(): pl.pallas_call(functools.partial(pack_kernel, order), out_shape=blocks_sh...  1.17 us
    pallas_call x1, Pallas kernels, shards(): pl.pallas_call(functools.partial(merge_kernel, ranks), out_shape=(jax.Sha...  0.88 us
    ppermute x1, waiting for transfers between devices, shards(): other = lax.ppermute(mine, 'tp', swap)  0.82 us
  transfers between devices with their start and end apart: 2, of which 1 were waited for; matrix products, arithmetic and copies ran while one was open for 0% of the time, Pallas kernels for 5%

profile of v10, /device:TPU:0, one launch (start us, length us, event | category | flops | bytes accessed | tf_op | source)
XLA Modules:
  0.0 21.9 jit_solution(2157498637809222379)
XLA Ops:
  0.6 0.1 shard_map.104
  0.7 0.0 copy-start
  0.8 1.4 %collective-permute-start = (bf16[2048,512]{1,0:T(8,128)(2,1)}, bf16[2048,512]{1,0:T(8,128)(2,1)S(1)}, u32[]{:S(2)}, u32[]{:S(2)}) collective-permute-start(bf16[2048,512]{1,0:T(8,128)(2,1)} %down_ref), channel_id=1, source_target_pairs={{0,1},{1,0},{2,3},{3,2},{4,5},{5,4},{6,7},{7,6},{8,9},{9,8},{10,11... | collective-permute-start | bytes 6291464 | tf_op jit(solution)/shard_map/ppermute | solution.py:314
  2.2 1.2 %shard_map.105 = bf16[8,4,2048]{2,1,0:T(4,128)(2,1)S(1)} custom-call(bf16[8,4,2048]{2,1,0:T(4,128)(2,1)S(1)} %get-tuple-element.32.blocks_ref, s32[1,32]{1,0:T(1,128)} %bitcast.11, s32[1,64]{1,0:T(1,128)} %bitcast.13, bf16[8,8,256]{2,1,0:T(8,128)(2,1)} %up_hbm.3, bf16[4,512,256]{2,1,0:T(8,128)(2,1)} %cache_ref, ...), custom_call_target="tpu_custom_call", output_to_operand_aliasing={{}: (0, {})} | custom-call | tf_op jit(solution)/shard_map/pallas_call | solution.py:315
  3.3 10.6 %all_to_all.10.got_ref = bf16[8,4,2048]{2,1,0:T(4,128)(2,1)S(1)} all-to-all(bf16[8,4,2048]{2,1,0:T(4,128)(2,1)S(1)} %shard_map.105), channel_id=1, replica_groups={{10,0,12,14,2,4,6,8},{11,1,13,15,3,5,7,9},{26,16,28,30,18,20,22,24},{27..., dimensions={0} | all-to-all | bytes 262144 | tf_op jit(solution)/shard_map/all_to_all | solution.py:293
  13.9 0.0 collective-permute-done.far_ref
  13.9 0.0 copy-done
  13.9 0.0 copy-start.1
  13.9 0.0 copy-start.2
  13.9 0.0 copy-start.4
  13.9 0.0 copy-start.3
  14.0 2.4 %shard_map.107 = (f32[32,128]{1,0:T(8,128)S(1)}, f32[64,128]{1,0:T(8,128)S(1)}) custom-call(bf16[8,4,2176]{2,1,0:T(4,128)(2,1)S(1)} %shard_map.106.low_ref, s32[1,4]{1,0:T(1,128)} %bitcast.7, bf16[4,1024]{1,0:T(4,128)(2,1)} %query_ref, bf16[4,512,256]{2,1,0:T(8,128)(2,1)} %cache_ref), custom_call_target="tpu_custom_call" | custom-call | tf_op jit(solution)/shard_map/pallas_call | solution.py:362
  16.4 0.1 conditional.1
  16.5 3.7 %collective-permute-start.1 = (bf16[80,128]{1,0:T(8,128)(2,1)S(1)}, bf16[80,128]{1,0:T(8,128)(2,1)S(1)}, u32[]{:S(2)}, u32[]{:S(2)}) collective-permute-start(bf16[80,128]{1,0:T(8,128)(2,1)S(1)} %get-tuple-element.49.mine_ref), channel_id=1, source_target_pairs={{0,1},{1,0},{2,3},{3,2},{4,5},{5,4},{6,7},{7,6},{8,9},{9,8},{10,11... | collective-permute-start | bytes 61448 | tf_op jit(solution)/shard_map/ppermute | solution.py:383
  20.2 0.0 copy-done.1
  20.2 0.0 copy-done.2
  20.2 0.0 copy-done.4
  20.2 0.8 %collective-permute-done.1.other_ref = bf16[80,128]{1,0:T(8,128)(2,1)S(1)} collective-permute-done((bf16[80,128]{1,0:T(8,128)(2,1)S(1)}, bf16[80,128]{1,0:T(8,128)(2,1)S(1)}, u32[]{:S(2)}, u32[]{:S(2)}) %collective-permute-start.1) | collective-permute-done | bytes 20512 | tf_op jit(solution)/shard_map/ppermute | solution.py:383
  21.0 0.0 copy-done.3
  21.0 0.9 %shard_map.109 = (bf16[4,256]{1,0:T(4,128)(2,1)}, bf16[4,1024]{1,0:T(4,128)(2,1)}) custom-call(bf16[80,128]{1,0:T(8,128)(2,1)S(1)} %get-tuple-element.49.mine_ref, bf16[80,128]{1,0:T(8,128)(2,1)S(1)} %collective-permute-done.1.other_ref, f32[32,128]{1,0:T(8,128)S(1)} %get-tuple-element.45.q_ref, f32[64,128]{1,0:T(8,128)S(1)} %get-tuple-element.46.stats_ref, ...), custom_call_target="tpu_custom_call" | custom-call | tf_op jit(solution)/shard_map/pallas_call | solution.py:392
  (3 shorter events, 0.1 us)
Async XLA Ops:
  0.7 13.1 %copy-start = (bf16[2048,512]{1,0:T(8,128)(2,1)S(1)}, bf16[2048,512]{1,0:T(8,128)(2,1)}, u32[]{:S(2)}) copy-start(bf16[2048,512]{1,0:T(8,128)(2,1)} %down_ref) | copy-start | bytes 6291460
  0.8 13.1 %collective-permute-start = (bf16[2048,512]{1,0:T(8,128)(2,1)}, bf16[2048,512]{1,0:T(8,128)(2,1)S(1)}, u32[]{:S(2)}, u32[]{:S(2)}) collective-permute-start(bf16[2048,512]{1,0:T(8,128)(2,1)} %down_ref), channel_id=1, source_target_pairs={{0,1},{1,0},{2,3},{3,2},{4,5},{5,4},{6,7},{7,6},{8,9},{9,8},{10,11... | collective-permute-start | bytes 6291464 | tf_op jit(solution)/shard_map/ppermute | solution.py:314
  13.9 6.3 %copy-start.1 = (bf16[4,512,256]{2,1,0:T(8,128)(2,1)S(1)}, bf16[4,512,256]{2,1,0:T(8,128)(2,1)}, u32[]{:S(2)}) copy-start(bf16[4,512,256]{2,1,0:T(8,128)(2,1)} %cache_ref) | copy-start | bytes 3145732
  13.9 6.3 %copy-start.2 = (bf16[4,1024]{1,0:T(4,128)(2,1)S(1)}, bf16[4,1024]{1,0:T(4,128)(2,1)}, u32[]{:S(2)}) copy-start(bf16[4,1024]{1,0:T(4,128)(2,1)} %query_ref) | copy-start | bytes 24580
  13.9 6.3 %copy-start.4 = (s32[4]{0:T(128)S(1)}, s32[4]{0:T(128)}, u32[]{:S(2)}) copy-start(s32[4]{0:T(128)} %param.14) | copy-start | bytes 52
  13.9 7.1 %copy-start.3 = (bf16[4,256]{1,0:T(4,128)(2,1)S(1)}, bf16[4,256]{1,0:T(4,128)(2,1)}, u32[]{:S(2)}) copy-start(bf16[4,256]{1,0:T(4,128)(2,1)} %base_ref.1) | copy-start | bytes 6148
  16.5 4.6 %collective-permute-start.1 = (bf16[80,128]{1,0:T(8,128)(2,1)S(1)}, bf16[80,128]{1,0:T(8,128)(2,1)S(1)}, u32[]{:S(2)}, u32[]{:S(2)}) collective-permute-start(bf16[80,128]{1,0:T(8,128)(2,1)S(1)} %get-tuple-element.49.mine_ref), channel_id=1, source_target_pairs={{0,1},{1,0},{2,3},{3,2},{4,5},{5,4},{6,7},{7,6},{8,9},{9,8},{10,11... | collective-permute-start | bytes 61448 | tf_op jit(solution)/shard_map/ppermute | solution.py:383

commit v11 on v10

--- a/solution.py
+++ b/solution.py
@@ -164,10 +164,15 @@
         out_ref[tall:, :] = jnp.concatenate([low] * (16 // count), axis=0).astype(BF16)
 
 
-def early_kernel(
-    low_ref, lengths_hbm, query_hbm, cache_hbm, q_ref, stats_ref,
-    lengths_ref, query_ref, cache_ref, sems
-):
+def middle_kernel(
+    order, ids_ref, home_ref, up_ref, got_ref, down_ref, far_ref, lengths_hbm, query_hbm,
+    cache_hbm, out_ref, q_ref, stats_ref, flat_ref, wide_ref, lengths_ref, query_ref,
+    cache_ref, sems
+):
+    low_kernel(
+        order, ids_ref, home_ref, up_ref, got_ref, down_ref, far_ref, out_ref, flat_ref, wide_ref
+    )
+
     @pl.when(lax.axis_index("tp") == 0)
     def _():
         early(lengths_hbm, query_hbm, cache_hbm, q_ref, stats_ref,
@@ -332,18 +337,28 @@
         pin(cache), pin(near_down), pin(cache), pin(near_down),
     )
     got = exchange(blocks)
-    packed = pl.pallas_call(
-        functools.partial(low_kernel, order),
-        out_shape=jax.ShapeDtypeStruct((parts, per_dev, span + 128), BF16),
-        in_specs=[VMEM] * 6,
-        out_specs=VMEM,
+    heads_shape = jax.ShapeDtypeStruct((per_dev * heads, HD), F32)
+    stats_shape = jax.ShapeDtypeStruct((2 * per_dev * heads, HD), F32)
+    packed, early_q, early_stats = pl.pallas_call(
+        functools.partial(middle_kernel, order),
+        out_shape=(
+            jax.ShapeDtypeStruct((parts, per_dev, span + 128), BF16), heads_shape, stats_shape
+        ),
+        in_specs=[VMEM] * 6 + [HBM] * 3,
+        out_specs=(VMEM,) * 3,
         scratch_shapes=[
             pltpu.VMEM((depth, span), F32),
             pltpu.VMEM((slots, ranks, width), F32),
+            pltpu.VMEM((1, per_dev), lengths.dtype),
+            pltpu.VMEM(query.shape, BF16),
+            pltpu.VMEM(cache.shape, BF16),
+            pltpu.SemaphoreType.DMA((3,)),
         ],
         compiler_params=PARAMS,
-    )(near_ids, near_home, near_up, got, near_down, far_down)
-
+    )(
+        near_ids, near_home, near_up, got, near_down, far_down,
+        pin(lengths.reshape(1, per_dev)), pin(query), pin(cache),
+    )
     packed, got, lower = lax.optimization_barrier((packed, got, lower))
 
     def fold(x):
@@ -356,23 +371,6 @@
             compiler_params=PARAMS,
         )(x)
 
-    heads_shape = jax.ShapeDtypeStruct((per_dev * heads, HD), F32)
-    stats_shape = jax.ShapeDtypeStruct((2 * per_dev * heads, HD), F32)
-
-    early_q, early_stats = pl.pallas_call(
-        early_kernel,
-        out_shape=(heads_shape, stats_shape),
-        in_specs=[VMEM] + [HBM] * 3,
-        out_specs=(VMEM, VMEM),
-        scratch_shapes=[
-            pltpu.VMEM((1, per_dev), lengths.dtype),
-            pltpu.VMEM(query.shape, BF16),
-            pltpu.VMEM(cache.shape, BF16),
-            pltpu.SemaphoreType.DMA((3,)),
-        ],
-        compiler_params=PARAMS,
-    )(packed, pin(lengths.reshape(1, per_dev)), pin(query), pin(cache))
-    packed, got, early_q = lax.optimization_barrier((packed, got, early_q))
     mine = lax.cond(
         lower,
         lambda packed, got: fold(got[:, :, :span]),

time: 22.2 us -> 22.1 us (level)
    pallas_call x2 -> x1, Pallas kernels: 2.45 us -> 2.45 us  [shards(): pl.pallas_call(functools.partial(middle_kernel, order), out_shape=(jax.Sh...]
where the time goes in v11:
time: 22.1 us; the launch traced here: 21.9 us
  blocking collectives  10.6 us (48%)
  starting transfers between devices  5.13 us (23%)
  Pallas kernels  4.63 us (21%)
  waiting for transfers between devices  0.82 us (4%)
  between operations  0.71 us (3%)
    all_to_all x1, blocking collectives, exchange(): lax.all_to_all(x, 'req', split_axis=0, concat_axis=0, tiled=True, axis_in...  10.6 us
    ppermute x1, starting transfers between devices, shards(): other = lax.ppermute(mine, 'tp', swap)  3.73 us
    pallas_call x1, Pallas kernels, shards(): pl.pallas_call(functools.partial(middle_kernel, order), out_shape=(jax.Sh...  2.45 us
    ppermute x1, starting transfers between devices, shards(): far_down = lax.ppermute(near_down, 'tp', swap)  1.4 us
    pallas_call x1, Pallas kernels, shards(): pl.pallas_call(functools.partial(pack_kernel, order), out_shape=blocks_sh...  1.17 us
    pallas_call x1, Pallas kernels, shards(): pl.pallas_call(functools.partial(merge_kernel, ranks), out_shape=(jax.Sha...  0.88 us
    ppermute x1, waiting for transfers between devices, shards(): other = lax.ppermute(mine, 'tp', swap)  0.82 us
  transfers between devices with their start and end apart: 2, of which 1 were waited for; matrix products, arithmetic and copies ran while one was open for 0% of the time, Pallas kernels for 5%

profile of v11, /device:TPU:0, one launch (start us, length us, event | category | flops | bytes accessed | tf_op | source)
XLA Modules:
  0.0 21.9 jit_solution(9840629353853604820)
XLA Ops:
  0.6 0.1 shard_map.104
  0.7 0.0 copy-start
  0.8 1.4 %collective-permute-start = (bf16[2048,512]{1,0:T(8,128)(2,1)}, bf16[2048,512]{1,0:T(8,128)(2,1)S(1)}, u32[]{:S(2)}, u32[]{:S(2)}) collective-permute-start(bf16[2048,512]{1,0:T(8,128)(2,1)} %down_ref), channel_id=1, source_target_pairs={{0,1},{1,0},{2,3},{3,2},{4,5},{5,4},{6,7},{7,6},{8,9},{9,8},{10,11... | collective-permute-start | bytes 6291464 | tf_op jit(solution)/shard_map/ppermute | solution.py:319
  2.2 1.2 %shard_map.105 = bf16[8,4,2048]{2,1,0:T(4,128)(2,1)S(1)} custom-call(bf16[8,4,2048]{2,1,0:T(4,128)(2,1)S(1)} %get-tuple-element.30.blocks_ref, s32[1,32]{1,0:T(1,128)} %bitcast.11, s32[1,64]{1,0:T(1,128)} %bitcast.13, bf16[8,8,256]{2,1,0:T(8,128)(2,1)} %up_hbm.3, bf16[4,512,256]{2,1,0:T(8,128)(2,1)} %cache_ref, ...), custom_call_target="tpu_custom_call", output_to_operand_aliasing={{}: (0, {})} | custom-call | tf_op jit(solution)/shard_map/pallas_call | solution.py:320
  3.3 10.6 %all_to_all.10.got_ref = bf16[8,4,2048]{2,1,0:T(4,128)(2,1)S(1)} all-to-all(bf16[8,4,2048]{2,1,0:T(4,128)(2,1)S(1)} %shard_map.105), channel_id=1, replica_groups={{10,0,12,14,2,4,6,8},{11,1,13,15,3,5,7,9},{26,16,28,30,18,20,22,24},{27..., dimensions={0} | all-to-all | bytes 262144 | tf_op jit(solution)/shard_map/all_to_all | solution.py:298
  13.9 0.0 collective-permute-done.far_ref
  13.9 0.0 copy-done
  13.9 0.0 copy-start.1
  13.9 0.0 copy-start.2
  13.9 0.0 copy-start.4
  13.9 0.0 copy-start.3
  13.9 2.4 %shard_map.106 = (bf16[8,4,2176]{2,1,0:T(4,128)(2,1)S(1)}, f32[32,128]{1,0:T(8,128)S(1)}, f32[64,128]{1,0:T(8,128)S(1)}) custom-call(s32[1,32]{1,0:T(1,128)S(1)} %get-tuple-element.26.ids_ref, s32[1,64]{1,0:T(1,128)S(1)} %get-tuple-element.27.home_ref, bf16[8,8,256]{2,1,0:T(8,128)(2,1)S(1)} %get-tuple-element.28.up_ref, ...), custom_call_target="tpu_custom_call" | custom-call | tf_op jit(solution)/shard_map/pallas_call | solution.py:342
  16.4 3.7 %collective-permute-start.1 = (bf16[80,128]{1,0:T(8,128)(2,1)S(1)}, bf16[80,128]{1,0:T(8,128)(2,1)S(1)}, u32[]{:S(2)}, u32[]{:S(2)}) collective-permute-start(bf16[80,128]{1,0:T(8,128)(2,1)S(1)} %get-tuple-element.45.mine_ref), channel_id=1, source_target_pairs={{0,1},{1,0},{2,3},{3,2},{4,5},{5,4},{6,7},{7,6},{8,9},{9,8},{10,11... | collective-permute-start | bytes 61448 | tf_op jit(solution)/shard_map/ppermute | solution.py:381
  20.2 0.0 copy-done.1
  20.2 0.0 copy-done.2
  20.2 0.0 copy-done.4
  20.2 0.8 %collective-permute-done.1.other_ref = bf16[80,128]{1,0:T(8,128)(2,1)S(1)} collective-permute-done((bf16[80,128]{1,0:T(8,128)(2,1)S(1)}, bf16[80,128]{1,0:T(8,128)(2,1)S(1)}, u32[]{:S(2)}, u32[]{:S(2)}) %collective-permute-start.1) | collective-permute-done | bytes 20512 | tf_op jit(solution)/shard_map/ppermute | solution.py:381
  21.0 0.0 copy-done.3
  21.0 0.9 %shard_map.108 = (bf16[4,256]{1,0:T(4,128)(2,1)}, bf16[4,1024]{1,0:T(4,128)(2,1)}) custom-call(bf16[80,128]{1,0:T(8,128)(2,1)S(1)} %get-tuple-element.45.mine_ref, bf16[80,128]{1,0:T(8,128)(2,1)S(1)} %collective-permute-done.1.other_ref, f32[32,128]{1,0:T(8,128)S(1)} %get-tuple-element.41.q_ref, f32[64,128]{1,0:T(8,128)S(1)} %get-tuple-element.42.stats_ref, ...), custom_call_target="tpu_custom_call" | custom-call | tf_op jit(solution)/shard_map/pallas_call | solution.py:390
  (3 shorter events, 0.1 us)
Async XLA Ops:
  0.7 13.1 %copy-start = (bf16[2048,512]{1,0:T(8,128)(2,1)S(1)}, bf16[2048,512]{1,0:T(8,128)(2,1)}, u32[]{:S(2)}) copy-start(bf16[2048,512]{1,0:T(8,128)(2,1)} %down_ref) | copy-start | bytes 6291460
  0.8 13.1 %collective-permute-start = (bf16[2048,512]{1,0:T(8,128)(2,1)}, bf16[2048,512]{1,0:T(8,128)(2,1)S(1)}, u32[]{:S(2)}, u32[]{:S(2)}) collective-permute-start(bf16[2048,512]{1,0:T(8,128)(2,1)} %down_ref), channel_id=1, source_target_pairs={{0,1},{1,0},{2,3},{3,2},{4,5},{5,4},{6,7},{7,6},{8,9},{9,8},{10,11... | collective-permute-start | bytes 6291464 | tf_op jit(solution)/shard_map/ppermute | solution.py:319
  13.9 6.3 %copy-start.1 = (bf16[4,512,256]{2,1,0:T(8,128)(2,1)S(1)}, bf16[4,512,256]{2,1,0:T(8,128)(2,1)}, u32[]{:S(2)}) copy-start(bf16[4,512,256]{2,1,0:T(8,128)(2,1)} %cache_ref) | copy-start | bytes 3145732
  13.9 6.3 %copy-start.2 = (bf16[4,1024]{1,0:T(4,128)(2,1)S(1)}, bf16[4,1024]{1,0:T(4,128)(2,1)}, u32[]{:S(2)}) copy-start(bf16[4,1024]{1,0:T(4,128)(2,1)} %query_ref) | copy-start | bytes 24580
  13.9 6.3 %copy-start.4 = (s32[4]{0:T(128)S(1)}, s32[4]{0:T(128)}, u32[]{:S(2)}) copy-start(s32[4]{0:T(128)} %param.14) | copy-start | bytes 52
  13.9 7.1 %copy-start.3 = (bf16[4,256]{1,0:T(4,128)(2,1)S(1)}, bf16[4,256]{1,0:T(4,128)(2,1)}, u32[]{:S(2)}) copy-start(bf16[4,256]{1,0:T(4,128)(2,1)} %base_ref.1) | copy-start | bytes 6148
  16.4 4.6 %collective-permute-start.1 = (bf16[80,128]{1,0:T(8,128)(2,1)S(1)}, bf16[80,128]{1,0:T(8,128)(2,1)S(1)}, u32[]{:S(2)}, u32[]{:S(2)}) collective-permute-start(bf16[80,128]{1,0:T(8,128)(2,1)S(1)} %get-tuple-element.45.mine_ref), channel_id=1, source_target_pairs={{0,1},{1,0},{2,3},{3,2},{4,5},{5,4},{6,7},{7,6},{8,9},{9,8},{10,11... | collective-permute-start | bytes 61448 | tf_op jit(solution)/shard_map/ppermute | solution.py:381

commit v12 on v10

--- a/solution.py
+++ b/solution.py
@@ -119,6 +119,9 @@
 
     @pl.when(lax.axis_index("tp") == 1)
     def _():
+        rows = needed_rows(ids_ref[...], home_ref[...], up_ref, flat_ref, wide_ref)
+        for p, q in enumerate(order):
+            out_ref[p, :, :span] = rows[q * per_dev : (q + 1) * per_dev]
         pieces = [got_ref[p].astype(F32)[:, :block] for p in range(parts)]
         blocks = jnp.concatenate(pieces, axis=0).astype(BF16)
         names = across(one_hot_ids(ids_ref[...]), iota((ADAPTERS, 128), 0).astype(BF16))
@@ -143,9 +146,7 @@
                 low = jnp.where(rank // 2 == j + half * ranks // 2, got, low)
         high = low.astype(BF16).astype(F32)
         low = jnp.where(lane < 2 * ranks, high, low - high).astype(BF16)
-        rows = needed_rows(ids_ref[...], home_ref[...], up_ref, flat_ref, wide_ref)
-        for p, q in enumerate(order):
-            out_ref[p, :, :span] = rows[q * per_dev : (q + 1) * per_dev]
+        for p in range(parts):
             out_ref[p, :, span:] = low[p * per_dev : (p + 1) * per_dev]
 
 

time: 22.2 us -> 22.2 us (level)
  no operation moved by 1% of the time
where the time goes in v12:
time: 22.2 us; the launch traced here: 22 us
  blocking collectives  10.6 us (48%)
  starting transfers between devices  5.21 us (23%)
  Pallas kernels  4.64 us (21%)
  waiting for transfers between devices  0.82 us (4%)
  between operations  0.72 us (3%)
    all_to_all x1, blocking collectives, exchange(): lax.all_to_all(x, 'req', split_axis=0, concat_axis=0, tiled=True, axis_in...  10.6 us
    ppermute x1, starting transfers between devices, shards(): other = lax.ppermute(mine, 'tp', swap)  3.81 us
    pallas_call x1, Pallas kernels, shards(): pl.pallas_call(early_kernel, out_shape=(heads_shape, stats_shape), in_spe...  2.44 us
    ppermute x1, starting transfers between devices, shards(): far_down = lax.ppermute(near_down, 'tp', swap)  1.4 us
    pallas_call x1, Pallas kernels, shards(): pl.pallas_call(functools.partial(pack_kernel, order), out_shape=blocks_sh...  1.17 us
    pallas_call x1, Pallas kernels, shards(): pl.pallas_call(functools.partial(merge_kernel, ranks), out_shape=(jax.Sha...  0.88 us
    ppermute x1, waiting for transfers between devices, shards(): other = lax.ppermute(mine, 'tp', swap)  0.82 us
  transfers between devices with their start and end apart: 2, of which 1 were waited for; matrix products, arithmetic and copies ran while one was open for 0% of the time, Pallas kernels for 5%

profile of v12, /device:TPU:0, one launch (start us, length us, event | category | flops | bytes accessed | tf_op | source)
XLA Modules:
  0.0 22.0 jit_solution(17766548362368118328)
XLA Ops:
  0.6 0.1 shard_map.104
  0.7 0.0 copy-start
  0.8 1.4 %collective-permute-start = (bf16[2048,512]{1,0:T(8,128)(2,1)}, bf16[2048,512]{1,0:T(8,128)(2,1)S(1)}, u32[]{:S(2)}, u32[]{:S(2)}) collective-permute-start(bf16[2048,512]{1,0:T(8,128)(2,1)} %down_ref), channel_id=1, source_target_pairs={{0,1},{1,0},{2,3},{3,2},{4,5},{5,4},{6,7},{7,6},{8,9},{9,8},{10,11... | collective-permute-start | bytes 6291464 | tf_op jit(solution)/shard_map/ppermute | solution.py:315
  2.2 1.2 %shard_map.105 = bf16[8,4,2048]{2,1,0:T(4,128)(2,1)S(1)} custom-call(bf16[8,4,2048]{2,1,0:T(4,128)(2,1)S(1)} %get-tuple-element.32.blocks_ref, s32[1,32]{1,0:T(1,128)} %bitcast.11, s32[1,64]{1,0:T(1,128)} %bitcast.13, bf16[8,8,256]{2,1,0:T(8,128)(2,1)} %up_hbm.3, bf16[4,512,256]{2,1,0:T(8,128)(2,1)} %cache_ref, ...), custom_call_target="tpu_custom_call", output_to_operand_aliasing={{}: (0, {})} | custom-call | tf_op jit(solution)/shard_map/pallas_call | solution.py:316
  3.3 10.6 %all_to_all.10.got_ref = bf16[8,4,2048]{2,1,0:T(4,128)(2,1)S(1)} all-to-all(bf16[8,4,2048]{2,1,0:T(4,128)(2,1)S(1)} %shard_map.105), channel_id=1, replica_groups={{10,0,12,14,2,4,6,8},{11,1,13,15,3,5,7,9},{26,16,28,30,18,20,22,24},{27..., dimensions={0} | all-to-all | bytes 262144 | tf_op jit(solution)/shard_map/all_to_all | solution.py:294
  13.9 0.0 collective-permute-done.far_ref
  13.9 0.0 copy-done
  13.9 0.0 copy-start.1
  13.9 0.0 copy-start.2
  13.9 0.0 copy-start.4
  13.9 0.0 copy-start.3
  14.0 2.4 %shard_map.107 = (f32[32,128]{1,0:T(8,128)S(1)}, f32[64,128]{1,0:T(8,128)S(1)}) custom-call(bf16[8,4,2176]{2,1,0:T(4,128)(2,1)S(1)} %shard_map.106.low_ref, s32[1,4]{1,0:T(1,128)} %bitcast.7, bf16[4,1024]{1,0:T(4,128)(2,1)} %query_ref, bf16[4,512,256]{2,1,0:T(8,128)(2,1)} %cache_ref), custom_call_target="tpu_custom_call" | custom-call | tf_op jit(solution)/shard_map/pallas_call | solution.py:363
  16.4 0.1 conditional.1
  16.5 3.8 %collective-permute-start.1 = (bf16[80,128]{1,0:T(8,128)(2,1)S(1)}, bf16[80,128]{1,0:T(8,128)(2,1)S(1)}, u32[]{:S(2)}, u32[]{:S(2)}) collective-permute-start(bf16[80,128]{1,0:T(8,128)(2,1)S(1)} %get-tuple-element.49.mine_ref), channel_id=1, source_target_pairs={{0,1},{1,0},{2,3},{3,2},{4,5},{5,4},{6,7},{7,6},{8,9},{9,8},{10,11... | collective-permute-start | bytes 61448 | tf_op jit(solution)/shard_map/ppermute | solution.py:384
  20.3 0.0 copy-done.1
  20.3 0.0 copy-done.2
  20.3 0.0 copy-done.4
  20.3 0.8 %collective-permute-done.1.other_ref = bf16[80,128]{1,0:T(8,128)(2,1)S(1)} collective-permute-done((bf16[80,128]{1,0:T(8,128)(2,1)S(1)}, bf16[80,128]{1,0:T(8,128)(2,1)S(1)}, u32[]{:S(2)}, u32[]{:S(2)}) %collective-permute-start.1) | collective-permute-done | bytes 20512 | tf_op jit(solution)/shard_map/ppermute | solution.py:384
  21.1 0.0 copy-done.3
  21.1 0.9 %shard_map.109 = (bf16[4,256]{1,0:T(4,128)(2,1)}, bf16[4,1024]{1,0:T(4,128)(2,1)}) custom-call(bf16[80,128]{1,0:T(8,128)(2,1)S(1)} %get-tuple-element.49.mine_ref, bf16[80,128]{1,0:T(8,128)(2,1)S(1)} %collective-permute-done.1.other_ref, f32[32,128]{1,0:T(8,128)S(1)} %get-tuple-element.45.q_ref, f32[64,128]{1,0:T(8,128)S(1)} %get-tuple-element.46.stats_ref, ...), custom_call_target="tpu_custom_call" | custom-call | tf_op jit(solution)/shard_map/pallas_call | solution.py:393
  (3 shorter events, 0.1 us)
Async XLA Ops:
  0.7 13.1 %copy-start = (bf16[2048,512]{1,0:T(8,128)(2,1)S(1)}, bf16[2048,512]{1,0:T(8,128)(2,1)}, u32[]{:S(2)}) copy-start(bf16[2048,512]{1,0:T(8,128)(2,1)} %down_ref) | copy-start | bytes 6291460
  0.8 13.1 %collective-permute-start = (bf16[2048,512]{1,0:T(8,128)(2,1)}, bf16[2048,512]{1,0:T(8,128)(2,1)S(1)}, u32[]{:S(2)}, u32[]{:S(2)}) collective-permute-start(bf16[2048,512]{1,0:T(8,128)(2,1)} %down_ref), channel_id=1, source_target_pairs={{0,1},{1,0},{2,3},{3,2},{4,5},{5,4},{6,7},{7,6},{8,9},{9,8},{10,11... | collective-permute-start | bytes 6291464 | tf_op jit(solution)/shard_map/ppermute | solution.py:315
  13.9 6.4 %copy-start.1 = (bf16[4,512,256]{2,1,0:T(8,128)(2,1)S(1)}, bf16[4,512,256]{2,1,0:T(8,128)(2,1)}, u32[]{:S(2)}) copy-start(bf16[4,512,256]{2,1,0:T(8,128)(2,1)} %cache_ref) | copy-start | bytes 3145732
  13.9 6.4 %copy-start.2 = (bf16[4,1024]{1,0:T(4,128)(2,1)S(1)}, bf16[4,1024]{1,0:T(4,128)(2,1)}, u32[]{:S(2)}) copy-start(bf16[4,1024]{1,0:T(4,128)(2,1)} %query_ref) | copy-start | bytes 24580
  13.9 6.4 %copy-start.4 = (s32[4]{0:T(128)S(1)}, s32[4]{0:T(128)}, u32[]{:S(2)}) copy-start(s32[4]{0:T(128)} %param.14) | copy-start | bytes 52
  13.9 7.2 %copy-start.3 = (bf16[4,256]{1,0:T(4,128)(2,1)S(1)}, bf16[4,256]{1,0:T(4,128)(2,1)}, u32[]{:S(2)}) copy-start(bf16[4,256]{1,0:T(4,128)(2,1)} %base_ref.1) | copy-start | bytes 6148
  16.5 4.7 %collective-permute-start.1 = (bf16[80,128]{1,0:T(8,128)(2,1)S(1)}, bf16[80,128]{1,0:T(8,128)(2,1)S(1)}, u32[]{:S(2)}, u32[]{:S(2)}) collective-permute-start(bf16[80,128]{1,0:T(8,128)(2,1)S(1)} %get-tuple-element.49.mine_ref), channel_id=1, source_target_pairs={{0,1},{1,0},{2,3},{3,2},{4,5},{5,4},{6,7},{7,6},{8,9},{9,8},{10,11... | collective-permute-start | bytes 61448 | tf_op jit(solution)/shard_map/ppermute | solution.py:384
